TPU v7x, 32 devices: a whole 2x2x4 slice. The times are simulated.
32 devices in a mesh: strip: 4 (over y, x), canvas: 8 (over z, core).
Axes of the slice: x: 2, y: 2, z: 4, core: 2. Of those that a mesh axis runs over, the one named last changes fastest.
Arguments:
- field: float32 [80, 56, 56, 384], P('canvas', 'strip'), may hold values from -6 to 6
- crop_ids: int32 [80, 56, 56], P('canvas', 'strip'), may hold values from 0 to 15, as said below
- norm1_gain: float32 [384], replicated, may hold values from 0.25 to 1.75
- norm1_bias: float32 [384], replicated, may hold values from -1.75 to 1.75
- qkv_weight: bfloat16 [384, 1152], P('canvas', 'strip'), may hold values from -0.3125 to 0.3125
- qkv_bias: float32 [1152], replicated, may hold values from -1.75 to 1.75
- rel_table: float32 [169, 12], replicated, may hold values from -6 to 6
- proj_weight: bfloat16 [384, 384], P('canvas', 'strip'), may hold values from -1.25 to 1.25
- proj_bias: float32 [384], replicated, may hold values from -1.75 to 1.75
- norm2_gain: float32 [384], replicated, may hold values from 0.25 to 1.75
- norm2_bias: float32 [384], replicated, may hold values from -1.75 to 1.75
- fc1_weight: bfloat16 [384, 1536], P('canvas', 'strip'), may hold values from -0.3125 to 0.3125
- fc1_bias: float32 [1536], replicated, may hold values from -1.75 to 1.75
- fc2_weight: bfloat16 [1536, 384], P('canvas', 'strip'), may hold values from -0.15625 to 0.15625
- fc2_bias: float32 [384], replicated, may hold values from -1.75 to 1.75
- cotangent: float32 [80, 56, 56, 384], P('canvas', 'strip'), may hold values from -6 to 6
Outputs:
- output: float32 [80, 56, 56, 384], P('canvas', 'strip')
- field_grad: float32 [80, 56, 56, 384], P('canvas', 'strip')
- norm1_gain_grad: float32 [384], replicated
- norm1_bias_grad: float32 [384], replicated
- qkv_weight_grad: float32 [384, 1152], P('canvas', 'strip')
- qkv_bias_grad: float32 [1152], replicated
- rel_table_grad: float32 [169, 12], replicated
- proj_weight_grad: float32 [384, 384], P('canvas', 'strip')
- proj_bias_grad: float32 [384], replicated
- norm2_gain_grad: float32 [384], replicated
- norm2_bias_grad: float32 [384], replicated
- fc1_weight_grad: float32 [384, 1536], P('canvas', 'strip')
- fc1_bias_grad: float32 [1536], replicated
- fc2_weight_grad: float32 [1536, 384], P('canvas', 'strip')
- fc2_bias_grad: float32 [384], replicated
Inputs may be any that keep to these rules, and one draw needn't show every extreme that they name: `crop_ids`: within a canvas each crop id marks one rectangle of cells; id 0 covers every row of its canvas.
All inputs are finite; a program needn't handle non-finite values.
Results may differ from a plain program's by a relative error of at most 0.018.
Values may be sent and summed in bfloat16 or wider, within the bound.
A program may use at most 384 MiB of HBM per device.

v0:
```python
import jax
import jax.numpy as jnp
from jax import lax
from jax.sharding import PartitionSpec as P

WIN = 7
SHIFT = 3


norm_eps = 1e-05
masked_score = -1e30


def from_behind(value, axis, steps):
    count = lax.axis_size(axis)
    pairs = [(source, (source + steps) % count) for source in range(count)]
    return lax.ppermute(value, axis, pairs)


def normalize(values, gain, offset):
    centre = values - jnp.mean(values, -1, keepdims=True)
    spread = jnp.mean(centre * centre, -1, keepdims=True)
    return centre * lax.rsqrt(spread + norm_eps) * gain + offset


def windows(values):
    canvases, strip_rows, columns, depth = values.shape
    blocks = values.reshape(canvases, strip_rows // WIN, WIN, columns // WIN, WIN, depth).transpose(
        0, 1, 3, 2, 4, 5
    )
    return blocks.reshape(-1, WIN * WIN, depth)


def unwindows(values, canvases, strip_rows, columns):
    depth = values.shape[-1]
    blocks = values.reshape(canvases, strip_rows // WIN, columns // WIN, WIN, WIN, depth).transpose(
        0, 1, 3, 2, 4, 5
    )
    return blocks.reshape(canvases, strip_rows, columns, depth)


def relative_index():
    places = jnp.arange(WIN * WIN, dtype=jnp.int32)
    place_row = places // WIN
    place_col = places % WIN
    return (
        (place_row[:, None] - place_row[None, :] + WIN - 1) * (2 * WIN - 1)
        + place_col[:, None]
        - place_col[None, :]
        + WIN
        - 1
    )


def weight_grad(left, right):
    return lax.dot_general(
        left.reshape(-1, left.shape[-1]),
        right.reshape(-1, right.shape[-1]),
        (((0,), (0,)), ((), ())),
        preferred_element_type=jnp.float32,
    )


def back_dot(grads, weight):
    return lax.dot_general(
        grads, weight, (((grads.ndim - 1,), (1,)), ((), ())), preferred_element_type=jnp.float32
    )


def token_sum(values):
    return jnp.sum(values.astype(jnp.float32), (0, 1, 2))


def exact_gelu(values):
    return jax.nn.gelu(values, approximate=False)


def spread_heads(values, head_mask):
    group = values.shape[0]
    heads = head_mask.shape[0]
    return (values[:, None] * head_mask[None, :, None, :]).reshape(
        group, heads * WIN * WIN, values.shape[-1]
    )


def fold_heads(grads, head_mask):
    group = grads.shape[0]
    heads = head_mask.shape[0]
    return jnp.sum(
        grads.reshape(group, heads, WIN * WIN, grads.shape[-1])
        * head_mask[None, :, None, :].astype(jnp.float32),
        1,
    )


def body(
    field,
    crop_ids,
    norm1_gain,
    norm1_bias,
    qkv_weight,
    qkv_bias,
    rel_table,
    proj_weight,
    proj_bias,
    norm2_gain,
    norm2_bias,
    fc1_weight,
    fc1_bias,
    fc2_weight,
    fc2_bias,
    cotangent,
):
    canvases, strip_rows, columns, channels = field.shape
    heads = rel_table.shape[1]
    head_size = channels // heads
    scale = head_size ** (-0.5)
    places = WIN * WIN
    half_gathered = (
        lax.all_gather(qkv_weight, "strip", axis=1, tiled=True),
        lax.all_gather(proj_weight, "strip", axis=1, tiled=True),
        lax.all_gather(fc1_weight, "strip", axis=1, tiled=True),
        lax.all_gather(fc2_weight, "strip", axis=1, tiled=True),
    )
    whole_w = (
        lax.all_gather(half_gathered[0], "canvas", axis=0, tiled=True),
        lax.all_gather(half_gathered[1], "canvas", axis=0, tiled=True),
        lax.all_gather(half_gathered[2], "canvas", axis=0, tiled=True),
        lax.all_gather(half_gathered[3], "canvas", axis=0, tiled=True),
    )
    w_qkv, w_proj, w_fc1, w_fc2 = whole_w
    normed_full, norm1_pull = jax.vjp(normalize, field, norm1_gain, norm1_bias)
    normed = normed_full.astype(jnp.bfloat16)
    rim_rows, rim_crops = from_behind(
        (normed[:, :SHIFT], crop_ids[:, :SHIFT].astype(jnp.bfloat16)), "strip", -1
    )
    shifted = jnp.roll(jnp.concatenate([normed[:, SHIFT:], rim_rows], 1), -SHIFT, 2)
    shifted_crops = jnp.roll(
        jnp.concatenate([crop_ids[:, SHIFT:], rim_crops.astype(jnp.int32)], 1), -SHIFT, 2
    )
    total_rows = strip_rows * lax.axis_size("strip")
    global_rows = lax.axis_index("strip") * strip_rows + jnp.arange(strip_rows, dtype=jnp.int32)
    col_index = jnp.arange(columns, dtype=jnp.int32)
    row_band = (global_rows >= total_rows - WIN).astype(jnp.int32) + (
        global_rows >= total_rows - SHIFT
    ).astype(jnp.int32)
    col_band = (col_index >= columns - WIN).astype(jnp.int32) + (
        col_index >= columns - SHIFT
    ).astype(jnp.int32)
    region = row_band[:, None] * 3 + col_band[None, :]
    ident = windows((shifted_crops * 9 + region[None])[..., None])[..., 0]
    allowed = ident[:, :, None] == ident[:, None, :]
    table_hot = (
        relative_index().reshape(-1)[:, None]
        == jnp.arange(rel_table.shape[0], dtype=jnp.int32)[None, :]
    ).astype(jnp.float32)
    pos_bias = (
        jnp.dot(table_hot, rel_table, precision=lax.Precision.HIGHEST)
        .reshape(places, places, heads)
        .transpose(0, 2, 1)
        .reshape(places, heads * places)
    )
    head_mask = (
        jnp.arange(channels, dtype=jnp.int32)[None, :] // head_size
        == jnp.arange(heads, dtype=jnp.int32)[:, None]
    ).astype(jnp.bfloat16)
    expand = (
        jnp.arange(heads * places, dtype=jnp.int32)[None, :] // places
        == jnp.arange(heads, dtype=jnp.int32)[:, None]
    ).astype(jnp.float32)
    block_ones = expand.T

    def widen(small):
        return jnp.dot(small, expand, precision=lax.Precision.HIGHEST)

    def head_total(wide):
        return jnp.dot(wide, block_ones, precision=lax.Precision.HIGHEST)

    qkv = jnp.dot(shifted, w_qkv, preferred_element_type=jnp.float32) + qkv_bias
    query = (qkv[..., :channels] * scale).astype(jnp.bfloat16)
    keys_all = qkv[..., channels : 2 * channels].astype(jnp.bfloat16)
    values_all = qkv[..., 2 * channels :].astype(jnp.bfloat16)
    query_w = windows(query)
    keys_w = windows(keys_all)
    values_w = windows(values_all)
    window_count = query_w.shape[0]
    group = max([size for size in range(1, 17) if window_count % size == 0])
    blocks = window_count // group

    def grouped(values):
        return values.reshape((blocks, group) + values.shape[1:])

    def block_scores(query_b, keys_b, allow_b):
        raw_scores = (
            jnp.einsum(
                "aqc,akc->aqk",
                query_b,
                spread_heads(keys_b, head_mask),
                preferred_element_type=jnp.float32,
            )
            + pos_bias[None]
        )
        return jnp.where(jnp.tile(allow_b, (1, 1, heads)), raw_scores, masked_score)

    def forward_block(items):
        query_b, keys_b, values_b, allow_b = items
        scores = block_scores(query_b, keys_b, allow_b)
        highest = jnp.max(scores.reshape(group, places, heads, places), -1)
        expo = jnp.exp(scores - widen(highest))
        denom = head_total(expo)
        probs = expo / widen(denom)
        log_total = highest + jnp.log(denom)
        mixed_b = jnp.einsum(
            "aqk,akc->aqc",
            probs.astype(jnp.bfloat16),
            spread_heads(values_b, head_mask),
            preferred_element_type=jnp.float32,
        ).astype(jnp.bfloat16)
        return (mixed_b, log_total)

    mixed_blocks, log_totals = lax.map(
        forward_block, (grouped(query_w), grouped(keys_w), grouped(values_w), grouped(allowed))
    )
    mixed = jnp.roll(
        unwindows(
            mixed_blocks.reshape(window_count, places, channels), canvases, strip_rows, columns
        ),
        SHIFT,
        2,
    )
    rim_mixed = from_behind(mixed[:, strip_rows - SHIFT :], "strip", 1)
    restored = jnp.concatenate([rim_mixed, mixed[:, : strip_rows - SHIFT]], 1)
    middle = field + jnp.dot(restored, w_proj, preferred_element_type=jnp.float32) + proj_bias
    normed_two_full, norm2_pull = jax.vjp(normalize, middle, norm2_gain, norm2_bias)
    normed_two = normed_two_full.astype(jnp.bfloat16)
    act = jnp.dot(normed_two, w_fc1, preferred_element_type=jnp.float32) + fc1_bias
    hidden_full, gelu_pull = jax.vjp(exact_gelu, act)
    hidden = hidden_full.astype(jnp.bfloat16)
    output = middle + jnp.dot(hidden, w_fc2, preferred_element_type=jnp.float32) + fc2_bias
    d_out = cotangent.astype(jnp.bfloat16)
    d_w_fc2 = weight_grad(hidden, d_out)
    d_b_fc2 = token_sum(d_out)
    d_hidden = back_dot(d_out, w_fc2)
    (d_act_full,) = gelu_pull(d_hidden)
    d_act = d_act_full.astype(jnp.bfloat16)
    d_w_fc1 = weight_grad(normed_two, d_act)
    d_b_fc1 = token_sum(d_act)
    d_normed_two = back_dot(d_act, w_fc1)
    d_middle_norm, d_gain_two, d_bias_two = norm2_pull(d_normed_two)
    d_middle = cotangent + d_middle_norm
    d_branch = d_middle.astype(jnp.bfloat16)
    d_w_proj = weight_grad(restored, d_branch)
    d_b_proj = token_sum(d_branch)
    d_restored = back_dot(d_branch, w_proj).astype(jnp.bfloat16)
    rim_grad = from_behind(d_restored[:, :SHIFT], "strip", -1)
    d_mixed = jnp.roll(jnp.concatenate([d_restored[:, SHIFT:], rim_grad], 1), -SHIFT, 2)
    d_mixed_w = windows(d_mixed)

    def backward_block(items):
        query_b, keys_b, values_b, allow_b, log_total, d_mixed_b = items
        probs = jnp.exp(block_scores(query_b, keys_b, allow_b) - widen(log_total))
        values_spread = spread_heads(values_b, head_mask)
        d_probs = jnp.einsum(
            "aqc,akc->aqk", d_mixed_b, values_spread, preferred_element_type=jnp.float32
        )
        row_terms = head_total(d_probs * probs)
        d_scores = (probs * (d_probs - widen(row_terms))).astype(jnp.bfloat16)
        d_pos_b = jnp.sum(d_scores.astype(jnp.float32), 0)
        d_values = fold_heads(
            jnp.einsum(
                "aqk,aqc->akc",
                probs.astype(jnp.bfloat16),
                d_mixed_b,
                preferred_element_type=jnp.float32,
            ),
            head_mask,
        )
        d_query = (
            jnp.einsum(
                "aqk,akc->aqc",
                d_scores,
                spread_heads(keys_b, head_mask),
                preferred_element_type=jnp.float32,
            )
            * scale
        )
        d_keys = fold_heads(
            jnp.einsum("aqk,aqc->akc", d_scores, query_b, preferred_element_type=jnp.float32),
            head_mask,
        )
        joined = jnp.concatenate([d_query, d_keys, d_values], -1).astype(jnp.bfloat16)
        return (joined, d_pos_b)

    joined_blocks, d_pos_blocks = lax.map(
        backward_block,
        (
            grouped(query_w),
            grouped(keys_w),
            grouped(values_w),
            grouped(allowed),
            log_totals,
            grouped(d_mixed_w),
        ),
    )
    d_pos = (
        jnp.sum(d_pos_blocks, 0)
        .reshape(places, heads, places)
        .transpose(0, 2, 1)
        .reshape(places * places, heads)
    )
    d_table = lax.dot_general(
        table_hot, d_pos, (((0,), (0,)), ((), ())), precision=lax.Precision.HIGHEST
    )
    d_qkv = unwindows(
        joined_blocks.reshape(window_count, places, 3 * channels), canvases, strip_rows, columns
    )
    d_w_qkv = weight_grad(shifted, d_qkv)
    d_b_qkv = token_sum(d_qkv)
    d_shifted = jnp.roll(back_dot(d_qkv, w_qkv), SHIFT, 2)
    rim_back = from_behind(
        d_shifted[:, strip_rows - SHIFT :].astype(jnp.bfloat16), "strip", 1
    ).astype(jnp.float32)
    d_normed = jnp.concatenate([rim_back, d_shifted[:, : strip_rows - SHIFT]], 1)
    d_field_norm, d_gain_one, d_bias_one = norm1_pull(d_normed)
    field_grad = d_middle + d_field_norm
    row_summed = (
        lax.psum_scatter(
            d_w_qkv.astype(jnp.bfloat16), "canvas", scatter_dimension=0, tiled=True
        ).astype(jnp.float32),
        lax.psum_scatter(
            d_w_proj.astype(jnp.bfloat16), "canvas", scatter_dimension=0, tiled=True
        ).astype(jnp.float32),
        lax.psum_scatter(
            d_w_fc1.astype(jnp.bfloat16), "canvas", scatter_dimension=0, tiled=True
        ).astype(jnp.float32),
        lax.psum_scatter(
            d_w_fc2.astype(jnp.bfloat16), "canvas", scatter_dimension=0, tiled=True
        ).astype(jnp.float32),
    )
    weight_shards = (
        lax.psum_scatter(
            row_summed[0].astype(jnp.bfloat16), "strip", scatter_dimension=1, tiled=True
        ).astype(jnp.float32),
        lax.psum_scatter(
            row_summed[1].astype(jnp.bfloat16), "strip", scatter_dimension=1, tiled=True
        ).astype(jnp.float32),
        lax.psum_scatter(
            row_summed[2].astype(jnp.bfloat16), "strip", scatter_dimension=1, tiled=True
        ).astype(jnp.float32),
        lax.psum_scatter(
            row_summed[3].astype(jnp.bfloat16), "strip", scatter_dimension=1, tiled=True
        ).astype(jnp.float32),
    )
    small = lax.psum(
        (
            d_gain_one,
            d_bias_one,
            d_b_qkv,
            d_table,
            d_b_proj,
            d_gain_two,
            d_bias_two,
            d_b_fc1,
            d_b_fc2,
        ),
        ("strip", "canvas"),
    )
    return (
        output,
        field_grad,
        small[0],
        small[1],
        weight_shards[0],
        small[2],
        small[3],
        weight_shards[1],
        small[4],
        small[5],
        small[6],
        weight_shards[2],
        small[7],
        weight_shards[3],
        small[8],
    )


def solution(mesh):
    in_specs = (
        P("canvas", "strip", None, None),
        P("canvas", "strip", None),
        P(),
        P(),
        P("canvas", "strip"),
        P(),
        P(),
        P("canvas", "strip"),
        P(),
        P(),
        P(),
        P("canvas", "strip"),
        P(),
        P("canvas", "strip"),
        P(),
        P("canvas", "strip", None, None),
    )
    out_specs = (
        P("canvas", "strip", None, None),
        P("canvas", "strip", None, None),
        P(),
        P(),
        P("canvas", "strip"),
        P(),
        P(),
        P("canvas", "strip"),
        P(),
        P(),
        P(),
        P("canvas", "strip"),
        P(),
        P("canvas", "strip"),
        P(),
    )
    return jax.shard_map(body, mesh=mesh, in_specs=in_specs, out_specs=out_specs, check_vma=False)
```

profile of v0, /device:TPU:0, one launch (start us, length us, event | category | flops | bytes accessed | tf_op | source)
XLA Modules:
  0.0 2442.8 jit_solution(10390944433417696868)
XLA Ops:
  32.3 32.3 %all_gather.28 = bf16[48,1536]{1,0:T(8,128)(2,1)} all-gather(bf16[48,384]{1,0:T(8,128)(2,1)S(1)} %copy-done.39), channel_id=1, replica_groups=mesh['strip'=4,'canvas'=8] {'strip'}, dimensions={1}, use_global_device_ids=true | all-gather | bytes 184320 | tf_op jit(solution)/shard_map/all_gather | solution.py:122
  73.6 20.8 all_gather.25
  120.6 24.4 fusion.143
  145.0 10.8 fusion.142
  155.8 9.9 reshape.442
  172.5 9.9 reshape.440
  197.3 9.9 reshape.439
  215.8 486.6 %while.32 = (s32[]{:T(128)}, bf16[10,16,49,384]{3,1,2,0:T(8,128)(2,1)}, f32[10,16,49,12]{2,3,1,0:T(8,128)}, pred[10,16,49,49]{3,1,2,0:T(8,128)(4,1)}, bf16[10,16...) while((s32[]{:T(128)}, ...), condition=%wide.wide.region_4.5_spmd.clone.clone.clone, body=%wide.wide.region_2.4_spmd.clone.clone.clone.sunk | while | flops 917576192 | bytes 59596152 | solution.py:221
  710.5 10.1 reshape.443
  725.6 34.0 %all_gather.30 = bf16[192,384]{0,1:T(8,128)(2,1)S(1)} all-gather(bf16[192,96]{0,1:T(8,128)(2,1)S(1)} %copy.94), channel_id=1, replica_groups=mesh['strip'=4,'canvas'=8] {'strip'}, dimensions={1}, use_global_device_ids=true | all-gather | bytes 184320 | tf_op jit(solution)/shard_map/all_gather | solution.py:123
  768.9 15.1 all_gather.27
  784.0 9.0 fusion.144
  801.1 31.2 %fusion.87 = (u16[10,56,1536]{2,1,0:T(8,128)(2,1)S(1)}, u16[10,56,1536]{2,1,0:T(8,128)(2,1)S(1)}, f32[10,14,56,1536]{3,2,1,0:T(8,128)}) fusion(f32[1536]{0:T(1024)S(1)} %copy-done.47, bf16[384,1536]{1,0:T(8,128)(2,1)} %all-gather.5.cloned.1.call-done, f32[10,14,56,384]{3,2,1,0:T(8,128)} %copy-done.8, f32[384]{0:T(512)S(1)} %copy-done.56, ...), kind=kOutput, calls=%fused_computation.120 | convolution fusion | flops 9430364160 | bytes 64903424 | tf_op jit(solution)/shard_map/dot_general | solution.py:236
  832.2 113.1 %multiply_convert_fusion.1 = (bf16[10,14,56,1536]{3,2,1,0:T(8,128)(2,1)}, f32[10,14,56,1536]{3,2,1,0:T(8,128)}) fusion(f32[10,14,56,1536]{3,2,1,0:T(8,128)} %get-tuple-element.481, f32[1536]{0:T(1024)S(1)} %copy-done.47, u16[10,56,1536]{2,1,0:T(8,128)(2,1)S(1)} %get-tuple-element.392, u16[10,56,1536]{2,1,0:T(8,128)(2,1)S(1)} %get-tuple-element.391), kind=kLoop, calls=%fused_computation.104 | loop fusion | flops 854999040 | bytes 123869184 | tf_op jit(solution)/shard_map/convert_element_type | solution.py:238
  945.4 48.5 %convert_reduce_fusion.1 = (f32[1536]{0:T(1024)}, bf16[10,14,56,1536]{3,2,1,0:T(8,128)(2,1)}) fusion(f32[10,14,56,1536]{3,2,1,0:T(8,128)} %get-tuple-element.458, bf16[1536,384]{1,0:T(8,128)(2,1)} %all-gather.7.cloned.1.call-done, f32[10,14,56,384]{3,2,1,0:T(8,128)} %param.35, f32[10,14,56,1536]{3,2,1,0:T(8,128)} %get-tuple-element.481, ...), kind=kOutput, calls=%fused_computation.102 | convolution fusion | flops 9456166912 | bytes 133656576 | tf_op jit(solution)/shard_map/dot_general | solution.py:65
  993.9 22.5 multiply_reduce_fusion.2
  1016.5 8.9 fusion.140
  1025.5 11.7 convert_reduce_fusion.4
  1045.3 17.3 fusion.94
  1062.6 11.7 reduce-scatter.19.cloned.1.call-done
  1088.1 20.7 fusion.93
  1108.9 22.4 add_add_fusion.4
  1145.9 10.0 reshape.444
  1162.5 1040.8 %while.33 = (s32[]{:T(128)}, bf16[10,16,49,1152]{3,1,2,0:T(8,128)(2,1)}, f32[10,49,588]{2,1,0:T(8,128)}, pred[10,16,49,49]{3,1,2,0:T(8,128)(4,1)}, bf16[10,16,49...) while((s32[]{:T(128)}, ...), condition=%wide.wide.region_13.14_spmd.clone.clone.clone, body=%wide.wide.region_9.13_spmd.clone.clone.clone.sunk | while | flops 2001090304 | bytes 223960816 | solution.py:294
  1233.6 14.9 copy.209
  1254.8 15.1 copy.210
  1269.9 11.1 multiply_reduce_fusion.10
  1334.6 14.9 copy.209
  1355.8 15.1 copy.210
  1370.9 11.1 multiply_reduce_fusion.10
  1435.6 14.9 copy.209
  1456.8 15.1 copy.210
  1471.9 11.1 multiply_reduce_fusion.10
  1536.6 14.9 copy.209
  1557.8 15.1 copy.210
  1572.9 11.1 multiply_reduce_fusion.10
  1637.6 14.9 copy.209
  1658.8 15.1 copy.210
  1673.9 11.1 multiply_reduce_fusion.10
  1738.6 14.9 copy.209
  1759.8 15.1 copy.210
  1774.9 11.1 multiply_reduce_fusion.10
  1839.6 14.9 copy.209
  1860.8 15.1 copy.210
  1875.9 11.1 multiply_reduce_fusion.10
  1940.6 14.9 copy.209
  1961.9 15.1 copy.210
  1976.9 11.1 multiply_reduce_fusion.10
  2041.6 14.9 copy.209
  2062.9 15.1 copy.210
  2077.9 11.1 multiply_reduce_fusion.10
  2142.7 14.9 copy.209
  2163.9 15.1 copy.210
  2179.0 11.1 multiply_reduce_fusion.10
  2203.3 19.2 copy.100
  2222.5 27.3 %reshape.445 = bf16[10,14,56,1152]{3,2,1,0:T(8,128)(2,1)} reshape(bf16[10,2,7,8,7,1152]{5,4,3,2,1,0:T(8,128)(2,1)} %copy.100) | data formatting | bytes 36126720 | tf_op jit(solution)/shard_map/reshape | solution.py:39
  2249.8 27.3 %reshape_reshape.30 = bf16[7840,1152]{1,0:T(8,128)(2,1)} reshape(bf16[10,2,7,8,7,1152]{5,4,3,2,1,0:T(8,128)(2,1)} %copy.100) | data formatting | bytes 36126720 | tf_op jit(solution)/shard_map/reshape;reshape | solution.py:58
  2277.2 14.1 convolution_convert_fusion.1
  2291.4 13.8 fusion.116
  2314.1 11.0 convert_reduce_fusion.2
  2327.3 9.1 fusion.139
  2343.0 9.7 multiply_reduce_fusion.4
  2363.5 25.1 %convert_reduce_fusion.3 = (f32[384]{0:T(512)S(1)}, f32[10,14,56,384]{3,2,1,0:T(8,128)}) fusion(f32[10,14,56,384]{3,2,1,0:T(8,128)} %param.35, f32[10,14,56]{2,1,0:T(8,128)S(1)} %negate_multiply_fusion.1, f32[10,14,56]{2,1,0:T(8,128)S(1)} %multiply_multiply_fusion.5, f32[10,14,56,384]{3,2,1,0:T(8,128)} %param.20, f32[10,14,56]{2,1,0:T(8,128)S(1)} %copy-done.19, ...), kind=kLoop, calls=%fused_computation.128 | loop fusion | flops 42147456 | bytes 60371072 | tf_op jit(solution)/shard_map/reduce_sum | solution.py:71
  2390.2 40.7 %all-reduce = (f32[384]{0:T(512)}, f32[384]{0:T(512)}, f32[1152]{0:T(1024)}, f32[169,12]{0,1:T(8,128)}, f32[384]{0:T(512)}, /*index=5*/f32[384]{0:T(512)}, f32[384]{0:T(512)}, f32[1536]{0:T(1024)}, f32[384]{0:T(512)}) all-reduce(f32[384]{0:T(512)S(1)} %get-tuple-element.393, ...), channel_id=1, replica_groups=mesh['strip'=4,'canvas'=8] {'strip','canvas'}, use_global_device_ids=true, to_apply=%region_17.18 | all-reduce | flops 7020 | bytes 56160 | tf_op jit(solution)/shard_map/psum | solution.py:354
  (749 shorter events, 1281.7 us)
Async XLA Ops:
  7.2 87.6 %copy-start = (f32[169,12]{0,1:T(8,128)S(1)}, f32[169,12]{0,1:T(8,128)}, u32[]{:S(2)}) copy-start(f32[169,12]{0,1:T(8,128)} %param.26) | copy-start | bytes 24340
  7.2 12.7 copy-start.41
  7.2 12.7 copy-start.50
  7.2 793.8 %all-gather.5.cloned.1.call-start = ((), (), s32[]{:S(2)}) async-start(), calls=%async_computation.8 | async-start | bytes 1327104 | tf_op jit(solution)/shard_map/all_gather | solution.py:128
  19.9 12.5 copy-start.39
  19.9 44.9 %copy-start.40 = (bf16[48,288]{1,0:T(8,128)(2,1)S(1)}, bf16[48,288]{1,0:T(8,128)(2,1)}, u32[]{:S(2)}) copy-start(bf16[48,288]{1,0:T(8,128)(2,1)} %param.24) | copy-start | bytes 82948
  27.3 85.1 %collective-permute-start.1 = (bf16[10,3,56,384]{3,2,1,0:T(8,128)(2,1)}, bf16[10,3,56,384]{3,2,1,0:T(8,128)(2,1)S(1)}, u32[]{:S(2)}, u32[]{:S(2)}) collective-permute-start(bf16[10,3,56,384]{3,2,1,0:T(8,128)(2,1)} %slice.108), channel_id=1, source_target_pairs={{0,24},{8,0},{16,8},{24,16},{1,25},{9,1},{17,9},{25,17},{2,26},{10... | collective-permute-start | bytes 3870728 | tf_op jit(solution)/shard_map/ppermute | solution.py:17
  31.8 71.0 %collective-permute-start = (bf16[10,3,56]{2,1,0:T(4,128)(2,1)}, bf16[10,3,56]{2,1,0:T(4,128)(2,1)S(1)}, u32[]{:S(2)}, u32[]{:S(2)}) collective-permute-start(bf16[10,3,56]{2,1,0:T(4,128)(2,1)} %slice_convert_fusion), channel_id=1, source_target_pairs={{0,24},{8,0},{16,8},{24,16},{1,25},{9,1},{17,9},{25,17},{2,26},{10... | collective-permute-start | bytes 10088 | tf_op jit(solution)/shard_map/ppermute | solution.py:17
  64.7 880.7 %all-gather.7.cloned.1.call-start = ((), (), s32[]{:S(2)}) async-start(), calls=%async_computation.9 | async-start | bytes 1327104 | tf_op jit(solution)/shard_map/all_gather | solution.py:129
  94.4 26.2 %copy-start.16 = (bf16[384,1152]{1,0:T(8,128)(2,1)}, bf16[384,1152]{1,0:T(8,128)(2,1)S(1)}, u32[]{:S(2)}) copy-start(bf16[384,1152]{1,0:T(8,128)(2,1)S(1)} %all_gather.25) | copy-start | bytes 2654212
  101.0 15.6 slice-start.5
  101.9 18.7 copy-start.14
  702.3 18.3 copy-start.20
  702.4 18.3 copy-start.34
  710.5 15.0 copy-start.38
  710.5 50.0 %copy-start.15 = (f32[49,12,49]{2,1,0:T(8,128)S(1)}, f32[49,12,49]{2,1,0:T(8,128)}, u32[]{:S(2)}) copy-start(f32[49,12,49]{2,1,0:T(8,128)} %get-tuple-element.868) | copy-start | bytes 345748
  710.5 50.8 %copy-start.46 = (bf16[48,96]{1,0:T(8,128)(2,1)S(1)}, bf16[48,96]{1,0:T(8,128)(2,1)}, u32[]{:S(2)}) copy-start(bf16[48,96]{1,0:T(8,128)(2,1)} %param.27) | copy-start | bytes 27652
  710.5 73.4 %copy-start.55 = (f32[384]{0:T(512)S(1)}, f32[384]{0:T(512)}, u32[]{:S(2)}) copy-start(f32[384]{0:T(512)} %param.28) | copy-start | bytes 4612
  722.1 70.9 %copy-start.22 = (bf16[10,14,3,384]{3,2,1,0:T(4,128)(2,1)}, bf16[10,14,3,384]{3,2,1,0:T(4,128)(2,1)S(1)}, u32[]{:S(2)}) copy-start(bf16[10,14,3,384]{3,2,1,0:T(4,128)(2,1)S(1)} %slice.114) | copy-start | bytes 967684
  724.2 59.8 %collective-permute-start.2 = (bf16[10,3,56,384]{3,2,1,0:T(8,128)(2,1)S(1)}, bf16[10,3,56,384]{3,2,1,0:T(8,128)(2,1)}, u32[]{:S(2)}, u32[]{:S(2)}) collective-permute-start(bf16[10,3,56,384]{3,2,1,0:T(8,128)(2,1)S(1)} %pad_maximum_fusion.6), channel_id=1, source_target_pairs={{0,8},{8,16},{16,24},{24,0},{1,9},{9,17},{17,25},{25,1},{2,10},{10... | collective-permute-start | bytes 3870728 | tf_op jit(solution)/shard_map/ppermute | solution.py:17
  760.4 313.8 %reduce-scatter.19.cloned.1.call-start = ((), (), s32[]{:S(2)}) async-start(), calls=%async_computation.11 | async-start | bytes 331776 | tf_op jit(solution)/shard_map/reduce_scatter | solution.py:330
  945.4 48.5 %copy-start.54 = (bf16[384,1536]{1,0:T(8,128)(2,1)S(1)}, bf16[384,1536]{1,0:T(8,128)(2,1)}, u32[]{:S(2)}) copy-start(bf16[384,1536]{1,0:T(8,128)(2,1)} %all-gather.5.cloned.1.call-done) | copy-start | bytes 3538948
  993.9 22.5 copy-start.33
  1025.4 11.7 copy-start.6
  1025.4 11.7 copy-start.28
  1025.5 14.3 copy-start.11
  1025.5 14.3 copy-start.23
  1045.2 30.6 %copy-start.27 = (bf16[384,384]{1,0:T(8,128)(2,1)S(1)}, bf16[384,384]{1,0:T(8,128)(2,1)}, u32[]{:S(2)}) copy-start(bf16[384,384]{1,0:T(8,128)(2,1)} %copy-done.26) | copy-start | bytes 884740
  1045.2 91.0 %reduce-scatter.27.cloned.1.call-start = ((), (), s32[]{:S(2)}) async-start(), calls=%async_computation.15 | async-start | bytes 122880
  1075.8 1249.3 %reduce-scatter.21.cloned.1.call-start = ((), (), s32[]{:S(2)}) async-start(), calls=%async_computation.12 | async-start | bytes 1327104 | tf_op jit(solution)/shard_map/reduce_scatter | solution.py:333
  1085.6 52.2 %collective-permute-start.3 = (bf16[10,3,56,384]{3,2,1,0:T(8,128)(2,1)S(1)}, bf16[10,3,56,384]{3,2,1,0:T(8,128)(2,1)S(1)}, u32[]{:S(2)}, u32[]{:S(2)}) collective-permute-start(bf16[10,3,56,384]{3,2,1,0:T(8,128)(2,1)S(1)} %slice.117), channel_id=1, source_target_pairs={{0,24},{8,0},{16,8},{24,16},{1,25},{9,1},{17,9},{25,17},{2,26},{10... | collective-permute-start | bytes 3870728 | tf_op jit(solution)/shard_map/ppermute | solution.py:17
  1088.1 1248.3 %reduce-scatter.23.cloned.1.call-start = ((), (), s32[]{:S(2)}) async-start(), calls=%async_computation.13 | async-start | bytes 1327104 | tf_op jit(solution)/shard_map/reduce_scatter | solution.py:336
  1088.1 20.8 copy-start.57
  1108.8 1252.8 %reduce-scatter.17.cloned.1.call-start = ((), (), s32[]{:S(2)}) async-start(), calls=%async_computation.10 | async-start | bytes 995328 | tf_op jit(solution)/shard_map/reduce_scatter | solution.py:327
  1145.9 16.7 copy-start.13
  1145.9 16.7 copy-start.21
  1145.9 16.7 copy-start.35
  1254.8 26.5 %slice-start = ((s8[7225344]{0:T(1024)(128)(4,1)}), s8[3031040]{0:T(1024)(128)(4,1)S(1)}, s32[]{:S(2)}) async-start(s8[7225344]{0:T(1024)(128)(4,1)} %bitcast.311), calls=%async_computation.18 | async-start | bytes 6062080 | tf_op jit(solution)/shard_map/while
  1269.9 11.4 copy-start.5
  1355.8 26.5 %slice-start = ((s8[7225344]{0:T(1024)(128)(4,1)}), s8[3031040]{0:T(1024)(128)(4,1)S(1)}, s32[]{:S(2)}) async-start(s8[7225344]{0:T(1024)(128)(4,1)} %bitcast.311), calls=%async_computation.18 | async-start | bytes 6062080 | tf_op jit(solution)/shard_map/while
  1370.9 11.4 copy-start.5
  1456.8 26.5 %slice-start = ((s8[7225344]{0:T(1024)(128)(4,1)}), s8[3031040]{0:T(1024)(128)(4,1)S(1)}, s32[]{:S(2)}) async-start(s8[7225344]{0:T(1024)(128)(4,1)} %bitcast.311), calls=%async_computation.18 | async-start | bytes 6062080 | tf_op jit(solution)/shard_map/while
  1557.8 26.5 %slice-start = ((s8[7225344]{0:T(1024)(128)(4,1)}), s8[3031040]{0:T(1024)(128)(4,1)S(1)}, s32[]{:S(2)}) async-start(s8[7225344]{0:T(1024)(128)(4,1)} %bitcast.311), calls=%async_computation.18 | async-start | bytes 6062080 | tf_op jit(solution)/shard_map/while
  1658.8 26.5 %slice-start = ((s8[7225344]{0:T(1024)(128)(4,1)}), s8[3031040]{0:T(1024)(128)(4,1)S(1)}, s32[]{:S(2)}) async-start(s8[7225344]{0:T(1024)(128)(4,1)} %bitcast.311), calls=%async_computation.18 | async-start | bytes 6062080 | tf_op jit(solution)/shard_map/while
  1759.8 26.5 %slice-start = ((s8[7225344]{0:T(1024)(128)(4,1)}), s8[3031040]{0:T(1024)(128)(4,1)S(1)}, s32[]{:S(2)}) async-start(s8[7225344]{0:T(1024)(128)(4,1)} %bitcast.311), calls=%async_computation.18 | async-start | bytes 6062080 | tf_op jit(solution)/shard_map/while
  1860.8 26.5 %slice-start = ((s8[7225344]{0:T(1024)(128)(4,1)}), s8[3031040]{0:T(1024)(128)(4,1)S(1)}, s32[]{:S(2)}) async-start(s8[7225344]{0:T(1024)(128)(4,1)} %bitcast.311), calls=%async_computation.18 | async-start | bytes 6062080 | tf_op jit(solution)/shard_map/while
  1961.9 26.5 %slice-start = ((s8[7225344]{0:T(1024)(128)(4,1)}), s8[3031040]{0:T(1024)(128)(4,1)S(1)}, s32[]{:S(2)}) async-start(s8[7225344]{0:T(1024)(128)(4,1)} %bitcast.311), calls=%async_computation.18 | async-start | bytes 6062080 | tf_op jit(solution)/shard_map/while
  2062.9 26.5 %slice-start = ((s8[7225344]{0:T(1024)(128)(4,1)}), s8[3031040]{0:T(1024)(128)(4,1)S(1)}, s32[]{:S(2)}) async-start(s8[7225344]{0:T(1024)(128)(4,1)} %bitcast.311), calls=%async_computation.18 | async-start | bytes 6062080 | tf_op jit(solution)/shard_map/while
  2163.9 26.5 %slice-start = ((s8[7225344]{0:T(1024)(128)(4,1)}), s8[3031040]{0:T(1024)(128)(4,1)S(1)}, s32[]{:S(2)}) async-start(s8[7225344]{0:T(1024)(128)(4,1)} %bitcast.311), calls=%async_computation.18 | async-start | bytes 6062080 | tf_op jit(solution)/shard_map/while
  2277.2 14.2 copy-start.17
  2291.3 139.6 %reduce-scatter.29.cloned.1.call-start = ((), (), s32[]{:S(2)}) async-start(), calls=%async_computation.16 | async-start | bytes 491520
  2311.2 30.0 %collective-permute-start.4 = (bf16[10,3,56,384]{3,2,1,0:T(8,128)(2,1)}, bf16[10,3,56,384]{3,2,1,0:T(8,128)(2,1)}, u32[]{:S(2)}, u32[]{:S(2)}) collective-permute-start(bf16[10,3,56,384]{3,2,1,0:T(8,128)(2,1)} %fusion.96), channel_id=1, source_target_pairs={{0,8},{8,16},{16,24},{24,0},{1,9},{9,17},{17,25},{25,1},{2,10},{10... | collective-permute-start | bytes 3870728 | tf_op jit(solution)/shard_map/ppermute | solution.py:17
  2327.0 15.9 copy-start.19
  2327.0 15.9 copy-start.42
  2327.0 105.5 %reduce-scatter.31.cloned.1.call-start = ((), (), s32[]{:S(2)}) async-start(), calls=%async_computation.17 | async-start | bytes 245760
  2338.2 95.9 %reduce-scatter.25.cloned.1.call-start = ((), (), s32[]{:S(2)}) async-start(), calls=%async_computation.14 | async-start | bytes 368640
  2341.2 11.5 slice-start.2
  2342.9 12.5 copy-start.3
  2342.9 12.5 copy-start.25
  2363.5 26.7 %copy-start.48 = (f32[384]{0:T(512)S(1)}, f32[384]{0:T(512)}, u32[]{:S(2)}) copy-start(f32[384]{0:T(512)} %get-tuple-element.451) | copy-start | bytes 4612
  2363.5 26.7 %copy-start.49 = (f32[1536]{0:T(1024)S(1)}, f32[1536]{0:T(1024)}, u32[]{:S(2)}) copy-start(f32[1536]{0:T(1024)} %get-tuple-element.483) | copy-start | bytes 18436
  2363.5 26.7 %copy-start.52 = (f32[384]{0:T(512)S(1)}, f32[384]{0:T(512)}, u32[]{:S(2)}) copy-start(f32[384]{0:T(512)} %get-tuple-element.395) | copy-start | bytes 4612
  2363.5 26.7 %copy-start.53 = (f32[384]{0:T(512)S(1)}, f32[384]{0:T(512)}, u32[]{:S(2)}) copy-start(f32[384]{0:T(512)} %get-tuple-element.397) | copy-start | bytes 4612
  2363.5 72.2 %copy-start.1 = (f32[169,12]{0,1:T(8,128)S(1)}, f32[169,12]{0,1:T(8,128)}, u32[]{:S(2)}) copy-start(f32[169,12]{0,1:T(8,128)} %param.26) | copy-start | bytes 24340
  (54 other events, 382.8 us)
Sparse Core Ops, SparseCore 0:
  64.8 28.7 all-gather.4
  760.6 22.0 all-gather.6
  1045.4 28.8 reduce-scatter.18
  1077.6 22.0 reduce-scatter.26
  1101.9 46.7 reduce-scatter.20
  1150.8 30.9 reduce-scatter.22
  2291.4 28.1 reduce-scatter.16
  2327.1 24.8 reduce-scatter.28
  2355.0 23.9 reduce-scatter.30
  2381.9 24.2 reduce-scatter.24
where the time goes:
time: 2460 us; the launch traced here: 2440 us
  matrix products  867 us (35%)
  local copies, waits for them, and re-layouts  786 us (32%)
  other arithmetic  558 us (23%)
  blocking collectives  159 us (6%)
  loops' own time  33.6 us (1%)
    dot_general x10, local copies, waits for them, and re-layouts, backward_block(): jnp.einsum('aqk,aqc->akc', probs.astype(jnp.bfloat16), d_mixed_b, preferr...  151 us
    dot_general x10, local copies, waits for them, and re-layouts, backward_block(): jnp.einsum('aqk,aqc->akc', d_scores, query_b, preferred_element_type=jnp....  149 us
    mul x20, other arithmetic, spread_heads(): values[:, None] * head_mask[None, :, None, :]  144 us
    dot_general x20, matrix products, block_scores(): jnp.einsum('aqc,akc->aqk', query_b, spread_heads(keys_b, head_mask), pref...  142 us
    convert_element_type x1, other arithmetic, body(): hidden = hidden_full.astype(jnp.bfloat16)  113 us
    reduce_sum x10, other arithmetic, fold_heads(): jnp.sum(grads.reshape(group, heads, WIN * WIN, grads.shape[-1]) * head_ma...  111 us
    dot_general x40, matrix products, widen(): return jnp.dot(small, expand, precision=lax.Precision.HIGHEST)  109 us
    another operation x60, local copies, waits for them, and re-layouts, block_scores(): return jnp.where(jnp.tile(allow_b, (1, 1, heads)), raw_scores, masked_score)  92 us
  transfers between devices with their start and end apart: 15, of which 2 were waited for; matrix products, arithmetic and copies ran while one was open for 84% of the time, Pallas kernels for 0%

commit v1 on v0

v1 whole, which is shorter than its diff:
```python
import functools
import math

import jax
import jax.numpy as jnp
from jax import lax
from jax.experimental import pallas as pl
from jax.experimental.pallas import tpu as pltpu
from jax.sharding import PartitionSpec as P

WIN = 7
SHIFT = 3
SIDE = 8
SLOTS = WIN * SIDE
LANES = 64
PACK = 4
STEP = 6
RING = 2 * STEP
NAT = 72

norm_eps = 1e-05
masked_score = -1e30
f32 = jnp.float32
bf16 = jnp.bfloat16


def nn(left, right):
    return lax.dot_general(left, right, (((1,), (0,)), ((), ())), preferred_element_type=f32)


def nt(left, right):
    return lax.dot_general(left, right, (((1,), (1,)), ((), ())), preferred_element_type=f32)


def tn(left, right):
    return lax.dot_general(left, right, (((0,), (0,)), ((), ())), preferred_element_type=f32)


def norm_parts(values):
    centre = values - jnp.mean(values, -1, keepdims=True)
    spread = jnp.mean(centre * centre, -1, keepdims=True)
    inv = lax.rsqrt(spread + norm_eps)
    return centre * inv, inv


def head_rows(channels, heads):
    size = channels // heads
    lane = lax.broadcasted_iota(jnp.int32, (PACK, PACK * size), 1) // size
    row = lax.broadcasted_iota(jnp.int32, (PACK, PACK * size), 0)
    return (lane == row).astype(bf16)


def spread(part, mask, order):
    padded = jnp.concatenate([part, jnp.zeros((LANES - SLOTS, part.shape[1]), part.dtype)], 0)
    return jnp.concatenate([padded * mask[h : h + 1] for h in order], 0)


def flip(wide):
    padded = jnp.concatenate([wide, jnp.zeros((LANES - SLOTS, wide.shape[1]), wide.dtype)], 0)
    half = wide.shape[1] // 2
    stacked = jnp.concatenate([padded[:, :half], padded[:, half:]], 0)
    turned = stacked.T
    return jnp.concatenate([turned[:LANES], turned[LANES:]], 1)


FLIPPED = (0, 2, 1, 3)


def put_rows(nat, row, values):
    nat[row, 8:64] = values
    nat[row, 64:72] = values[:8]


def take_window(nat, w):
    start = SIDE + SHIFT + WIN * w
    return jnp.concatenate([nat[r, start : start + SIDE] for r in range(WIN)], 0)


def put_window(nat, w, values, lanes):
    start = SIDE + SHIFT + WIN * w
    for r in range(WIN):
        nat[r, start : start + SIDE, lanes] = values[r * SIDE : (r + 1) * SIDE]


def take_rows(nat, row):
    head = lax.broadcasted_iota(jnp.int32, (8, nat.shape[2]), 0) < SHIFT
    first = jnp.where(head, nat[row, 64:72], nat[row, 8:16])
    return jnp.concatenate([first, nat[row, 16:64]], 0)


def attend_kernel(local, heads, *refs):
    if local < WIN:
        field, rim, *refs = refs
    else:
        field, *refs = refs
    (ident_k, ident_q, gain, bias, weight, wbias, place, mixed, cells, qkv_out, probs_out, nat, wide, raw) = refs
    windows = qkv_out.shape[2]
    channels = field.shape[3]
    scale = (channels // heads) ** (-0.5) * math.log2(math.e)
    for r in range(local):
        hat, _ = norm_parts(field[0, r])
        put_rows(nat, r, hat * gain[...] + bias[...])
    for r in range(local, WIN):
        put_rows(nat, r, rim[0, r - local].astype(f32))
    x = jnp.concatenate([take_window(nat, w) for w in range(windows)], 0).astype(bf16)
    cells[0, 0] = x
    wide[...] = nn(x, weight[...]) + wbias[...]
    mask = head_rows(channels, heads)
    group = PACK * (channels // heads)
    def part(w, base, p):
        return qkv_out[0, 0, w, :, base + p * group : base + (p + 1) * group]

    packs = [(w, p) for w in range(windows) for p in range(heads // PACK)]

    def first(i):
        w, p = packs[i]
        if p == 0:
            rows = slice(w * SLOTS, (w + 1) * SLOTS)
            qkv_out[0, 0, w, :, :channels] = (wide[rows, :channels] * scale).astype(bf16)
            qkv_out[0, 0, w, :, channels:] = wide[rows, channels:].astype(bf16)
        raw[i % RING] = nt(part(w, channels, p), spread(part(w, 0, p), mask, range(PACK)))

    def second(i):
        w, p = packs[i]
        wide_p = slice(p * PACK * LANES, (p + 1) * PACK * LANES)
        same = ident_k[0, 0, w] == ident_q[0, 0, w : w + 1]
        same = jnp.concatenate([same, same], 1)
        scores = raw[i % RING] + place[:, wide_p]
        scores = jnp.where(same, scores, masked_score)
        expo = jnp.exp2(scores - jnp.max(scores, 0, keepdims=True))
        probs_out[0, 0, w, :, wide_p] = (expo * (1.0 / jnp.sum(expo, 0, keepdims=True))).astype(bf16)

    def third(i):
        w, p = packs[i]
        wide_p = slice(p * PACK * LANES, (p + 1) * PACK * LANES)
        got = nn(flip(probs_out[0, 0, w, :, wide_p]), spread(part(w, 2 * channels, p), mask, FLIPPED))
        put_window(nat, w, got[:SLOTS], slice(p * group, (p + 1) * group))

    for i in range(0, len(packs) + 2 * STEP, STEP):
        for j in range(i, i + STEP):
            if j < len(packs):
                first(j)
        for j in range(i - STEP, i):
            if 0 <= j < len(packs):
                second(j)
        for j in range(i - 2 * STEP, i - STEP):
            if 0 <= j < len(packs):
                third(j)
    for r in range(WIN):
        mixed[0, 0, r] = take_rows(nat, r).astype(bf16)


def attend(local, row_of, steps, field, rim, ident_k, ident_q, gain, bias, weight, wbias, place):
    canvases, _, columns, channels = field.shape
    heads = place.shape[1] // LANES
    windows = columns // WIN
    grid = (canvases, steps)
    whole = lambda a: pl.BlockSpec(a.shape, lambda n, s: (0,) * a.ndim)
    block = lambda *shape: pl.BlockSpec((1, 1) + shape, lambda n, s: (n, s) + (0,) * len(shape))
    specs = [
        pl.BlockSpec(
            (pl.Element(1), pl.Element(local), pl.Element(columns), pl.Element(channels)),
            lambda n, s: (n, row_of(s), 0, 0),
        )
    ]
    args = [field]
    if local < WIN:
        specs.append(pl.BlockSpec((1,) + rim.shape[1:], lambda n, s: (n, 0, 0, 0)))
        args.append(rim)
    specs += [block(windows, SLOTS, 2 * LANES), block(windows, 2 * LANES)]
    specs += [whole(a) for a in (gain, bias, weight, wbias, place)]
    args += [ident_k, ident_q, gain, bias, weight, wbias, place]
    lead = (canvases, steps)
    tokens = canvases * steps * windows * SLOTS
    return pl.pallas_call(
        functools.partial(attend_kernel, local, heads),
        grid=grid,
        in_specs=specs,
        out_specs=[
            block(WIN, columns, channels),
            block(windows * SLOTS, channels),
            block(windows, SLOTS, 3 * channels),
            block(windows, SLOTS, heads * LANES),
        ],
        out_shape=[
            jax.ShapeDtypeStruct(lead + (WIN, columns, channels), bf16),
            jax.ShapeDtypeStruct(lead + (windows * SLOTS, channels), bf16),
            jax.ShapeDtypeStruct(lead + (windows, SLOTS, 3 * channels), bf16),
            jax.ShapeDtypeStruct(lead + (windows, SLOTS, heads * LANES), bf16),
        ],
        scratch_shapes=[
            pltpu.VMEM((WIN, NAT, channels), f32),
            pltpu.VMEM((windows * SLOTS, 3 * channels), f32),
            pltpu.VMEM((RING, SLOTS, PACK * LANES), f32),
        ],
        compiler_params=pltpu.CompilerParams(vmem_limit_bytes=56 << 20),
        cost_estimate=pl.CostEstimate(
            flops=2 * tokens * channels * (3 * channels + 2 * heads * LANES), bytes_accessed=tokens * 9000, transcendentals=0
        ),
        name="attend",
    )(*args)


def tail_probability(size, decay):
    t = pl.reciprocal(1.0 + (0.3275911 * 0.5**0.5) * size, approx=True)
    poly = 0.5 * 1.061405429 * t - 0.5 * 1.453152027
    poly = poly * t + 0.5 * 1.421413741
    poly = poly * t - 0.5 * 0.284496736
    poly = poly * t + 0.5 * 0.254829592
    return poly * t * decay


def gelu_parts(act):
    decay = jnp.exp2(act * act * (-0.5 * math.log2(math.e)))
    tail = tail_probability(jnp.abs(act), decay)
    phi = jnp.where(act >= 0.0, 1.0 - tail, tail)
    return act * phi, phi + act * decay * (1.0 / math.sqrt(2.0 * math.pi))


HIDDEN_STEP = 256
ROWS_STEP = 16


def feed_kernel(pieces, together, rows, *refs):
    mixed_in, refs = refs[: len(pieces)], refs[len(pieces) :]
    field, cot, w_proj, b_proj, gain, bias, w1, b1, w2, b2, *refs = refs
    out, d_mid, refs = refs[0], refs[1], refs[2:]
    rest_out, refs = refs[: len(pieces)], refs[len(pieces) :]
    g1, g2t, gp, gs = refs[:4]
    mix, x_hat, inv_s, mid, n2, n2t, d_out, d_outt, mixt, act, dh, hid, dact, acc, branch = refs[4:]
    columns, channels = field.shape[2], field.shape[3]
    hidden = w1.shape[1]
    tokens = together * rows * columns
    padded = n2.shape[0]

    @pl.when(pl.program_id(0) == 0)
    def _():
        for ref in (g1, g2t, gp, gs):
            ref[...] = jnp.zeros(ref.shape, ref.dtype)
        n2t[channels:] = jnp.ones((n2t.shape[0] - channels, padded), bf16)
        if padded > tokens:
            for ref in (n2, d_out, mix, branch):
                ref[tokens:] = jnp.zeros((padded - tokens, channels), bf16)
            for ref in (hid, dact):
                ref[tokens:] = jnp.zeros((padded - tokens, hidden), bf16)

    places = []
    for c in range(together):
        r = 0
        for i, count in enumerate(pieces):
            for k in range(count):
                places.append((i, c, k, r, (c * rows + r) * columns))
                r += 1
    for a in range(0, len(places), 2):
        pair = places[a : a + 2]
        parts = [mixed_in[i][c, k].astype(f32) for i, c, k, _, _ in pair]
        start = pair[0][4]
        mix[start : start + len(pair) * columns] = jnp.concatenate(parts, 0).astype(bf16)
    mid[...] = nn(mix[:tokens], w_proj[...])
    for i, c, k, r, start in places:
        rows_here = slice(start, start + columns)
        middle = mid[rows_here] + (field[c, r] + b_proj[...])
        mid[rows_here] = middle
        hat, inv = norm_parts(middle)
        x_hat[rows_here] = hat
        inv_s[rows_here] = inv
    for start in range(0, tokens, 112):
        some = slice(start, min(start + 112, tokens))
        n2[some] = (x_hat[some] * gain[...] + bias[...]).astype(bf16)
    for a in range(0, len(places), 2):
        pair = places[a : a + 2]
        start = pair[0][4]
        d_out[start : start + len(pair) * columns] = jnp.concatenate([cot[c, r] for _, c, _, r, _ in pair], 0).astype(bf16)
    n2t[:channels] = n2[...].T
    d_outt[...] = d_out[...].T
    mixt[...] = mix[...].T

    chunks = hidden // HIDDEN_STEP
    for j in range(chunks + 2):
        if j < chunks:
            cols = slice(j * HIDDEN_STEP, (j + 1) * HIDDEN_STEP)
            act[j % 2] = nn(n2[:tokens], w1[:, cols])
            dh[j % 2] = nt(d_out[:tokens], w2[cols])
        if 0 <= j - 1 < chunks:
            cols = slice((j - 1) * HIDDEN_STEP, j * HIDDEN_STEP)
            for start in range(0, tokens, ROWS_STEP):
                some = slice(start, min(start + ROWS_STEP, tokens))
                value, slope = gelu_parts(act[(j - 1) % 2, some] + b1[:, cols])
                hid[some, cols] = value.astype(bf16)
                dact[some, cols] = (dh[(j - 1) % 2, some] * slope).astype(bf16)
        if 0 <= j - 2:
            cols = slice((j - 2) * HIDDEN_STEP, (j - 1) * HIDDEN_STEP)
            g1[:, cols] += nn(n2t[...], dact[:, cols])
            g2t[:, cols] += nn(d_outt[...], hid[:, cols])

    acc[...] = nt(dact[:tokens], w1[...])
    x_out = nn(hid[:tokens], w2[...])
    total = [jnp.zeros((8, channels), f32) for _ in range(4)]
    fold = lambda v: jnp.sum(v.reshape(-1, 8, channels), 0)
    for i, c, k, r, start in places:
        rows_here = slice(start, start + columns)
        out[c, r] = mid[rows_here] + x_out[rows_here] + b2[...]
        hat = x_hat[rows_here]
        back = acc[rows_here]
        scaled = back * gain[...]
        low = jnp.mean(scaled, -1, keepdims=True)
        slope = jnp.mean(scaled * hat, -1, keepdims=True)
        d_middle = cot[c, r] + inv_s[rows_here] * (scaled - low - hat * slope)
        d_mid[c, r] = d_middle
        mid[rows_here] = d_middle
        total[0] += fold(back * hat)
        total[1] += fold(back)
        total[2] += fold(d_middle)
        total[3] += fold(cot[c, r])
    for start in range(0, tokens, 112):
        some = slice(start, min(start + 112, tokens))
        branch[some] = mid[some].astype(bf16)
    for n in range(4):
        gs[n : n + 1] += jnp.sum(total[n], 0, keepdims=True)
    acc[...] = nt(branch[:tokens], w_proj[...])
    gp[...] += nn(mixt[...], branch[...])
    for i, c, k, r, start in places:
        rest_out[i][c, k] = acc[start : start + columns].astype(bf16)


def feed(mixed_parts, first_row, together, field, cot, prev, w_proj, b_proj, gain, bias, w1, b1, w2, b2):
    canvases, _, columns, channels = field.shape
    hidden = w1.shape[1]
    pieces = tuple(count for _, count in mixed_parts)
    rows = sum(pieces)
    tokens = together * rows * columns
    padded = -(-tokens // 128) * 128
    big = pl.BlockSpec(
        (pl.Element(together), pl.Element(rows), pl.Element(columns), pl.Element(channels)),
        lambda n: (n * together, first_row, 0, 0),
    )
    part = lambda count: pl.BlockSpec((together, count, columns, channels), lambda n: (n, 0, 0, 0))
    whole = lambda shape: pl.BlockSpec(shape, lambda n: (0,) * len(shape))
    consts = (w_proj, b_proj, gain, bias, w1, b1, w2, b2)
    args = [a for a, _ in mixed_parts] + [field, cot] + list(consts)
    specs = [part(count) for count in pieces] + [big, big] + [whole(a.shape) for a in consts]
    aliases = {}
    kernel = functools.partial(feed_kernel, pieces, together, rows)
    if prev is not None:
        base = len(args)
        args += list(prev)
        specs += [pl.BlockSpec(memory_space=pl.ANY)] * 2
        aliases = {base: 0, base + 1: 1}
        inner = kernel
        kernel = lambda *refs: inner(*refs[:base], *refs[base + 2 :])
    grads = [(channels + 16, hidden), (channels, hidden), (channels, channels), (8, channels)]
    return pl.pallas_call(
        kernel,
        grid=(canvases // together,),
        in_specs=specs,
        out_specs=[big, big] + [part(count) for count in pieces] + [whole(s) for s in grads],
        out_shape=[jax.ShapeDtypeStruct(field.shape, f32)] * 2
        + [jax.ShapeDtypeStruct((canvases, count, columns, channels), bf16) for count in pieces]
        + [jax.ShapeDtypeStruct(s, f32) for s in grads],
        scratch_shapes=[
            pltpu.VMEM((padded, channels), bf16),
            pltpu.VMEM((tokens, channels), f32),
            pltpu.VMEM((tokens, 1), f32),
            pltpu.VMEM((tokens, channels), f32),
            pltpu.VMEM((padded, channels), bf16),
            pltpu.VMEM((channels + 16, padded), bf16),
            pltpu.VMEM((padded, channels), bf16),
            pltpu.VMEM((channels, padded), bf16),
            pltpu.VMEM((channels, padded), bf16),
            pltpu.VMEM((2, tokens, HIDDEN_STEP), f32),
            pltpu.VMEM((2, tokens, HIDDEN_STEP), f32),
            pltpu.VMEM((padded, hidden), bf16),
            pltpu.VMEM((padded, hidden), bf16),
            pltpu.VMEM((tokens, channels), f32),
            pltpu.VMEM((padded, channels), bf16),
        ],
        input_output_aliases=aliases,
        compiler_params=pltpu.CompilerParams(vmem_limit_bytes=60 << 20),
        cost_estimate=pl.CostEstimate(
            flops=6 * canvases * rows * columns * channels * (2 * hidden + channels),
            bytes_accessed=canvases * rows * columns * channels * 20,
            transcendentals=0,
        ),
        name="feed",
    )(*args)


def unattend_kernel(local, heads, refs):
    rest, refs = refs[0], refs[1:]
    if local < WIN:
        rim, refs = refs[0], refs[1:]
    cells, qkv, probs, field, d_mid, gain, weight, grad = refs[:8]
    refs = refs[8:]
    if local < WIN:
        rim_out, refs = refs[0], refs[1:]
    gw, gb, gt, gs, nat, d_win, raw, ds, wide = refs
    windows = qkv.shape[2]
    channels = field.shape[3]
    scale = (channels // heads) ** (-0.5)
    group = PACK * (channels // heads)
    first_step = (pl.program_id(0) == 0) & (pl.program_id(1) == 0)

    @pl.when(first_step)
    def _():
        for ref in (gw, gb, gt, gs):
            ref[...] = jnp.zeros(ref.shape, ref.dtype)

    for r in range(WIN):
        source = rest[0, 0, r] if local == WIN else (rest[0, r] if r < local else rim[0, r - local])
        put_rows(nat, r, source.astype(f32))
    real = lax.broadcasted_iota(jnp.int32, (SLOTS, 1), 0) % SIDE < WIN
    for w in range(windows):
        d_win[w] = jnp.where(real, take_window(nat, w), 0.0).astype(bf16)
    mask = head_rows(channels, heads)
    packs = [(w, p) for w in range(windows) for p in range(heads // PACK)]

    def part(w, base, p):
        return qkv[0, 0, w, :, base + p * group : base + (p + 1) * group]

    def spread_d(i):
        w, p = packs[i]
        return spread(d_win[w, :, p * group : (p + 1) * group], mask, range(PACK))

    def first(i):
        w, p = packs[i]
        raw[i % RING] = nt(part(w, 2 * channels, p), spread_d(i))

    def second(i):
        w, p = packs[i]
        wide_p = slice(p * PACK * LANES, (p + 1) * PACK * LANES)
        prob = probs[0, 0, w, :, wide_p].astype(f32)
        weighted = prob * raw[i % RING]
        d_score = weighted - prob * jnp.sum(weighted, 0, keepdims=True)
        gt[:, wide_p] += d_score
        ds[i % RING] = d_score.astype(bf16)

    def third(i):
        w, p = packs[i]
        rows = slice(w * SLOTS, (w + 1) * SLOTS)
        wide_p = slice(p * PACK * LANES, (p + 1) * PACK * LANES)
        at = lambda base: slice(base + p * group, base + (p + 1) * group)
        d_score = ds[i % RING]
        wide[rows, at(2 * channels)] = nn(probs[0, 0, w, :, wide_p], spread_d(i))
        wide[rows, at(channels)] = nn(d_score, spread(part(w, 0, p), mask, range(PACK))) * math.log(2.0)
        wide[rows, at(0)] = nn(flip(d_score), spread(part(w, channels, p), mask, FLIPPED))[:SLOTS] * scale

    for i in range(0, len(packs) + 2 * STEP, STEP):
        for j in range(i, i + STEP):
            if j < len(packs):
                first(j)
        for j in range(i - STEP, i):
            if 0 <= j < len(packs):
                second(j)
        for j in range(i - 2 * STEP, i - STEP):
            if 0 <= j < len(packs):
                third(j)

    d_qkv = wide[...].astype(bf16)
    gb[...] += jnp.sum(wide[...], 0, keepdims=True)
    gw[...] += tn(cells[0, 0], d_qkv)
    back = nt(d_qkv, weight[...])
    for w in range(windows):
        put_window(nat, w, back[w * SLOTS : (w + 1) * SLOTS], slice(0, channels))
    total = [jnp.zeros((8, channels), f32) for _ in range(2)]
    fold = lambda v: jnp.sum(v.reshape(-1, 8, channels), 0)
    for r in range(WIN):
        d_normed = take_rows(nat, r)
        if r < local:
            hat, inv = norm_parts(field[0, r])
            scaled = d_normed * gain[...]
            low = jnp.mean(scaled, -1, keepdims=True)
            slope = jnp.mean(scaled * hat, -1, keepdims=True)
            grad[0, r] = d_mid[0, r] + inv * (scaled - low - hat * slope)
            total[0] += fold(d_normed * hat)
            total[1] += fold(d_normed)
        else:
            rim_out[0, r - local] = d_normed.astype(bf16)
    for n in range(2):
        gs[n : n + 1] += jnp.sum(total[n], 0, keepdims=True)


def unattend(local, row_of, steps, rest, rim, cells, qkv, probs, field, d_mid, prev, gain, weight):
    canvases, _, columns, channels = field.shape
    heads = probs.shape[4] // LANES
    windows = columns // WIN
    whole = lambda shape: pl.BlockSpec(shape, lambda n, s: (0,) * len(shape))
    block = lambda *shape: pl.BlockSpec((1, 1) + shape, lambda n, s: (n, s) + (0,) * len(shape))
    line = lambda *shape: pl.BlockSpec((1,) + shape, lambda n, s: (n,) + (0,) * len(shape))
    big = pl.BlockSpec(
        (pl.Element(1), pl.Element(local), pl.Element(columns), pl.Element(channels)),
        lambda n, s: (n, row_of(s), 0, 0),
    )
    if local < WIN:
        args, specs = [rest, rim], [line(local, columns, channels), line(WIN - local, columns, channels)]
    else:
        args, specs = [rest], [block(WIN, columns, channels)]
    args += [cells, qkv, probs, field, d_mid, gain, weight]
    specs += [block(*a.shape[2:]) for a in (cells, qkv, probs)] + [big, big] + [whole(a.shape) for a in (gain, weight)]
    aliases = {}
    kernel = lambda *refs: unattend_kernel(local, heads, refs)
    if prev is not None:
        base = len(args)
        args.append(prev)
        specs.append(pl.BlockSpec(memory_space=pl.ANY))
        aliases = {base: 0}
        inner = kernel
        kernel = lambda *refs: inner(*refs[:base], *refs[base + 1 :])
    outs, out_specs = [jax.ShapeDtypeStruct(field.shape, f32)], [big]
    if local < WIN:
        outs.append(jax.ShapeDtypeStruct((canvases, WIN - local, columns, channels), bf16))
        out_specs.append(line(WIN - local, columns, channels))
    grads = [(channels, 3 * channels), (1, 3 * channels), (SLOTS, heads * LANES), (8, channels)]
    outs += [jax.ShapeDtypeStruct(s, f32) for s in grads]
    out_specs += [whole(s) for s in grads]
    tokens = canvases * steps * windows * SLOTS
    return pl.pallas_call(
        kernel,
        grid=(canvases, steps),
        in_specs=specs,
        out_specs=out_specs,
        out_shape=outs,
        scratch_shapes=[
            pltpu.VMEM((WIN, NAT, channels), f32),
            pltpu.VMEM((windows, SLOTS, channels), bf16),
            pltpu.VMEM((RING, SLOTS, PACK * LANES), f32),
            pltpu.VMEM((RING, SLOTS, PACK * LANES), bf16),
            pltpu.VMEM((windows * SLOTS, 3 * channels), f32),
        ],
        input_output_aliases=aliases,
        compiler_params=pltpu.CompilerParams(vmem_limit_bytes=56 << 20),
        cost_estimate=pl.CostEstimate(
            flops=2 * tokens * channels * (6 * channels + 4 * heads * LANES), bytes_accessed=tokens * 9000, transcendentals=0
        ),
        name="unattend",
    )(*args)


def rim_kernel(d_normed, field, d_mid, gain, _, grad, gs):
    @pl.when(pl.program_id(0) == 0)
    def _():
        gs[...] = jnp.zeros(gs.shape, gs.dtype)

    channels = field.shape[3]
    total = [jnp.zeros((8, channels), f32) for _ in range(2)]
    fold = lambda v: jnp.sum(v.reshape(-1, 8, channels), 0)
    for c in range(field.shape[0]):
        for r in range(field.shape[1]):
            back = d_normed[c, r].astype(f32)
            hat, inv = norm_parts(field[c, r])
            scaled = back * gain[...]
            low = jnp.mean(scaled, -1, keepdims=True)
            slope = jnp.mean(scaled * hat, -1, keepdims=True)
            grad[c, r] = d_mid[c, r] + inv * (scaled - low - hat * slope)
            total[0] += fold(back * hat)
            total[1] += fold(back)
    for n in range(2):
        gs[n : n + 1] += jnp.sum(total[n], 0, keepdims=True)


def rim_grad(d_normed, field, d_mid, gain, prev):
    canvases, rows, columns, channels = d_normed.shape
    together = 2
    big = pl.BlockSpec(
        (pl.Element(together), pl.Element(rows), pl.Element(columns), pl.Element(channels)),
        lambda n: (n * together, 0, 0, 0),
    )
    return pl.pallas_call(
        rim_kernel,
        grid=(canvases // together,),
        in_specs=[
            pl.BlockSpec((together, rows, columns, channels), lambda n: (n, 0, 0, 0)),
            big,
            big,
            pl.BlockSpec(gain.shape, lambda n: (0, 0)),
            pl.BlockSpec(memory_space=pl.ANY),
        ],
        out_specs=[big, pl.BlockSpec((8, channels), lambda n: (0, 0))],
        out_shape=[jax.ShapeDtypeStruct(field.shape, f32), jax.ShapeDtypeStruct((8, channels), f32)],
        input_output_aliases={4: 0},
        name="rim_grad",
    )(d_normed, field, d_mid, gain, prev)


def from_behind(value, axis, steps):
    count = lax.axis_size(axis)
    pairs = [(source, (source + steps) % count) for source in range(count)]
    return lax.ppermute(value, axis, pairs)


def relative_index():
    places = jnp.arange(WIN * WIN, dtype=jnp.int32)
    place_row = places // WIN
    place_col = places % WIN
    return (
        (place_row[:, None] - place_row[None, :] + WIN - 1) * (2 * WIN - 1)
        + place_col[:, None]
        - place_col[None, :]
        + WIN
        - 1
    )


def table_hot(entries):
    key = jnp.arange(SLOTS, dtype=jnp.int32)[:, None]
    query = jnp.arange(LANES, dtype=jnp.int32)[None, :]
    at = (query // SIDE - key // SIDE + WIN - 1) * (2 * WIN - 1) + query % SIDE - key % SIDE + WIN - 1
    real = (key % SIDE < WIN) & (query % SIDE < WIN) & (query < SLOTS)
    return (jnp.where(real, at, -1)[..., None] == jnp.arange(entries, dtype=jnp.int32)).astype(f32)


def window_idents(ident):
    canvases, steps, _, columns = ident.shape
    cells = ident.reshape(canvases, steps, WIN, columns // WIN, WIN).transpose(0, 1, 3, 2, 4)
    lead = cells.shape[:3]
    none = [(0, 0)] * 4
    keys = jnp.pad(cells, none + [(0, SIDE - WIN)], constant_values=-1).reshape(lead + (SLOTS,))
    queries = jnp.pad(cells, none + [(0, SIDE - WIN)], constant_values=-2).reshape(lead + (SLOTS,))
    queries = jnp.pad(queries, [(0, 0)] * 3 + [(0, LANES - SLOTS)], constant_values=-2)
    return jnp.broadcast_to(keys[..., None], lead + (SLOTS, 2 * LANES)), jnp.concatenate([queries, queries], -1)


def body(
    field,
    crop_ids,
    norm1_gain,
    norm1_bias,
    qkv_weight,
    qkv_bias,
    rel_table,
    proj_weight,
    proj_bias,
    norm2_gain,
    norm2_bias,
    fc1_weight,
    fc1_bias,
    fc2_weight,
    fc2_bias,
    cotangent,
):
    canvases, strip_rows, columns, channels = field.shape
    entries, heads = rel_table.shape
    tops = strip_rows // WIN - 1
    row = lambda v: v.reshape(1, -1)

    def gather(weight):
        return lax.all_gather(lax.all_gather(weight, "strip", axis=1, tiled=True), "canvas", axis=0, tiled=True)

    w_qkv, w_proj, w_fc1, w_fc2 = (gather(w) for w in (qkv_weight, proj_weight, fc1_weight, fc2_weight))
    first = field[:, :SHIFT]
    hat, _ = norm_parts(first)
    rim_rows, rim_crops = from_behind(
        ((hat * norm1_gain + norm1_bias).astype(bf16), crop_ids[:, :SHIFT]), "strip", -1
    )
    shifted_crops = jnp.roll(jnp.concatenate([crop_ids[:, SHIFT:], rim_crops], 1), -SHIFT, 2)
    total_rows = strip_rows * lax.axis_size("strip")
    global_rows = lax.axis_index("strip") * strip_rows + jnp.arange(strip_rows, dtype=jnp.int32)
    col_index = jnp.arange(columns, dtype=jnp.int32)
    row_band = (global_rows >= total_rows - WIN).astype(jnp.int32) + (
        global_rows >= total_rows - SHIFT
    ).astype(jnp.int32)
    col_band = (col_index >= columns - WIN).astype(jnp.int32) + (
        col_index >= columns - SHIFT
    ).astype(jnp.int32)
    region = row_band[:, None] * 3 + col_band[None, :]
    ident = (shifted_crops * 9 + region[None]).reshape(canvases, tops + 1, WIN, columns)
    hot = table_hot(entries)
    place = jnp.einsum(
        "kqe,eh->khq", hot, rel_table * math.log2(math.e), precision=lax.Precision.HIGHEST
    ).reshape(SLOTS, heads * LANES)
    gain1, bias1, gain2, bias2 = (row(v) for v in (norm1_gain, norm1_bias, norm2_gain, norm2_bias))
    fixed = (gain1, bias1, w_qkv, row(qkv_bias), place)
    top_row = lambda s: SHIFT + WIN * s
    low_row = strip_rows - (WIN - SHIFT)
    low = WIN - SHIFT

    keys_low, queries_low = window_idents(ident[:, tops:])
    mixed_low, cells_low, qkv_low, probs_low = attend(
        low, lambda s: low_row, 1, field, rim_rows, keys_low, queries_low, *fixed
    )
    mixed_low = mixed_low[:, 0]
    rim_mixed = from_behind(mixed_low[:, low:], "strip", 1)
    if tops:
        keys_top, queries_top = window_idents(ident[:, :tops])
        mixed_top, cells_top, qkv_top, probs_top = attend(
            WIN, top_row, tops, field, None, keys_top, queries_top, *fixed
        )
    feed_fixed = (w_proj, row(proj_bias), gain2, bias2, w_fc1, row(fc1_bias), w_fc2, row(fc2_bias))
    together = max(n for n in (1, 2, 5) if canvases % n == 0)
    out_rim, mid_rim, rest_rim, *grads_rim = feed(
        [(rim_mixed, SHIFT)], 0, together, field, cotangent, None, *feed_fixed
    )
    rim_rest = from_behind(rest_rim, "strip", -1)
    parts = [(mixed_low, low)]
    if tops:
        parts = [(mixed_top.reshape(canvases, tops * WIN, columns, channels), tops * WIN)] + parts
    together = max(n for n in (1, 2) if canvases % n == 0)
    output, d_mid, *others = feed(
        parts, SHIFT, together, field, cotangent, (out_rim, mid_rim), *feed_fixed
    )
    rest_low = others[len(parts) - 1]
    grads_main = others[len(parts) :]
    grad, rim_back, *grads_low = unattend(
        low, lambda s: low_row, 1, rest_low, rim_rest, cells_low, qkv_low, probs_low, field, d_mid, None, gain1, w_qkv
    )
    rim_d_normed = from_behind(rim_back, "strip", 1)
    attn = [grads_low]
    if tops:
        rest_top = others[0].reshape(canvases, tops, WIN, columns, channels)
        grad, *grads_top = unattend(
            WIN, top_row, tops, rest_top, None, cells_top, qkv_top, probs_top, field, d_mid, grad, gain1, w_qkv
        )
        attn.append(grads_top)
    grad, small_rim = rim_grad(rim_d_normed, field, d_mid, gain1, grad)

    g1, g2t, gp, gs = (a + b for a, b in zip(grads_main, grads_rim))
    gw, gb, gt = (sum(g[n] for g in attn) for n in range(3))
    g_norm1 = sum(g[3] for g in attn) + small_rim

    def scatter(value, row_axis):
        part = lax.psum_scatter(value.astype(bf16), "canvas", scatter_dimension=row_axis, tiled=True)
        return lax.psum_scatter(part, "strip", scatter_dimension=1 - row_axis, tiled=True).astype(f32)

    d_qkv = scatter(gw, 0)
    d_proj = scatter(gp, 0)
    d_fc1 = scatter(g1[:channels], 0)
    d_fc2 = scatter(g2t, 1).T
    d_table = jnp.einsum(
        "kqe,khq->eh", hot, gt.reshape(SLOTS, heads, LANES), precision=lax.Precision.HIGHEST
    )
    small = lax.psum(
        (g_norm1[0], g_norm1[1], gb[0], d_table, gs[2], gs[0], gs[1], g1[channels], gs[3]),
        ("strip", "canvas"),
    )
    return (
        output,
        grad,
        small[0],
        small[1],
        d_qkv,
        small[2],
        small[3],
        d_proj,
        small[4],
        small[5],
        small[6],
        d_fc1,
        small[7],
        d_fc2,
        small[8],
    )


def solution(mesh):
    tokens = P("canvas", "strip", None, None)
    weight = P("canvas", "strip")
    in_specs = (
        tokens,
        P("canvas", "strip", None),
        P(),
        P(),
        weight,
        P(),
        P(),
        weight,
        P(),
        P(),
        P(),
        weight,
        P(),
        weight,
        P(),
        tokens,
    )
    out_specs = (
        tokens,
        tokens,
        P(),
        P(),
        weight,
        P(),
        P(),
        weight,
        P(),
        P(),
        P(),
        weight,
        P(),
        weight,
        P(),
    )
    return jax.shard_map(body, mesh=mesh, in_specs=in_specs, out_specs=out_specs, check_vma=False)
```

time: 2460 us -> 595 us (0.24)
  matrix products: 867 us -> 3.6 us
  local copies, waits for them, and re-layouts: 786 us -> 28.5 us
  other arithmetic: 558 us -> 21.1 us
  Pallas kernels: 0 us -> 259 us
  waiting for transfers between devices: 15 us -> 95 us
  loops' own time: 33.6 us -> 0 us
    dot_general x144 -> x2, matrix products: 867 us -> 3.6 us  [the longest x1 2.32 us: body(): jnp.einsum('kqe,eh->khq', hot, rel_table * math.log2(math.e), precision=l...]
    dot_general x20 -> x0, local copies, waits for them, and re-layouts: 299 us -> none  [the longest x10 151 us: backward_block(): jnp.einsum('aqk,aqc->akc', probs.astype(jnp.bfloat16), d_mixed_b, preferr...]
    pallas_call x0 -> x7, Pallas kernels: none -> 259 us  [the longest x2 141 us: feed(): pl.pallas_call(kernel, grid=(canvases // together,), in_specs=specs, out_...]
    reduce_sum x23 -> x2, other arithmetic: 210 us -> 4.33 us  [the longest x1 2.3 us: norm_parts(): spread = jnp.mean(centre * centre, -1, keepdims=True)]
    mul x21 -> x0, other arithmetic: 145 us -> none  [the longest x20 144 us: spread_heads(): values[:, None] * head_mask[None, :, None, :]]
    reshape x20 -> x14, local copies, waits for them, and re-layouts: 143 us -> 6.01 us  [the longest x8 4.58 us: body(): row = lambda v: v.reshape(1, -1)]
    another operation x61 -> x0, local copies, waits for them, and re-layouts: 119 us -> none  [the longest x60 92 us: block_scores(): return jnp.where(jnp.tile(allow_b, (1, 1, heads)), raw_scores, masked_score)]
    convert_element_type x29 -> x7, other arithmetic: 128 us -> 10.5 us  [the longest x3 6.48 us: scatter(): value.astype(bf16)]
  transfers between devices with their start and end apart: 15 -> 15, of which waited for: 2 -> 5; matrix products, arithmetic and copies ran while one was open for 84% -> 8% of each run, Pallas kernels for 0% -> 20%
where the time goes in v1:
time: 595 us; the launch traced here: 586 us
  Pallas kernels  259 us (44%)
  blocking collectives  156 us (26%)
  waiting for transfers between devices  95 us (16%)
  local copies, waits for them, and re-layouts  28.5 us (5%)
  other arithmetic  21.1 us (4%)
  between operations  15.2 us (3%)
  starting transfers between devices  7.89 us (1%)
    pallas_call x2, Pallas kernels, feed(): pl.pallas_call(kernel, grid=(canvases // together,), in_specs=specs, out_...  141 us
    all_gather x4, blocking collectives, gather(): lax.all_gather(weight, 'strip', axis=1, tiled=True)  79.5 us
    pallas_call x2, Pallas kernels, unattend(): pl.pallas_call(kernel, grid=(canvases, steps), in_specs=specs, out_specs=...  66.8 us
    unnamed x14, waiting for transfers between devices  48.5 us
    pallas_call x2, Pallas kernels, attend(): pl.pallas_call(functools.partial(attend_kernel, local, heads), grid=grid,...  44.2 us
    psum x1, blocking collectives, body(): lax.psum((g_norm1[0], g_norm1[1], gb[0], d_table, gs[2], gs[0], gs[1], g1...  38.9 us
    all_gather x2, blocking collectives, gather(): lax.all_gather(lax.all_gather(weight, 'strip', axis=1, tiled=True), 'canv...  37.3 us
    reduce_scatter x3, waiting for transfers between devices, scatter(): lax.psum_scatter(value.astype(bf16), 'canvas', scatter_dimension=row_axis...  35.8 us
  transfers between devices with their start and end apart: 15, of which 5 were waited for; matrix products, arithmetic and copies ran while one was open for 8% of the time, Pallas kernels for 20%

profile of v1, /device:TPU:0, one launch (start us, length us, event | category | flops | bytes accessed | tf_op | source)
XLA Modules:
  0.0 585.7 jit_solution(10935535765982563602)
XLA Ops:
  7.2 0.9 copy.59
  8.1 10.2 %all_gather.30 = bf16[192,384]{0,1:T(8,128)(2,1)S(1)} all-gather(bf16[192,96]{0,1:T(8,128)(2,1)S(1)} %copy.59), channel_id=1, replica_groups=mesh['strip'=4,'canvas'=8] {'strip'}, dimensions={1}, use_global_device_ids=true | all-gather | bytes 184320 | tf_op jit(solution)/shard_map/all_gather | solution.py:646
  18.3 0.8 copy.60
  19.2 0.8 slice.52
  19.9 1.5 collective-permute-start
  21.4 2.0 slice_reduce_fusion
  23.5 2.3 multiply_reduce_fusion
  25.8 2.1 add_convert_fusion
  28.0 1.5 collective-permute-start.1
  29.5 31.1 %all_gather.28 = bf16[48,1536]{1,0:T(8,128)(2,1)} all-gather(bf16[48,384]{1,0:T(8,128)(2,1)S(1)} %copy-done.6), channel_id=1, replica_groups=mesh['strip'=4,'canvas'=8] {'strip'}, dimensions={1}, use_global_device_ids=true | all-gather | bytes 184320 | tf_op jit(solution)/shard_map/all_gather | solution.py:646
  60.7 7.7 %all-gather = bf16[4,288,48]{1,2,0:T(8,128)(2,1)S(1)} all-gather(bf16[1,288,48]{1,2,0:T(8,128)(2,1)S(1)} %bitcast.60), channel_id=1, replica_groups=mesh['strip'=4,'canvas'=8] {'strip'}, dimensions={0}, use_global_device_ids=true | all-gather | bytes 138240 | tf_op jit(solution)/shard_map/all_gather | solution.py:646
  68.7 22.0 %all_gather.25.refs_5_.refs_6_.refs_8_.refs_7_ = bf16[384,1152]{1,0:T(8,128)(2,1)} all-gather(bf16[48,1152]{1,0:T(8,128)(2,1)S(1)} %bitcast.52), channel_id=1, replica_groups=mesh['strip'=4,'canvas'=8] {'canvas'}, dimensions={0}, use_global_device_ids=true | all-gather | bytes 995328 | tf_op jit(solution)/shard_map/all_gather | solution.py:646
  90.8 2.3 fusion.4
  93.2 0.6 reshape.367.refs_3_.refs_4_.refs_7_.refs_6_.gain
  94.4 0.6 reshape.369.refs_6_.refs_7_
  95.0 0.8 reshape.370.refs_7_.refs_8_
  97.0 0.7 pad_add_fusion.2.refs_3_
  97.7 1.7 broadcast_in_dim.13.refs_2_
  99.4 21.9 %attend.3 = (bf16[10,1,7,56,384]{4,3,2,1,0:T(8,128)(2,1)}, bf16[10,1,448,384]{3,2,1,0:T(8,128)(2,1)}, bf16[10,1,8,56,1152]{4,3,2,1,0:T(8,128)(2,1)}, bf16[10,1,8,56,768]{4,3,2,1,0:T(8,128)(2,1)}) custom-call(f32[10,14,56,384]{3,2,1,0:T(8,128)} %field.1, bf16[10,3,56,384]{3,2,1,0:T(8,128)(2,1)} %collective-permute-done.1.refs_1_, ...), custom_call_target="tpu_custom_call" | custom-call | flops 9248440320 | bytes 40320000 | tf_op jit(solution)/shard_map/attend/pallas_call | solution.py:175
  121.4 1.5 slice.71
  122.9 1.4 collective-permute-start.2
  124.2 0.6 reshape.374.refs_4_.refs_5_
  124.8 0.6 reshape.375.refs_5_.refs_6_
  125.9 0.6 reshape.378.refs_10_.refs_11_
  126.5 0.6 reshape.377.refs_8_.refs_9_
  127.1 30.5 %all-gather.1 = bf16[4,96,48]{1,2,0:T(8,128)(2,1)S(1)} all-gather(bf16[1,96,48]{1,2,0:T(8,128)(2,1)S(1)} %bitcast.62), channel_id=1, replica_groups=mesh['strip'=4,'canvas'=8] {'strip'}, dimensions={0}, use_global_device_ids=true | all-gather | bytes 46080 | tf_op jit(solution)/shard_map/all_gather | solution.py:646
  157.7 15.3 %all_gather.27.refs_3_.refs_4_ = bf16[384,384]{1,0:T(8,128)(2,1)} all-gather(bf16[48,384]{1,0:T(8,128)(2,1)S(1)} %bitcast.57), channel_id=1, replica_groups=mesh['strip'=4,'canvas'=8] {'canvas'}, dimensions={0}, use_global_device_ids=true | all-gather | bytes 331776 | tf_op jit(solution)/shard_map/all_gather | solution.py:646
  173.4 0.7 pad_add_fusion.1.refs_2_
  174.1 1.7 broadcast_in_dim.11.refs_1_
  175.8 22.3 %attend.2 = (bf16[10,1,7,56,384]{4,3,2,1,0:T(8,128)(2,1)}, bf16[10,1,448,384]{3,2,1,0:T(8,128)(2,1)}, bf16[10,1,8,56,1152]{4,3,2,1,0:T(8,128)(2,1)}, bf16[10,1,8,56,768]{4,3,2,1,0:T(8,128)(2,1)}) custom-call(f32[10,14,56,384]{3,2,1,0:T(8,128)} %field.1, s32[10,1,8,56,128]{4,3,2,1,0:T(8,128)} %broadcast_in_dim.11.refs_1_, ...), custom_call_target="tpu_custom_call" | custom-call | flops 9248440320 | bytes 40320000 | tf_op jit(solution)/shard_map/attend/pallas_call | solution.py:175
  198.2 1.0 copy-done.25
  199.2 31.7 %feed.2 = (f32[10,14,56,384]{3,2,1,0:T(8,128)}, f32[10,14,56,384]{3,2,1,0:T(8,128)}, bf16[10,3,56,384]{3,2,1,0:T(8,128)(2,1)}, f32[400,1536]{1,0:T(8,128)}, f32[...) custom-call(bf16[10,3,56,384]{3,2,1,0:T(8,128)(2,1)} %copy-done.25, f32[10,14,56,384]{3,2,1,0:T(8,128)} %field.1, ...), custom_call_target="tpu_custom_call" | custom-call | flops 13377208320 | bytes 12902400 | tf_op jit(solution)/shard_map/feed/pallas_call | solution.py:352
  230.9 109.2 %feed.3 = (f32[10,14,56,384]{3,2,1,0:T(8,128)}, f32[10,14,56,384]{3,2,1,0:T(8,128)}, bf16[10,7,56,384]{3,2,1,0:T(8,128)(2,1)}, bf16[10,4,56,384]{3,2,1,0:T(8,128...) custom-call(bf16[10,7,56,384]{3,2,1,0:T(8,128)(2,1)} %bitcast.64, ...), custom_call_target="tpu_custom_call", output_to_operand_aliasing={{0}: (12, {}), {1}: (13, {})} | custom-call | flops 49049763840 | bytes 47308800 | tf_op jit(solution)/shard_map/feed/pallas_call | solution.py:352
  340.2 1.8 add_convert_fusion.3
  342.1 2.0 add_convert_fusion.1
  344.0 1.4 copy.68
  345.5 1.6 collective-permute-start.3
  347.1 24.1 %reduce-scatter.19.cloned.1.call-done = bf16[48,384]{1,0:T(8,128)(2,1)} async-done(((bf16[384,384]{1,0:T(8,128)(2,1)}), bf16[48,384]{1,0:T(8,128)(2,1)}) %reduce-scatter.19.cloned.1.call-update) | async-done | bytes 36880 | tf_op jit(solution)/shard_map/reduce_scatter | solution.py:720
  371.2 1.5 copy.64
  372.8 2.8 add.251
  375.6 1.2 slice.93
  376.8 33.0 %unattend.2 = (f32[10,14,56,384]{3,2,1,0:T(8,128)}, bf16[10,3,56,384]{3,2,1,0:T(8,128)(2,1)}, f32[384,1152]{1,0:T(8,128)}, f32[1,1152]{1,0:T(1,128)}, f32[56,768]{1,0:T(8,128)}, /*index=5*/f32[8,384]{1,0:T(8,128)}) custom-call(bf16[10,4,56,384]{3,2,1,0:T(8,128)(2,1)} %get-tuple-element.56.refs_0_, bf16[10,3,56,384]{3,2,1,0:T(8,128)(2,1)} %collective-permute-done.3.refs_1_, ...), custom_call_target="tpu_custom_call" | custom-call | flops 18496880640 | bytes 40320000 | tf_op jit(solution)/shard_map/unattend/pallas_call | solution.py:516
  409.8 33.8 %unattend.3 = (f32[10,14,56,384]{3,2,1,0:T(8,128)}, f32[384,1152]{1,0:T(8,128)}, f32[1,1152]{1,0:T(1,128)}, f32[56,768]{1,0:T(8,128)}, f32[8,384]{1,0:T(8,128)}) custom-call(bf16[10,1,7,56,384]{4,3,2,1,0:T(8,128)(2,1)} %bitcast.63, bf16[10,1,448,384]{3,2,1,0:T(8,128)(2,1)} %get-tuple-element.64.refs_1_, ...), custom_call_target="tpu_custom_call", output_to_operand_aliasing={{0}: (8, {})} | custom-call | flops 18496880640 | bytes 40320000 | tf_op jit(solution)/shard_map/unattend/pallas_call | solution.py:516
  443.7 2.7 add_convert_fusion.2
  446.5 1.6 collective-permute-start.4
  448.1 1.7 copy.69
  450.0 0.8 copy.65
  450.8 0.6 convert_element_type.62
  451.6 1.3 fusion.5
  452.9 11.7 %reduce-scatter.21.cloned.1.call-done = bf16[48,1536]{1,0:T(8,128)(2,1)} async-done(((bf16[384,1536]{1,0:T(8,128)(2,1)}), bf16[48,1536]{1,0:T(8,128)(2,1)}) %reduce-scatter.21.cloned.1.call-update) | async-done | bytes 147472 | tf_op jit(solution)/shard_map/reduce_scatter | solution.py:720
  464.7 1.8 copy.66
  466.6 10.6 %collective-permute-done.4.d_normed = bf16[10,3,56,384]{3,2,1,0:T(8,128)(2,1)} collective-permute-done((bf16[10,3,56,384]{3,2,1,0:T(8,128)(2,1)}, bf16[10,3,56,384]{3,2,1,0:T(8,128)(2,1)}, u32[]{:S(2)}, u32[]{:S(2)}) %collective-permute-start.4) | collective-permute-done | bytes 1290272 | tf_op jit(solution)/shard_map/ppermute | solution.py:587
  477.2 6.7 %rim_grad.1 = (f32[10,14,56,384]{3,2,1,0:T(8,128)}, f32[8,384]{1,0:T(8,128)}) custom-call(bf16[10,3,56,384]{3,2,1,0:T(8,128)(2,1)} %collective-permute-done.4.d_normed, f32[10,14,56,384]{3,2,1,0:T(8,128)} %field.1, f32[10,14,56,384]{3,2,1,0:T(8,128)} %get-tuple-element.61.refs_6_.refs_5_.d_mid, ...), custom_call_target="tpu_custom_call", output_to_operand_aliasing={{0}: (4, {})} | custom-call | tf_op jit(solution)/shard_map/rim_grad/pallas_call | solution.py:567
  484.0 0.7 add_add_fusion
  484.7 38.9 %all-reduce.6 = (f32[384]{0:T(512)}, f32[384]{0:T(512)}, f32[1152]{0:T(1024)}, f32[169,12]{0,1:T(8,128)}, f32[384]{0:T(512)}, /*index=5*/f32[384]{0:T(512)}, f32[384]{0:T(512)}, f32[1536]{0:T(1024)}, f32[384]{0:T(512)}) all-reduce(f32[384]{0:T(512)S(1)} %get-tuple-element.137, ...), channel_id=1, replica_groups=mesh['strip'=4,'canvas'=8] {'strip','canvas'}, use_global_device_ids=true, to_apply=%region_2.3 | all-reduce | flops 7020 | bytes 56160 | tf_op jit(solution)/shard_map/psum | solution.py:730
  523.6 1.8 copy.62
  525.4 0.8 convert_bitcast_fusion
  526.2 0.7 copy.61
  527.0 22.9 %reduce-scatter.29.cloned.1.call-done = bf16[384,48]{1,0:T(8,128)(2,1)} async-done(((bf16[1536,48]{1,0:T(8,128)(2,1)}), bf16[384,48]{1,0:T(8,128)(2,1)}) %reduce-scatter.29.cloned.1.call-update) | async-done | bytes 36880
  549.8 1.0 copy.67
  550.8 0.6 convert_element_type.63
  551.5 25.4 %reduce-scatter.25.cloned.1.call-done = bf16[288,48]{1,0:T(8,128)(2,1)} async-done(((bf16[1152,48]{1,0:T(8,128)(2,1)}), bf16[288,48]{1,0:T(8,128)(2,1)}) %reduce-scatter.25.cloned.1.call-update) | async-done | bytes 27664
  576.9 1.0 copy.63
  577.9 0.6 convert_element_type.60
  (124 shorter events, 4.1 us)
Async XLA Ops:
  7.2 191.0 %all-gather.7.cloned.1.call-start = ((), (), s32[]{:S(2)}) async-start(), calls=%async_computation.9 | async-start | bytes 1327104 | tf_op jit(solution)/shard_map/all_gather | solution.py:646
  19.1 179.0 %all-gather.5.cloned.1.call-start = ((), (), s32[]{:S(2)}) async-start(), calls=%async_computation.8 | async-start | bytes 1327104 | tf_op jit(solution)/shard_map/all_gather | solution.py:646
  19.9 5.9 %copy-start.15 = (f32[384]{0:T(512)S(1)}, f32[384]{0:T(512)}, u32[]{:S(2)}) copy-start(f32[384]{0:T(512)} %param.18) | copy-start | bytes 4612
  19.9 5.9 %copy-start.16 = (f32[384]{0:T(512)S(1)}, f32[384]{0:T(512)}, u32[]{:S(2)}) copy-start(f32[384]{0:T(512)} %param.19) | copy-start | bytes 4612
  19.9 75.8 %collective-permute-start = (s32[10,3,56]{2,1,0:T(4,128)S(1)}, s32[10,3,56]{2,1,0:T(4,128)S(1)}, u32[]{:S(2)}, u32[]{:S(2)}) collective-permute-start(s32[10,3,56]{2,1,0:T(4,128)S(1)} %slice.52), channel_id=1, source_target_pairs={{0,24},{8,0},{16,8},{24,16},{1,25},{9,1},{17,9},{25,17},{2,26},{10... | collective-permute-start | bytes 20168 | tf_op jit(solution)/shard_map/ppermute | solution.py:587
  25.8 3.7 copy-start.6
  25.8 34.9 %copy-start.7 = (bf16[48,288]{1,0:T(8,128)(2,1)S(1)}, bf16[48,288]{1,0:T(8,128)(2,1)}, u32[]{:S(2)}) copy-start(bf16[48,288]{1,0:T(8,128)(2,1)} %param.20) | copy-start | bytes 82948
  25.8 65.0 %copy-start.26 = (f32[169,12]{0,1:T(8,128)S(1)}, f32[169,12]{0,1:T(8,128)}, u32[]{:S(2)}) copy-start(f32[169,12]{0,1:T(8,128)} %param.22) | copy-start | bytes 24340
  27.9 66.4 %copy-start.5 = (s32[10,14,56]{2,1,0:T(8,128)S(1)}, s32[10,14,56]{2,1,0:T(8,128)}, u32[]{:S(2)}) copy-start(s32[10,14,56]{2,1,0:T(8,128)} %param.17) | copy-start | bytes 94084
  28.0 66.4 %copy-start.18 = (f32[1152]{0:T(1024)S(1)}, f32[1152]{0:T(1024)}, u32[]{:S(2)}) copy-start(f32[1152]{0:T(1024)} %param.21) | copy-start | bytes 13828
  28.0 69.7 %collective-permute-start.1 = (bf16[10,3,56,384]{3,2,1,0:T(8,128)(2,1)S(1)}, bf16[10,3,56,384]{3,2,1,0:T(8,128)(2,1)}, u32[]{:S(2)}, u32[]{:S(2)}) collective-permute-start(bf16[10,3,56,384]{3,2,1,0:T(8,128)(2,1)S(1)} %add_convert_fusion), channel_id=1, source_target_pairs={{0,24},{8,0},{16,8},{24,16},{1,25},{9,1},{17,9},{25,17},{2,26},{10... | collective-permute-start | bytes 3870728 | tf_op jit(solution)/shard_map/ppermute | solution.py:587
  60.6 310.6 %reduce-scatter.19.cloned.1.call-start = ((), (), s32[]{:S(2)}) async-start(), calls=%async_computation.11 | async-start | bytes 331776 | tf_op jit(solution)/shard_map/reduce_scatter | solution.py:720
  90.8 2.3 copy-start.8
  121.3 2.9 copy-start.21
  121.4 3.5 copy-start.22
  121.4 4.0 copy-start.23
  121.4 4.6 copy-start.24
  121.4 5.1 copy-start.17
  121.4 5.7 copy-start.14
  122.9 75.3 %collective-permute-start.2 = (bf16[10,3,56,384]{3,2,1,0:T(8,128)(2,1)S(1)}, bf16[10,3,56,384]{3,2,1,0:T(8,128)(2,1)S(1)}, u32[]{:S(2)}, u32[]{:S(2)}) collective-permute-start(bf16[10,3,56,384]{3,2,1,0:T(8,128)(2,1)S(1)} %slice.71), channel_id=1, source_target_pairs={{0,8},{8,16},{16,24},{24,0},{1,9},{9,17},{17,25},{25,1},{2,10},{10... | collective-permute-start | bytes 3870728 | tf_op jit(solution)/shard_map/ppermute | solution.py:587
  198.2 1.1 copy-start.25
  230.9 109.3 %copy-start.2 = (f32[384,384]{1,0:T(8,128)S(1)}, f32[384,384]{1,0:T(8,128)}, u32[]{:S(2)}) copy-start(f32[384,384]{1,0:T(8,128)} %get-tuple-element.80) | copy-start | bytes 1769476
  230.9 111.2 %copy-start = (f32[384,1536]{1,0:T(8,128)S(1)}, f32[384,1536]{1,0:T(8,128)}, u32[]{:S(2)}) copy-start(f32[384,1536]{1,0:T(8,128)} %get-tuple-element.86) | copy-start | bytes 7077892
  342.0 106.1 %reduce-scatter.31.cloned.1.call-start = ((), (), s32[]{:S(2)}) async-start(), calls=%async_computation.17 | async-start | bytes 1327104
  345.5 104.5 %reduce-scatter.27.cloned.1.call-start = ((), (), s32[]{:S(2)}) async-start(), calls=%async_computation.15 | async-start | bytes 122880
  345.5 31.3 %collective-permute-start.3 = (bf16[10,3,56,384]{3,2,1,0:T(8,128)(2,1)}, bf16[10,3,56,384]{3,2,1,0:T(8,128)(2,1)}, u32[]{:S(2)}, u32[]{:S(2)}) collective-permute-start(bf16[10,3,56,384]{3,2,1,0:T(8,128)(2,1)} %get-tuple-element.57), channel_id=1, source_target_pairs={{0,24},{8,0},{16,8},{24,16},{1,25},{9,1},{17,9},{25,17},{2,26},{10... | collective-permute-start | bytes 3870728 | tf_op jit(solution)/shard_map/ppermute | solution.py:587
  372.7 92.0 %reduce-scatter.21.cloned.1.call-start = ((), (), s32[]{:S(2)}) async-start(), calls=%async_computation.12 | async-start | bytes 1327104 | tf_op jit(solution)/shard_map/reduce_scatter | solution.py:720
  376.8 146.8 %reduce-scatter.17.cloned.1.call-start = ((), (), s32[]{:S(2)}) async-start(), calls=%async_computation.10 | async-start | bytes 995328 | tf_op jit(solution)/shard_map/reduce_scatter | solution.py:720
  409.8 33.8 %copy-start.1 = (f32[384,1152]{1,0:T(8,128)S(1)}, f32[384,1152]{1,0:T(8,128)}, u32[]{:S(2)}) copy-start(f32[384,1152]{1,0:T(8,128)} %get-tuple-element.73) | copy-start | bytes 5308420
  443.6 4.4 copy-start.10
  443.6 4.4 copy-start.11
  443.7 7.8 %copy-start.3 = (f32[56,768]{1,0:T(8,128)S(1)}, f32[56,768]{1,0:T(8,128)}, u32[]{:S(2)}) copy-start(f32[56,768]{1,0:T(8,128)} %get-tuple-element.77) | copy-start | bytes 516100
  443.7 7.8 %copy-start.4 = (f32[56,768]{1,0:T(8,128)S(1)}, f32[56,768]{1,0:T(8,128)}, u32[]{:S(2)}) copy-start(f32[56,768]{1,0:T(8,128)} %get-tuple-element.78) | copy-start | bytes 516100
  443.7 7.9 %copy-start.19 = (f32[1,1152]{1,0:T(1,128)S(1)}, f32[1,1152]{1,0:T(1,128)}, u32[]{:S(2)}) copy-start(f32[1,1152]{1,0:T(1,128)} %get-tuple-element.75) | copy-start | bytes 13828
  443.7 7.9 %copy-start.20 = (f32[1,1152]{1,0:T(1,128)S(1)}, f32[1,1152]{1,0:T(1,128)}, u32[]{:S(2)}) copy-start(f32[1,1152]{1,0:T(1,128)} %get-tuple-element.76) | copy-start | bytes 13828
  443.7 7.9 %copy-start.9 = (s32[56,64]{1,0:T(8,128)S(1)}, s32[56,64]{1,0:T(8,128)}, u32[]{:S(2)}) copy-start(s32[56,64]{1,0:T(8,128)} %copy-done.8) | copy-start | bytes 43012
  446.4 79.0 %reduce-scatter.23.cloned.1.call-start = ((), (), s32[]{:S(2)}) async-start(), calls=%async_computation.13 | async-start | bytes 245760 | tf_op jit(solution)/shard_map/reduce_scatter | solution.py:721
  446.5 30.7 %collective-permute-start.4 = (bf16[10,3,56,384]{3,2,1,0:T(8,128)(2,1)}, bf16[10,3,56,384]{3,2,1,0:T(8,128)(2,1)}, u32[]{:S(2)}, u32[]{:S(2)}) collective-permute-start(bf16[10,3,56,384]{3,2,1,0:T(8,128)(2,1)} %get-tuple-element.62), channel_id=1, source_target_pairs={{0,8},{8,16},{16,24},{24,0},{1,9},{9,17},{17,25},{25,1},{2,10},{10... | collective-permute-start | bytes 3870728 | tf_op jit(solution)/shard_map/ppermute | solution.py:587
  449.9 100.0 %reduce-scatter.29.cloned.1.call-start = ((), (), s32[]{:S(2)}) async-start(), calls=%async_computation.16 | async-start | bytes 491520
  466.5 110.4 %reduce-scatter.25.cloned.1.call-start = ((), (), s32[]{:S(2)}) async-start(), calls=%async_computation.14 | async-start | bytes 368640
  477.2 6.8 %copy-start.12 = (f32[8,384]{1,0:T(8,128)S(1)}, f32[8,384]{1,0:T(8,128)}, u32[]{:S(2)}) copy-start(f32[8,384]{1,0:T(8,128)} %get-tuple-element.70) | copy-start | bytes 36868
  477.2 6.8 %copy-start.13 = (f32[8,384]{1,0:T(8,128)S(1)}, f32[8,384]{1,0:T(8,128)}, u32[]{:S(2)}) copy-start(f32[8,384]{1,0:T(8,128)} %get-tuple-element.71) | copy-start | bytes 36868
Sparse Core Ops, SparseCore 0:
  19.2 22.9 all-gather.6
  60.7 28.3 all-gather.4
  342.1 28.9 reduce-scatter.18
  373.4 30.9 reduce-scatter.30
  407.7 21.9 reduce-scatter.26
  431.9 32.7 reduce-scatter.20
  466.9 29.9 reduce-scatter.16
  499.9 22.3 reduce-scatter.22
  525.4 24.4 reduce-scatter.28
  552.7 24.1 reduce-scatter.24

commit v2 on v1

--- a/solution.py
+++ b/solution.py
@@ -93,7 +93,10 @@
         field, rim, *refs = refs
     else:
         field, *refs = refs
-    (ident_k, ident_q, gain, bias, weight, wbias, place, mixed, cells, qkv_out, probs_out, nat, wide, raw) = refs
+    ident_k, ident_q, gain, bias, weight, wbias, place, mixed, *refs = refs
+    if local < WIN:
+        mixed_rim, *refs = refs
+    cells, qkv_out, probs_out, nat, wide, raw = refs
     windows = qkv_out.shape[2]
     channels = field.shape[3]
     scale = (channels // heads) ** (-0.5) * math.log2(math.e)
@@ -101,7 +104,7 @@
         hat, _ = norm_parts(field[0, r])
         put_rows(nat, r, hat * gain[...] + bias[...])
     for r in range(local, WIN):
-        put_rows(nat, r, rim[0, r - local].astype(f32))
+        put_rows(nat, r, rim[0, r - local].astype(f32) * gain[...] + bias[...])
     x = jnp.concatenate([take_window(nat, w) for w in range(windows)], 0).astype(bf16)
     cells[0, 0] = x
     wide[...] = nn(x, weight[...]) + wbias[...]
@@ -147,7 +150,10 @@
             if 0 <= j < len(packs):
                 third(j)
     for r in range(WIN):
-        mixed[0, 0, r] = take_rows(nat, r).astype(bf16)
+        if r < local:
+            mixed[0, 0, r] = take_rows(nat, r).astype(bf16)
+        else:
+            mixed_rim[0, 0, r - local] = take_rows(nat, r).astype(bf16)
 
 
 def attend(local, row_of, steps, field, rim, ident_k, ident_q, gain, bias, weight, wbias, place):
@@ -171,19 +177,20 @@
     specs += [whole(a) for a in (gain, bias, weight, wbias, place)]
     args += [ident_k, ident_q, gain, bias, weight, wbias, place]
     lead = (canvases, steps)
+    runs = [local, WIN - local] if local < WIN else [WIN]
     tokens = canvases * steps * windows * SLOTS
     return pl.pallas_call(
         functools.partial(attend_kernel, local, heads),
         grid=grid,
         in_specs=specs,
         out_specs=[
-            block(WIN, columns, channels),
+            *[block(count, columns, channels) for count in runs],
             block(windows * SLOTS, channels),
             block(windows, SLOTS, 3 * channels),
             block(windows, SLOTS, heads * LANES),
         ],
         out_shape=[
-            jax.ShapeDtypeStruct(lead + (WIN, columns, channels), bf16),
+            *[jax.ShapeDtypeStruct(lead + (count, columns, channels), bf16) for count in runs],
             jax.ShapeDtypeStruct(lead + (windows * SLOTS, channels), bf16),
             jax.ShapeDtypeStruct(lead + (windows, SLOTS, 3 * channels), bf16),
             jax.ShapeDtypeStruct(lead + (windows, SLOTS, heads * LANES), bf16),
@@ -221,13 +228,18 @@
 ROWS_STEP = 16
 
 
-def feed_kernel(pieces, together, rows, *refs):
+def feed_kernel(pieces, together, rows, chain, *refs):
     mixed_in, refs = refs[: len(pieces)], refs[len(pieces) :]
     field, cot, w_proj, b_proj, gain, bias, w1, b1, w2, b2, *refs = refs
+    if chain:
+        before, refs = refs[:4], refs[4:]
     out, d_mid, refs = refs[0], refs[1], refs[2:]
     rest_out, refs = refs[: len(pieces)], refs[len(pieces) :]
-    g1, g2t, gp, gs = refs[:4]
-    mix, x_hat, inv_s, mid, n2, n2t, d_out, d_outt, mixt, act, dh, hid, dact, acc, branch = refs[4:]
+    if chain:
+        packed, gs, g1, g2t, gp, *refs = refs
+    else:
+        g1, g2t, gp, gs, *refs = refs
+    mix, x_hat, inv_s, mid, n2, n2t, d_out, d_outt, mixt, act, dh, hid, dact, acc, branch = refs
     columns, channels = field.shape[2], field.shape[3]
     hidden = w1.shape[1]
     tokens = together * rows * columns
@@ -235,8 +247,13 @@
 
     @pl.when(pl.program_id(0) == 0)
     def _():
-        for ref in (g1, g2t, gp, gs):
-            ref[...] = jnp.zeros(ref.shape, ref.dtype)
+        if chain:
+            for ref, old in zip((g1, g2t, gp), before):
+                pltpu.sync_copy(old, ref)
+            gs[:8] = before[3][...]
+        else:
+            for ref in (g1, g2t, gp, gs):
+                ref[...] = jnp.zeros(ref.shape, ref.dtype)
         n2t[channels:] = jnp.ones((n2t.shape[0] - channels, padded), bf16)
         if padded > tokens:
             for ref in (n2, d_out, mix, branch):
@@ -322,6 +339,25 @@
     for i, c, k, r, start in places:
         rest_out[i][c, k] = acc[start : start + columns].astype(bf16)
 
+    if chain:
+
+        @pl.when(pl.program_id(0) == pl.num_programs(0) - 1)
+        def _():
+            lines, strips, height, _ = packed.shape
+            sums = g1[channels : channels + 1]
+            for k in range(hidden // channels):
+                gs[8 + k : 9 + k] = sums[:, k * channels : (k + 1) * channels]
+            wide, tall = hidden // strips, channels // strips
+            deep = hidden // lines
+            for c in range(lines):
+                own = slice(c * height, (c + 1) * height)
+                for m in range(strips):
+                    parts = [gp[own, m * tall : (m + 1) * tall], g1[own, m * wide : (m + 1) * wide]]
+                    for k in range(tall // height):
+                        at = m * tall + k * height
+                        parts.append(g2t[at : at + height, c * deep : (c + 1) * deep])
+                    packed[c, m] = jnp.concatenate(parts, 1).astype(bf16)
+
 
 def feed(mixed_parts, first_row, together, field, cot, prev, w_proj, b_proj, gain, bias, w1, b1, w2, b2):
     canvases, _, columns, channels = field.shape
@@ -340,24 +376,32 @@
     args = [a for a, _ in mixed_parts] + [field, cot] + list(consts)
     specs = [part(count) for count in pieces] + [big, big] + [whole(a.shape) for a in consts]
     aliases = {}
-    kernel = functools.partial(feed_kernel, pieces, together, rows)
+    kernel = functools.partial(feed_kernel, pieces, together, rows, prev is not None)
+    grads = [(channels + 16, hidden), (channels, hidden), (channels, channels)]
     if prev is not None:
         base = len(args)
         args += list(prev)
-        specs += [pl.BlockSpec(memory_space=pl.ANY)] * 2
+        specs += [pl.BlockSpec(memory_space=pl.ANY)] * 5 + [whole(prev[5].shape)]
         aliases = {base: 0, base + 1: 1}
         inner = kernel
         kernel = lambda *refs: inner(*refs[:base], *refs[base + 2 :])
-    grads = [(channels + 16, hidden), (channels, hidden), (channels, channels), (8, channels)]
+        strips, lines = lax.axis_size("strip"), lax.axis_size("canvas")
+        shard = (lines, strips, channels // lines, (channels + 2 * hidden) // strips)
+        sums = [jax.ShapeDtypeStruct(shard, bf16), jax.ShapeDtypeStruct((16, channels), f32)]
+        held = [pltpu.VMEM(g, f32) for g in grads]
+    else:
+        sums = [jax.ShapeDtypeStruct(g, f32) for g in grads + [(8, channels)]]
+        held = []
     return pl.pallas_call(
         kernel,
         grid=(canvases // together,),
         in_specs=specs,
-        out_specs=[big, big] + [part(count) for count in pieces] + [whole(s) for s in grads],
+        out_specs=[big, big] + [part(count) for count in pieces] + [whole(g.shape) for g in sums],
         out_shape=[jax.ShapeDtypeStruct(field.shape, f32)] * 2
         + [jax.ShapeDtypeStruct((canvases, count, columns, channels), bf16) for count in pieces]
-        + [jax.ShapeDtypeStruct(s, f32) for s in grads],
-        scratch_shapes=[
+        + sums,
+        scratch_shapes=held
+        + [
             pltpu.VMEM((padded, channels), bf16),
             pltpu.VMEM((tokens, channels), f32),
             pltpu.VMEM((tokens, 1), f32),
@@ -388,7 +432,7 @@
 def unattend_kernel(local, heads, refs):
     rest, refs = refs[0], refs[1:]
     if local < WIN:
-        rim, refs = refs[0], refs[1:]
+        rim, rim_hat, refs = refs[0], refs[1], refs[2:]
     cells, qkv, probs, field, d_mid, gain, weight, grad = refs[:8]
     refs = refs[8:]
     if local < WIN:
@@ -475,11 +519,13 @@
             total[1] += fold(d_normed)
         else:
             rim_out[0, r - local] = d_normed.astype(bf16)
+            total[0] += fold(d_normed * rim_hat[0, r - local].astype(f32))
+            total[1] += fold(d_normed)
     for n in range(2):
         gs[n : n + 1] += jnp.sum(total[n], 0, keepdims=True)
 
 
-def unattend(local, row_of, steps, rest, rim, cells, qkv, probs, field, d_mid, prev, gain, weight):
+def unattend(local, row_of, steps, rest, rim, rim_hat, cells, qkv, probs, field, d_mid, prev, gain, weight):
     canvases, _, columns, channels = field.shape
     heads = probs.shape[4] // LANES
     windows = columns // WIN
@@ -491,7 +537,8 @@
         lambda n, s: (n, row_of(s), 0, 0),
     )
     if local < WIN:
-        args, specs = [rest, rim], [line(local, columns, channels), line(WIN - local, columns, channels)]
+        args = [rest, rim, rim_hat]
+        specs = [line(local, columns, channels)] + [line(WIN - local, columns, channels)] * 2
     else:
         args, specs = [rest], [block(WIN, columns, channels)]
     args += [cells, qkv, probs, field, d_mid, gain, weight]
@@ -535,26 +582,14 @@
     )(*args)
 
 
-def rim_kernel(d_normed, field, d_mid, gain, _, grad, gs):
-    @pl.when(pl.program_id(0) == 0)
-    def _():
-        gs[...] = jnp.zeros(gs.shape, gs.dtype)
-
-    channels = field.shape[3]
-    total = [jnp.zeros((8, channels), f32) for _ in range(2)]
-    fold = lambda v: jnp.sum(v.reshape(-1, 8, channels), 0)
+def rim_kernel(d_normed, field, d_mid, gain, _, grad):
     for c in range(field.shape[0]):
         for r in range(field.shape[1]):
-            back = d_normed[c, r].astype(f32)
             hat, inv = norm_parts(field[c, r])
-            scaled = back * gain[...]
+            scaled = d_normed[c, r].astype(f32) * gain[...]
             low = jnp.mean(scaled, -1, keepdims=True)
             slope = jnp.mean(scaled * hat, -1, keepdims=True)
             grad[c, r] = d_mid[c, r] + inv * (scaled - low - hat * slope)
-            total[0] += fold(back * hat)
-            total[1] += fold(back)
-    for n in range(2):
-        gs[n : n + 1] += jnp.sum(total[n], 0, keepdims=True)
 
 
 def rim_grad(d_normed, field, d_mid, gain, prev):
@@ -574,11 +609,233 @@
             pl.BlockSpec(gain.shape, lambda n: (0, 0)),
             pl.BlockSpec(memory_space=pl.ANY),
         ],
-        out_specs=[big, pl.BlockSpec((8, channels), lambda n: (0, 0))],
-        out_shape=[jax.ShapeDtypeStruct(field.shape, f32), jax.ShapeDtypeStruct((8, channels), f32)],
+        out_specs=big,
+        out_shape=jax.ShapeDtypeStruct(field.shape, f32),
         input_output_aliases={4: 0},
+        cost_estimate=pl.CostEstimate(flops=d_normed.size * 30, bytes_accessed=d_normed.size * 14, transcendentals=0),
         name="rim_grad",
     )(d_normed, field, d_mid, gain, prev)
+
+
+MESH = pl.DeviceIdType.MESH
+
+
+def gather_kernel(strips, lines, shard, qkv, proj, fc1, fc2, blocks, send_sem, recv_sem):
+    strip, line = lax.axis_index("strip"), lax.axis_index("canvas")
+    core, chip, chips = line % 2, line // 2, lines // 2
+    other = (strip, line + 1 - 2 * core)
+    along = [((strip + n) % strips, line) for n in range(1, strips)]
+    across = [(strip, ((chip + n) % chips) * 2 + core) for n in range(1, chips)]
+    partners = along + across + [other]
+
+    barrier = pltpu.get_barrier_semaphore()
+    for partner in partners:
+        pl.semaphore_signal(barrier, inc=1, device_id=partner, device_id_type=MESH)
+    pl.semaphore_wait(barrier, len(partners))
+
+    place = lambda n, m: (((chip + n) % chips) * 2 + core, (strip + m) % strips)
+    twin = lambda n, m: (((chip + n) % chips) * 2 + 1 - core, (strip + m) % strips)
+    number = lambda n, m, kind: (kind * chips + n) * strips + m
+
+    def copy(source, at, target, index):
+        return pltpu.make_async_remote_copy(
+            src_ref=source,
+            dst_ref=blocks.at[at[0], at[1]],
+            send_sem=send_sem.at[index],
+            recv_sem=recv_sem.at[index],
+            device_id=target,
+            device_id_type=MESH,
+        )
+
+    def arrived(at, index):
+        copy(blocks.at[at[0], at[1]], at, other, index).wait_recv()
+
+    sent = []
+
+    def send(source, at, target, index):
+        sent.append(copy(source, at, target, index))
+        sent[-1].start()
+
+    for n in range(1, chips):
+        send(shard, place(0, 0), across[n - 1], number(chips - n, 0, 0))
+    for m in range(1, strips):
+        send(shard, place(0, 0), along[m - 1], number(0, strips - m, 0))
+    send(shard, place(0, 0), other, number(0, 0, 1))
+    blocks[line, strip] = shard[...]
+    for n in range(1, chips):
+        at = place(n, 0)
+        arrived(at, number(n, 0, 0))
+        for m in range(1, strips):
+            send(blocks.at[at[0], at[1]], at, along[m - 1], number(n, strips - m, 0))
+        send(blocks.at[at[0], at[1]], at, other, number(n, 0, 1))
+    for n in range(chips):
+        for m in range(1, strips):
+            at = place(n, m)
+            arrived(at, number(n, m, 0))
+            send(blocks.at[at[0], at[1]], at, other, number(n, m, 1))
+    for n in range(chips):
+        for m in range(strips):
+            arrived(twin(n, m), number(n, m, 1))
+    for c in sent:
+        c.wait_send()
+    rows = shard.shape[0]
+    if len(qkv.shape) == 2:
+        sizes = [ref.shape[1] // strips for ref in (qkv, proj, fc1)]
+        edges = [0, sizes[0], sizes[0] + sizes[1], sum(sizes)]
+        narrow = fc2.shape[1] // strips
+        for c in range(lines):
+            for ref, low, high in zip((qkv, proj, fc1), edges, edges[1:]):
+                ref[c * rows : (c + 1) * rows] = jnp.concatenate([blocks[c, m, :, low:high] for m in range(strips)], 1)
+            deep = fc2.shape[0] // lines // rows
+            for k in range(deep):
+                low = edges[3] + k * narrow
+                fc2[(c * deep + k) * rows : (c * deep + k + 1) * rows] = jnp.concatenate(
+                    [blocks[c, m, :, low : low + narrow] for m in range(strips)], 1
+                )
+    else:
+        qkv[...] = blocks[...]
+
+
+def gather_weights(qkv, proj, fc1, fc2):
+    strips, lines = lax.axis_size("strip"), lax.axis_size("canvas")
+    rows = qkv.shape[0]
+    deep = fc2.shape[0] // rows
+    narrow = fc2.shape[1]
+    shard = jnp.concatenate([qkv, proj, fc1] + [fc2[k * rows : (k + 1) * rows] for k in range(deep)], 1)
+    joined = rows % 16 == 0
+    full = [jax.ShapeDtypeStruct((lines * w.shape[0], strips * w.shape[1]), w.dtype) for w in (qkv, proj, fc1, fc2)]
+    blocks = (lines, strips) + shard.shape
+    kernel = functools.partial(gather_kernel, strips, lines)
+    if not joined:
+        full = [jax.ShapeDtypeStruct(blocks, shard.dtype)]
+        inner = kernel
+        kernel = lambda shard, out, *refs: inner(shard, out, None, None, None, *refs)
+    vmem = pl.BlockSpec(memory_space=pltpu.VMEM)
+    got = pl.pallas_call(
+        kernel,
+        in_specs=[vmem],
+        out_specs=[vmem] * len(full),
+        out_shape=full,
+        scratch_shapes=[pltpu.VMEM(blocks, shard.dtype)]
+        + [pltpu.SemaphoreType.DMA((lines * strips,))] * 2,
+        compiler_params=pltpu.CompilerParams(collective_id=0, has_side_effects=True, vmem_limit_bytes=40 << 20),
+        name="gather_weights",
+    )(shard)
+    if joined:
+        return got
+    got, at, out = got[0], 0, []
+    for w in (qkv, proj, fc1):
+        part = got[..., at : at + w.shape[1]]
+        out.append(part.transpose(0, 2, 1, 3).reshape(lines * rows, -1))
+        at += w.shape[1]
+    part = got[..., at:].reshape(lines, strips, rows, deep, narrow)
+    out.append(part.transpose(0, 3, 2, 1, 4).reshape(lines * rows * deep, -1))
+    return out
+
+
+def reduce_kernel(strips, lines, first, second, small, out, small_out, *refs):
+    line_bits, strip_bits = lines.bit_length() - 1, strips.bit_length() - 1
+    phases = line_bits + strip_bits
+    acc, *refs = refs
+    sends, recvs, kept = refs[:phases], refs[phases : 2 * phases], refs[2 * phases : 3 * phases]
+    small_sends, small_recv, send_sem, recv_sem, small_send_sem, small_recv_sem = refs[3 * phases :]
+    strip, line = lax.axis_index("strip"), lax.axis_index("canvas")
+    partners, bits = [], []
+    for t in range(line_bits):
+        bit = (line // 2**t) % 2
+        bits.append(bit)
+        partners.append((strip, line + (1 - 2 * bit) * 2**t))
+    for t in reversed(range(strip_bits)):
+        bit = (strip // 2**t) % 2
+        bits.append(bit)
+        partners.append((strip + (1 - 2 * bit) * 2**t, line))
+
+    barrier = pltpu.get_barrier_semaphore()
+    for partner in partners:
+        pl.semaphore_signal(barrier, inc=1, device_id=partner, device_id_type=MESH)
+    small_sends[0] = small[...]
+    acc[...] = first[...] + second[...] if second is not None else first[...]
+    pl.semaphore_wait(barrier, phases)
+
+    def copy(source, target, send, recv, partner):
+        return pltpu.make_async_remote_copy(
+            src_ref=source, dst_ref=target, send_sem=send, recv_sem=recv, device_id=partner, device_id_type=MESH
+        )
+
+    current = acc
+    for t in range(phases):
+        bit = bits[t]
+        small_copy = copy(
+            small_sends.at[t], small_recv.at[t], small_send_sem.at[t], small_recv_sem.at[t], partners[t]
+        )
+        small_copy.start()
+        if t < line_bits:
+            count = sends[t].shape[0]
+            for k in range(count):
+                sends[t][k] = current[2 * k + 1 - bit].astype(bf16)
+        else:
+            width = current.shape[-1] // 2
+            block = current[0] if t == line_bits else current[...]
+            for k in range(2):
+                kept[t][k] = block[:, k * width : (k + 1) * width]
+            sends[t][...] = kept[t][1 - bit].astype(bf16)
+        big_copy = copy(sends[t], recvs[t], send_sem.at[t], recv_sem.at[t], partners[t])
+        big_copy.start()
+        small_copy.wait()
+        summed = small_sends[t] + small_recv[t]
+        if t + 1 < phases:
+            small_sends[t + 1] = summed
+        else:
+            small_out[...] = summed
+        big_copy.wait()
+        if t < line_bits:
+            for k in range(count):
+                kept[t][k] = current[2 * k + bit] + recvs[t][k].astype(f32)
+            current = kept[t]
+        else:
+            total = kept[t][bit] + recvs[t][...].astype(f32)
+            if t + 1 < phases:
+                acc_next = kept[t].at[0]
+                acc_next[...] = total
+                current = acc_next
+            else:
+                out[...] = total
+
+
+def reduce_weight(first, second, small):
+    strips, lines = lax.axis_size("strip"), lax.axis_size("canvas")
+    rows, columns = first.shape
+    rows //= lines
+    line_bits, strip_bits = lines.bit_length() - 1, strips.bit_length() - 1
+    phases = line_bits + strip_bits
+    sends = [(lines >> (t + 1), rows, columns) for t in range(line_bits)]
+    sends += [(rows, columns >> (t + 1)) for t in range(strip_bits)]
+    kept = [(lines >> (t + 1), rows, columns) for t in range(line_bits)]
+    kept += [(2, rows, columns >> (t + 1)) for t in range(strip_bits)]
+    blocked = lambda a: a.reshape(lines, rows, columns)
+    args = [blocked(first)] + ([] if second is None else [blocked(second)]) + [small]
+    kernel = functools.partial(reduce_kernel, strips, lines)
+    if second is None:
+        inner = kernel
+        kernel = lambda first, *refs: inner(first, None, *refs)
+    vmem = pl.BlockSpec(memory_space=pltpu.VMEM)
+    return pl.pallas_call(
+        kernel,
+        in_specs=[vmem] * len(args),
+        out_specs=[vmem] * 2,
+        out_shape=[
+            jax.ShapeDtypeStruct((rows, columns // strips), f32),
+            jax.ShapeDtypeStruct(small.shape, f32),
+        ],
+        scratch_shapes=[pltpu.VMEM((lines, rows, columns), f32)]
+        + [pltpu.VMEM(s, bf16) for s in sends]
+        + [pltpu.VMEM(s, bf16) for s in sends]
+        + [pltpu.VMEM(s, f32) for s in kept]
+        + [pltpu.VMEM((phases,) + small.shape, f32)] * 2
+        + [pltpu.SemaphoreType.DMA((phases,))] * 4,
+        compiler_params=pltpu.CompilerParams(collective_id=1, has_side_effects=True, vmem_limit_bytes=40 << 20),
+        name="reduce_weight",
+    )(*args)
 
 
 def from_behind(value, axis, steps):
@@ -642,15 +899,10 @@
     tops = strip_rows // WIN - 1
     row = lambda v: v.reshape(1, -1)
 
-    def gather(weight):
-        return lax.all_gather(lax.all_gather(weight, "strip", axis=1, tiled=True), "canvas", axis=0, tiled=True)
-
-    w_qkv, w_proj, w_fc1, w_fc2 = (gather(w) for w in (qkv_weight, proj_weight, fc1_weight, fc2_weight))
+    w_qkv, w_proj, w_fc1, w_fc2 = gather_weights(qkv_weight, proj_weight, fc1_weight, fc2_weight)
     first = field[:, :SHIFT]
     hat, _ = norm_parts(first)
-    rim_rows, rim_crops = from_behind(
-        ((hat * norm1_gain + norm1_bias).astype(bf16), crop_ids[:, :SHIFT]), "strip", -1
-    )
+    rim_hat, rim_crops = from_behind((hat.astype(bf16), crop_ids[:, :SHIFT]), "strip", -1)
     shifted_crops = jnp.roll(jnp.concatenate([crop_ids[:, SHIFT:], rim_crops], 1), -SHIFT, 2)
     total_rows = strip_rows * lax.axis_size("strip")
     global_rows = lax.axis_index("strip") * strip_rows + jnp.arange(strip_rows, dtype=jnp.int32)
@@ -673,64 +925,80 @@
     low_row = strip_rows - (WIN - SHIFT)
     low = WIN - SHIFT
 
-    keys_low, queries_low = window_idents(ident[:, tops:])
-    mixed_low, cells_low, qkv_low, probs_low = attend(
-        low, lambda s: low_row, 1, field, rim_rows, keys_low, queries_low, *fixed
-    )
-    mixed_low = mixed_low[:, 0]
-    rim_mixed = from_behind(mixed_low[:, low:], "strip", 1)
     if tops:
         keys_top, queries_top = window_idents(ident[:, :tops])
         mixed_top, cells_top, qkv_top, probs_top = attend(
             WIN, top_row, tops, field, None, keys_top, queries_top, *fixed
         )
+    keys_low, queries_low = window_idents(ident[:, tops:])
+    mixed_low, mixed_rim, cells_low, qkv_low, probs_low = attend(
+        low, lambda s: low_row, 1, field, rim_hat, keys_low, queries_low, *fixed
+    )
+    mixed_rim = from_behind(mixed_rim[:, 0], "strip", 1)
     feed_fixed = (w_proj, row(proj_bias), gain2, bias2, w_fc1, row(fc1_bias), w_fc2, row(fc2_bias))
-    together = max(n for n in (1, 2, 5) if canvases % n == 0)
-    out_rim, mid_rim, rest_rim, *grads_rim = feed(
-        [(rim_mixed, SHIFT)], 0, together, field, cotangent, None, *feed_fixed
-    )
-    rim_rest = from_behind(rest_rim, "strip", -1)
-    parts = [(mixed_low, low)]
+    parts = [(mixed_low[:, 0], low)]
     if tops:
         parts = [(mixed_top.reshape(canvases, tops * WIN, columns, channels), tops * WIN)] + parts
     together = max(n for n in (1, 2) if canvases % n == 0)
-    output, d_mid, *others = feed(
-        parts, SHIFT, together, field, cotangent, (out_rim, mid_rim), *feed_fixed
-    )
+    output, d_mid, *others = feed(parts, SHIFT, together, field, cotangent, None, *feed_fixed)
     rest_low = others[len(parts) - 1]
     grads_main = others[len(parts) :]
-    grad, rim_back, *grads_low = unattend(
-        low, lambda s: low_row, 1, rest_low, rim_rest, cells_low, qkv_low, probs_low, field, d_mid, None, gain1, w_qkv
+    together = max(n for n in (1, 2, 5) if canvases % n == 0)
+    output, d_mid, rest_rim, packed, gs = feed(
+        [(mixed_rim, SHIFT)], 0, together, field, cotangent, (output, d_mid, *grads_main), *feed_fixed
     )
-    rim_d_normed = from_behind(rim_back, "strip", 1)
-    attn = [grads_low]
+    rest_rim = from_behind(rest_rim, "strip", -1)
+    shard = lax.psum_scatter(packed, "canvas", scatter_dimension=0)
+    shard = lax.psum_scatter(shard, "strip", scatter_dimension=0).astype(f32)
+    grad, attn = None, []
     if tops:
         rest_top = others[0].reshape(canvases, tops, WIN, columns, channels)
         grad, *grads_top = unattend(
-            WIN, top_row, tops, rest_top, None, cells_top, qkv_top, probs_top, field, d_mid, grad, gain1, w_qkv
+            WIN, top_row, tops, rest_top, None, None, cells_top, qkv_top, probs_top, field, d_mid, grad, gain1, w_qkv
         )
         attn.append(grads_top)
-    grad, small_rim = rim_grad(rim_d_normed, field, d_mid, gain1, grad)
-
-    g1, g2t, gp, gs = (a + b for a, b in zip(grads_main, grads_rim))
-    gw, gb, gt = (sum(g[n] for g in attn) for n in range(3))
-    g_norm1 = sum(g[3] for g in attn) + small_rim
-
-    def scatter(value, row_axis):
-        part = lax.psum_scatter(value.astype(bf16), "canvas", scatter_dimension=row_axis, tiled=True)
-        return lax.psum_scatter(part, "strip", scatter_dimension=1 - row_axis, tiled=True).astype(f32)
-
-    d_qkv = scatter(gw, 0)
-    d_proj = scatter(gp, 0)
-    d_fc1 = scatter(g1[:channels], 0)
-    d_fc2 = scatter(g2t, 1).T
+    grad, rim_back, *grads_low = unattend(
+        low,
+        lambda s: low_row,
+        1,
+        rest_low,
+        rest_rim,
+        rim_hat,
+        cells_low,
+        qkv_low,
+        probs_low,
+        field,
+        d_mid,
+        grad,
+        gain1,
+        w_qkv,
+    )
+    attn.append(grads_low)
+    rim_back = from_behind(rim_back, "strip", 1)
+    grad = rim_grad(rim_back, field, d_mid, gain1, grad)
+
+    n_proj, n_fc1 = proj_weight.shape[1], fc1_weight.shape[1]
+    d_proj = shard[:, :n_proj]
+    d_fc1 = shard[:, n_proj : n_proj + n_fc1]
+    width = fc2_weight.shape[0]
+    d_fc2 = jnp.concatenate(
+        [shard[:, at : at + width] for at in range(n_proj + n_fc1, shard.shape[1], width)], 0
+    ).T
+
+    gb, gt, g_norm1 = (sum(g[n] for g in attn) for n in (1, 2, 3))
     d_table = jnp.einsum(
         "kqe,khq->eh", hot, gt.reshape(SLOTS, heads, LANES), precision=lax.Precision.HIGHEST
     )
-    small = lax.psum(
-        (g_norm1[0], g_norm1[1], gb[0], d_table, gs[2], gs[0], gs[1], g1[channels], gs[3]),
-        ("strip", "canvas"),
-    )
+    g_fc1 = gs[8 : 8 + fc1_bias.shape[0] // channels]
+    pieces = (g_norm1[0], g_norm1[1], gb[0], d_table, gs[2], gs[0], gs[1], g_fc1.reshape(-1), gs[3])
+    packed = jnp.concatenate([v.reshape(-1) for v in pieces])
+    count = -(-packed.size // 1024) * 1024
+    packed = jnp.pad(packed, (0, count - packed.size)).reshape(-1, 128)
+    d_qkv, packed = reduce_weight(grads_low[0], grads_top[0] if tops else None, packed)
+    packed, small, at = packed.reshape(-1), [], 0
+    for v in pieces:
+        small.append(packed[at : at + v.size].reshape(v.shape))
+        at += v.size
     return (
         output,
         grad,

time: 595 us -> 425 us (0.71); the launches traced: 586 us -> 423 us
  blocking collectives: 156 us -> 0 us
  waiting for transfers between devices: 95 us -> 11.2 us
  Pallas kernels: 259 us -> 334 us
  other arithmetic: 21.1 us -> 13.1 us
    all_gather x6 -> x0, blocking collectives: 117 us -> none  [the longest x4 79.5 us: gather(): lax.all_gather(weight, 'strip', axis=1, tiled=True)]
    pallas_call x0 -> x2, Pallas kernels: none -> 70.8 us  [the longest x1 42.8 us: gather_weights(): pl.pallas_call(kernel, in_specs=[vmem], out_specs=[vmem] * len(full), out...]
    psum x1 -> x0, blocking collectives: 38.9 us -> none  [body(): lax.psum((g_norm1[0], g_norm1[1], gb[0], d_table, gs[2], gs[0], gs[1], g1...]
    unnamed x14 -> x3, waiting for transfers between devices: 48.5 us -> 11.2 us
    reduce_scatter x4 -> x1, waiting for transfers between devices: 35.8 us -> 0.01 us  [body(): shard = lax.psum_scatter(packed, 'canvas', scatter_dimension=0)]
    ppermute x5, waiting for transfers between devices: 10.6 us -> 0.01 us  [from_behind(): return lax.ppermute(value, axis, pairs)]
    convert_element_type x7 -> x2, other arithmetic: 10.5 us -> 3.24 us  [the longest x1 2.34 us: body(): hat.astype(bf16)]
    unnamed x68 -> x61, local copies, waits for them, and re-layouts: 14.2 us -> 9.17 us
  transfers between devices with their start and end apart: 15 -> 7, of which waited for: 5 -> 1; matrix products, arithmetic and copies ran while one was open for 8% -> 10% of each run, Pallas kernels for 20% -> 65%
where the time goes in v2:
time: 425 us; the launch traced here: 423 us
  Pallas kernels  334 us (79%)
  local copies, waits for them, and re-layouts  34.2 us (8%)
  between operations  14.8 us (3%)
  other arithmetic  13.1 us (3%)
  waiting for transfers between devices  11.2 us (3%)
  matrix products  8.09 us (2%)
  starting transfers between devices  7.59 us (2%)
    pallas_call x2, Pallas kernels, feed(): pl.pallas_call(kernel, grid=(canvases // together,), in_specs=specs, out_...  145 us
    pallas_call x2, Pallas kernels, unattend(): pl.pallas_call(kernel, grid=(canvases, steps), in_specs=specs, out_specs=...  67.1 us
    pallas_call x2, Pallas kernels, attend(): pl.pallas_call(functools.partial(attend_kernel, local, heads), grid=grid,...  44 us
    pallas_call x1, Pallas kernels, gather_weights(): pl.pallas_call(kernel, in_specs=[vmem], out_specs=[vmem] * len(full), out...  42.8 us
    pallas_call x1, Pallas kernels, reduce_weight(): pl.pallas_call(kernel, in_specs=[vmem] * len(args), out_specs=[vmem] * 2,...  28 us
    unnamed x3, waiting for transfers between devices  11.2 us
    unnamed x61, local copies, waits for them, and re-layouts  9.17 us
  transfers between devices with their start and end apart: 7, of which 1 were waited for; matrix products, arithmetic and copies ran while one was open for 10% of the time, Pallas kernels for 65%

profile of v2, /device:TPU:0, one launch (start us, length us, event | category | flops | bytes accessed | tf_op | source)
XLA Modules:
  0.0 422.8 jit_solution(10650210474959319301)
XLA Ops:
  7.2 0.8 slice.106
  8.0 3.9 collective-permute-start.1
  11.9 2.0 slice_reduce_fusion
  14.0 2.3 multiply_reduce_fusion
  16.4 2.3 multiply_convert_fusion
  18.8 0.6 collective-permute-start
  19.6 2.3 fusion.6
  22.0 0.6 reshape.391.refs_4_.refs_3_.refs_6_.refs_8_.gain
  22.6 0.6 reshape.392.refs_5_.refs_4_
  23.2 0.6 reshape.395.refs_5_.refs_4_
  23.7 0.6 reshape.396.refs_6_.refs_5_
  24.3 0.6 reshape.397.refs_7_.refs_6_
  24.9 0.6 reshape.399.refs_11_.refs_10_
  25.4 0.6 reshape.393.refs_7_.refs_6_
  26.0 0.6 reshape.398.refs_9_.refs_8_
  26.6 0.8 reshape.394.refs_8_.refs_7_
  27.5 42.8 %gather_weights.1 = (bf16[384,1152]{1,0:T(8,128)(2,1)S(1)}, bf16[384,384]{1,0:T(8,128)(2,1)S(1)}, bf16[384,1536]{1,0:T(8,128)(2,1)S(1)}, bf16[1536,384]{1,0:T(8,128)(2,1)S(1)}) custom-call(bf16[48,1152]{1,0:T(8,128)(2,1)S(1)} %concatenate.32.shard), custom_call_target="tpu_custom_call" | custom-call | tf_op jit(solution)/shard_map/gather_weights/pallas_call | solution.py:714
  70.4 1.0 copy-done.2
  71.4 1.0 copy-done.3
  72.4 0.7 copy-done.4
  73.2 0.9 copy-done.8
  74.4 0.1 reshape.400
  74.8 0.2 fusion.18
  74.9 0.1 reshape.401
  75.5 0.7 pad_add_fusion.2.refs_2_
  76.2 0.7 pad_add_fusion.1.refs_3_
  76.9 1.7 broadcast_in_dim.13.refs_1_
  78.7 22.3 %attend.3 = (bf16[10,1,7,56,384]{4,3,2,1,0:T(8,128)(2,1)}, bf16[10,1,448,384]{3,2,1,0:T(8,128)(2,1)}, bf16[10,1,8,56,1152]{4,3,2,1,0:T(8,128)(2,1)}, bf16[10,1,8,56,768]{4,3,2,1,0:T(8,128)(2,1)}) custom-call(f32[10,14,56,384]{3,2,1,0:T(8,128)} %field.1, s32[10,1,8,56,128]{4,3,2,1,0:T(8,128)} %broadcast_in_dim.13.refs_1_, ...), custom_call_target="tpu_custom_call" | custom-call | flops 9248440320 | bytes 40320000 | tf_op jit(solution)/shard_map/attend/pallas_call | solution.py:182
  101.0 1.8 broadcast_in_dim.11.refs_2_
  102.7 21.7 %attend.2 = (bf16[10,1,4,56,384]{4,3,2,1,0:T(8,128)(2,1)}, bf16[10,1,3,56,384]{4,3,2,1,0:T(8,128)(2,1)}, bf16[10,1,448,384]{3,2,1,0:T(8,128)(2,1)}, bf16[10,1,8,...) custom-call(f32[10,14,56,384]{3,2,1,0:T(8,128)} %field.1, ...), custom_call_target="tpu_custom_call" | custom-call | flops 9248440320 | bytes 40320000 | tf_op jit(solution)/shard_map/attend/pallas_call | solution.py:182
  124.4 0.3 collective-permute-start.2
  124.8 109.4 %feed.2 = (f32[10,14,56,384]{3,2,1,0:T(8,128)}, f32[10,14,56,384]{3,2,1,0:T(8,128)}, bf16[10,7,56,384]{3,2,1,0:T(8,128)(2,1)}, bf16[10,4,56,384]{3,2,1,0:T(8,128...) custom-call(bf16[10,7,56,384]{3,2,1,0:T(8,128)(2,1)} %bitcast.54, ...), custom_call_target="tpu_custom_call" | custom-call | flops 49049763840 | bytes 47308800 | tf_op jit(solution)/shard_map/feed/pallas_call | solution.py:395
  234.2 1.0 copy-done.9
  235.3 35.9 %feed.3 = (f32[10,14,56,384]{3,2,1,0:T(8,128)}, f32[10,14,56,384]{3,2,1,0:T(8,128)}, bf16[10,3,56,384]{3,2,1,0:T(8,128)(2,1)}, bf16[8,4,48,864]{3,2,1,0:T(8,128)(2,1)}, f32[16,384]{1,0:T(8,128)}) custom-call(bf16[10,3,56,384]{3,2,1,0:T(8,128)(2,1)} %copy-done.9, f32[10,14,56,384]{3,2,1,0:T(8,128)} %field.1, ...), custom_call_target="tpu_custom_call", output_to_operand_aliasing={{0}: (11, {}), {1}: (12, {})} | custom-call | flops 13377208320 | bytes 12902400 | tf_op jit(solution)/shard_map/feed/pallas_call | solution.py:395
  271.3 0.8 slice.120
  272.1 0.4 copy-done.25
  272.5 2.6 collective-permute-start.3
  275.2 33.7 %unattend.2 = (f32[10,14,56,384]{3,2,1,0:T(8,128)}, f32[384,1152]{1,0:T(8,128)}, f32[1,1152]{1,0:T(1,128)}, f32[56,768]{1,0:T(8,128)}, f32[8,384]{1,0:T(8,128)}) custom-call(bf16[10,1,7,56,384]{4,3,2,1,0:T(8,128)(2,1)} %bitcast.53, bf16[10,1,448,384]{3,2,1,0:T(8,128)(2,1)} %get-tuple-element.75.refs_1_, ...), custom_call_target="tpu_custom_call" | custom-call | flops 18496880640 | bytes 40320000 | tf_op jit(solution)/shard_map/unattend/pallas_call | solution.py:563
  308.9 1.1 copy-done.26
  309.9 33.4 %unattend.3 = (f32[10,14,56,384]{3,2,1,0:T(8,128)}, bf16[10,3,56,384]{3,2,1,0:T(8,128)(2,1)}, f32[384,1152]{1,0:T(8,128)}, f32[1,1152]{1,0:T(1,128)}, f32[56,768]{1,0:T(8,128)}, /*index=5*/f32[8,384]{1,0:T(8,128)}) custom-call(bf16[10,4,56,384]{3,2,1,0:T(8,128)(2,1)} %get-tuple-element.68.refs_0_, ...), custom_call_target="tpu_custom_call", output_to_operand_aliasing={{0}: (10, {})} | custom-call | flops 18496880640 | bytes 40320000 | tf_op jit(solution)/shard_map/unattend/pallas_call | solution.py:563
  343.4 1.5 slice_reduce_fusion.3
  344.9 1.6 add.190
  346.5 1.8 reshape.406
  348.3 5.8 %fusion.7 = f32[169,12]{1,0:T(8,128)} fusion(f32[56,12,64]{2,1,0:T(8,128)} %reshape.406, s32[56,64]{1,0:T(8,128)} %copy-done.15), kind=kOutput, calls=%fused_computation.10 | convolution fusion | flops 88431616 | bytes 194480 | tf_op jit(solution)/shard_map/kqe,khq->eh/dot_general | solution.py:989
  354.1 1.0 reshape.407
  355.1 0.7 add.188
  355.8 0.6 slice_reduce_fusion.1
  356.4 1.3 add_reduce_fusion
  357.7 1.5 concatenate.34
  359.2 0.8 pad_bitcast_fusion.small
  360.0 28.0 %reduce_weight.1 = (f32[48,288]{1,0:T(8,128)S(1)}, f32[56,128]{1,0:T(8,128)S(1)}) custom-call(f32[8,48,1152]{2,1,0:T(8,128)S(1)} %bitcast.43, f32[8,48,1152]{2,1,0:T(8,128)S(1)} %bitcast.42, f32[56,128]{1,0:T(8,128)S(1)} %pad_bitcast_fusion.small), custom_call_target="tpu_custom_call" | custom-call | tf_op jit(solution)/shard_map/reduce_weight/pallas_call | solution.py:822
  388.0 0.6 copy-done.5
  388.6 0.7 slice.150
  389.4 0.7 copy.56
  390.1 1.3 slice_bitcast_fusion.1
  391.4 1.5 fusion.23
  392.9 1.3 slice_bitcast_fusion
  394.2 6.7 %rim_grad.1 = f32[10,14,56,384]{3,2,1,0:T(8,128)} custom-call(bf16[10,3,56,384]{3,2,1,0:T(8,128)(2,1)} %collective-permute-done.4.d_normed, f32[10,14,56,384]{3,2,1,0:T(8,128)} %field.1, f32[10,14,56,384]{3,2,1,0:T(8,128)} %get-tuple-element.73.refs_5_.refs_7_.d_mid, ...), custom_call_target="tpu_custom_call", output_to_operand_aliasing={{}: (4, {})} | custom-call | flops 19353600 | bytes 9031680 | tf_op jit(solution)/shard_map/rim_grad/pallas_call | solution.py:602
  400.9 11.2 %reduce-scatter.7.cloned.1.call-done = bf16[1,48,864]{2,1,0:T(8,128)(2,1)} async-done(((bf16[4,48,864]{2,1,0:T(8,128)(2,1)}), bf16[1,48,864]{2,1,0:T(8,128)(2,1)}) %reduce-scatter.7.cloned.1.call-update) | async-done | bytes 82960
  412.1 0.9 bitcast_convert_fusion
  413.0 0.6 slice.145
  413.6 0.7 slice.149
  414.4 0.7 copy.57
  415.2 0.6 copy.69
  (91 shorter events, 1.8 us)
Async XLA Ops:
  7.2 382.9 %reduce-scatter.5.cloned.1.call-start = ((), (), s32[]{:S(2)}) async-start(), calls=%async_computation.2 | async-start | bytes 3096576 | tf_op jit(solution)/shard_map/reduce_scatter | solution.py:951
  8.0 66.1 %collective-permute-start.1 = (s32[10,3,56]{2,1,0:T(4,128)S(1)}, s32[10,3,56]{2,1,0:T(4,128)S(1)}, u32[]{:S(2)}, u32[]{:S(2)}) collective-permute-start(s32[10,3,56]{2,1,0:T(4,128)S(1)} %slice.106), channel_id=1, source_target_pairs={{0,24},{8,0},{16,8},{24,16},{1,25},{9,1},{17,9},{25,17},{2,26},{10... | collective-permute-start | bytes 20168 | tf_op jit(solution)/shard_map/ppermute | solution.py:844
  16.3 3.2 copy-start.12
  16.3 3.3 copy-start.27
  16.3 5.7 %copy-start.11 = (s32[10,14,56]{2,1,0:T(8,128)S(1)}, s32[10,14,56]{2,1,0:T(8,128)}, u32[]{:S(2)}) copy-start(s32[10,14,56]{2,1,0:T(8,128)} %param.17) | copy-start | bytes 94084
  16.3 5.7 %copy-start.19 = (f32[384]{0:T(512)S(1)}, f32[384]{0:T(512)}, u32[]{:S(2)}) copy-start(f32[384]{0:T(512)} %param.18) | copy-start | bytes 4612
  16.3 6.3 %copy-start.20 = (f32[384]{0:T(512)S(1)}, f32[384]{0:T(512)}, u32[]{:S(2)}) copy-start(f32[384]{0:T(512)} %param.19) | copy-start | bytes 4612
  16.3 6.8 %copy-start.21 = (f32[384]{0:T(512)S(1)}, f32[384]{0:T(512)}, u32[]{:S(2)}) copy-start(f32[384]{0:T(512)} %param.24) | copy-start | bytes 4612
  16.4 7.4 %copy-start.22 = (f32[384]{0:T(512)S(1)}, f32[384]{0:T(512)}, u32[]{:S(2)}) copy-start(f32[384]{0:T(512)} %param.25) | copy-start | bytes 4612
  16.4 7.9 %copy-start.23 = (f32[384]{0:T(512)S(1)}, f32[384]{0:T(512)}, u32[]{:S(2)}) copy-start(f32[384]{0:T(512)} %param.26) | copy-start | bytes 4612
  16.4 8.5 %copy-start.24 = (f32[384]{0:T(512)S(1)}, f32[384]{0:T(512)}, u32[]{:S(2)}) copy-start(f32[384]{0:T(512)} %param.30) | copy-start | bytes 4612
  16.4 9.0 %copy-start.18 = (f32[1152]{0:T(1024)S(1)}, f32[1152]{0:T(1024)}, u32[]{:S(2)}) copy-start(f32[1152]{0:T(1024)} %param.21) | copy-start | bytes 13828
  16.4 9.6 %copy-start.17 = (f32[1536]{0:T(1024)S(1)}, f32[1536]{0:T(1024)}, u32[]{:S(2)}) copy-start(f32[1536]{0:T(1024)} %param.28) | copy-start | bytes 18436
  16.4 11.0 %copy-start.13 = (bf16[48,288]{1,0:T(8,128)(2,1)S(1)}, bf16[48,288]{1,0:T(8,128)(2,1)}, u32[]{:S(2)}) copy-start(bf16[48,288]{1,0:T(8,128)(2,1)} %param.20) | copy-start | bytes 82948
  16.4 11.0 %copy-start.14 = (bf16[48,384]{1,0:T(8,128)(2,1)S(1)}, bf16[48,384]{1,0:T(8,128)(2,1)}, u32[]{:S(2)}) copy-start(bf16[48,384]{1,0:T(8,128)(2,1)} %param.27) | copy-start | bytes 110596
  16.4 11.0 %copy-start.16 = (bf16[48,96]{1,0:T(8,128)(2,1)S(1)}, bf16[48,96]{1,0:T(8,128)(2,1)}, u32[]{:S(2)}) copy-start(bf16[48,96]{1,0:T(8,128)(2,1)} %param.23) | copy-start | bytes 27652
  18.8 82.2 %collective-permute-start = (bf16[10,3,56,384]{3,2,1,0:T(8,128)(2,1)S(1)}, bf16[10,3,56,384]{3,2,1,0:T(8,128)(2,1)}, u32[]{:S(2)}, u32[]{:S(2)}) collective-permute-start(bf16[10,3,56,384]{3,2,1,0:T(8,128)(2,1)S(1)} %multiply_convert_fusion), channel_id=1, source_target_pairs={{0,24},{8,0},{16,8},{24,16},{1,25},{9,1},{17,9},{25,17},{2,26},{10... | collective-permute-start | bytes 3870728 | tf_op jit(solution)/shard_map/ppermute | solution.py:844
  19.6 2.3 copy-start.15
  70.4 1.0 copy-start.2
  71.4 1.0 copy-start.3
  72.4 0.7 copy-start.4
  73.2 0.9 copy-start.8
  124.4 109.7 %collective-permute-start.2 = (bf16[10,3,56,384]{3,2,1,0:T(8,128)(2,1)}, bf16[10,3,56,384]{3,2,1,0:T(8,128)(2,1)S(1)}, u32[]{:S(2)}, u32[]{:S(2)}) collective-permute-start(bf16[10,3,56,384]{3,2,1,0:T(8,128)(2,1)} %bitcast.52), channel_id=1, source_target_pairs={{0,8},{8,16},{16,24},{24,0},{1,9},{9,17},{17,25},{25,1},{2,10},{10... | collective-permute-start | bytes 3870728 | tf_op jit(solution)/shard_map/ppermute | solution.py:844
  234.2 1.1 copy-start.9
  271.2 1.3 copy-start.25
  271.2 140.9 %reduce-scatter.7.cloned.1.call-start = ((), (), s32[]{:S(2)}) async-start(), calls=%async_computation.3 | async-start | bytes 430080
  272.5 36.3 %collective-permute-start.3 = (bf16[10,3,56,384]{3,2,1,0:T(8,128)(2,1)S(1)}, bf16[10,3,56,384]{3,2,1,0:T(8,128)(2,1)S(1)}, u32[]{:S(2)}, u32[]{:S(2)}) collective-permute-start(bf16[10,3,56,384]{3,2,1,0:T(8,128)(2,1)S(1)} %copy-done.25), channel_id=1, source_target_pairs={{0,24},{8,0},{16,8},{24,16},{1,25},{9,1},{17,9},{25,17},{2,26},{10... | collective-permute-start | bytes 3870728 | tf_op jit(solution)/shard_map/ppermute | solution.py:844
  308.9 1.1 copy-start.26
  309.9 35.0 %copy-start.10 = (f32[56,768]{1,0:T(8,128)S(1)}, f32[56,768]{1,0:T(8,128)}, u32[]{:S(2)}) copy-start(f32[56,768]{1,0:T(8,128)} %get-tuple-element.87) | copy-start | bytes 516100
  343.3 16.7 %copy-start = (f32[384,1152]{1,0:T(8,128)S(1)}, f32[384,1152]{1,0:T(8,128)}, u32[]{:S(2)}) copy-start(f32[384,1152]{1,0:T(8,128)} %get-tuple-element.82) | copy-start | bytes 5308420
  343.3 16.7 %copy-start.1 = (f32[384,1152]{1,0:T(8,128)S(1)}, f32[384,1152]{1,0:T(8,128)}, u32[]{:S(2)}) copy-start(f32[384,1152]{1,0:T(8,128)} %get-tuple-element.81) | copy-start | bytes 5308420
  343.3 50.9 %collective-permute-start.4 = (bf16[10,3,56,384]{3,2,1,0:T(8,128)(2,1)}, bf16[10,3,56,384]{3,2,1,0:T(8,128)(2,1)}, u32[]{:S(2)}, u32[]{:S(2)}) collective-permute-start(bf16[10,3,56,384]{3,2,1,0:T(8,128)(2,1)} %get-tuple-element.79), channel_id=1, source_target_pairs={{0,8},{8,16},{16,24},{24,0},{1,9},{9,17},{17,25},{25,1},{2,10},{10... | collective-permute-start | bytes 3870728 | tf_op jit(solution)/shard_map/ppermute | solution.py:844
  387.9 0.6 copy-start.5
  388.6 0.7 copy-start.7
  394.2 21.0 %copy-start.6 = (f32[48,288]{1,0:T(8,128)S(1)}, f32[48,288]{1,0:T(8,128)}, u32[]{:S(2)}) copy-start(f32[48,288]{1,0:T(8,128)} %copy-done.5) | copy-start | bytes 165892
Sparse Core Ops, SparseCore 0:
  271.3 39.4 reduce-scatter.4
  390.2 21.8 reduce-scatter.6

commit v3 on v2

--- a/solution.py
+++ b/solution.py
@@ -3,6 +3,7 @@
 
 import jax
 import jax.numpy as jnp
+import numpy as np
 from jax import lax
 from jax.experimental import pallas as pl
 from jax.experimental.pallas import tpu as pltpu
@@ -10,13 +11,21 @@
 
 WIN = 7
 SHIFT = 3
+IDENT_ROWS = 1
 SIDE = 8
 SLOTS = WIN * SIDE
 LANES = 64
 PACK = 4
-STEP = 6
+STEP = 8
 RING = 2 * STEP
 NAT = 72
+
+GAIN1, BIAS1, GAIN2, BIAS2, BIAS_PROJ, BIAS_FC2, BIAS_QKV = range(7)
+BIAS_FC1 = BIAS_QKV + 3
+SMALL = 32
+D_GAIN1, D_BIAS1, D_QKV, D_FEED, D_FC1, D_TABLE = 0, 1, 2, 5, 9, 16
+
+VMEM_BYTES = 63 << 20
 
 norm_eps = 1e-05
 masked_score = -1e30
@@ -34,6 +43,10 @@
 
 def tn(left, right):
     return lax.dot_general(left, right, (((0,), (0,)), ((), ())), preferred_element_type=f32)
+
+
+def across(rows, first, count):
+    return jnp.concatenate([rows[n : n + 1] for n in range(first, first + count)], 1)
 
 
 def norm_parts(values):
@@ -93,7 +106,8 @@
         field, rim, *refs = refs
     else:
         field, *refs = refs
-    ident_k, ident_q, gain, bias, weight, wbias, place, mixed, *refs = refs
+    ident, par, weight, place, mixed, *refs = refs
+    gain, bias = par[GAIN1 : GAIN1 + 1], par[BIAS1 : BIAS1 + 1]
     if local < WIN:
         mixed_rim, *refs = refs
     cells, qkv_out, probs_out, nat, wide, raw = refs
@@ -102,18 +116,19 @@
     scale = (channels // heads) ** (-0.5) * math.log2(math.e)
     for r in range(local):
         hat, _ = norm_parts(field[0, r])
-        put_rows(nat, r, hat * gain[...] + bias[...])
+        put_rows(nat, r, hat * gain + bias)
     for r in range(local, WIN):
-        put_rows(nat, r, rim[0, r - local].astype(f32) * gain[...] + bias[...])
+        put_rows(nat, r, rim[0, r - local].astype(f32) * gain + bias)
     x = jnp.concatenate([take_window(nat, w) for w in range(windows)], 0).astype(bf16)
     cells[0, 0] = x
-    wide[...] = nn(x, weight[...]) + wbias[...]
+    wide[...] = nn(x, weight[...]) + across(par, BIAS_QKV, 3)
     mask = head_rows(channels, heads)
     group = PACK * (channels // heads)
     def part(w, base, p):
         return qkv_out[0, 0, w, :, base + p * group : base + (p + 1) * group]
 
     packs = [(w, p) for w in range(windows) for p in range(heads // PACK)]
+    keys = jnp.where(ident[0, 0] < 0, -1, ident[0, 0]).T
 
     def first(i):
         w, p = packs[i]
@@ -126,7 +141,7 @@
     def second(i):
         w, p = packs[i]
         wide_p = slice(p * PACK * LANES, (p + 1) * PACK * LANES)
-        same = ident_k[0, 0, w] == ident_q[0, 0, w : w + 1]
+        same = keys[:SLOTS, w : w + 1] == ident[0, 0, w : w + 1]
         same = jnp.concatenate([same, same], 1)
         scores = raw[i % RING] + place[:, wide_p]
         scores = jnp.where(same, scores, masked_score)
@@ -156,7 +171,7 @@
             mixed_rim[0, 0, r - local] = take_rows(nat, r).astype(bf16)
 
 
-def attend(local, row_of, steps, field, rim, ident_k, ident_q, gain, bias, weight, wbias, place):
+def attend(local, row_of, steps, field, rim, ident, par, weight, place):
     canvases, _, columns, channels = field.shape
     heads = place.shape[1] // LANES
     windows = columns // WIN
@@ -173,9 +188,9 @@
     if local < WIN:
         specs.append(pl.BlockSpec((1,) + rim.shape[1:], lambda n, s: (n, 0, 0, 0)))
         args.append(rim)
-    specs += [block(windows, SLOTS, 2 * LANES), block(windows, 2 * LANES)]
-    specs += [whole(a) for a in (gain, bias, weight, wbias, place)]
-    args += [ident_k, ident_q, gain, bias, weight, wbias, place]
+    specs += [block(windows, 2 * LANES)]
+    specs += [whole(a) for a in (par, weight, place)]
+    args += [ident, par, weight, place]
     lead = (canvases, steps)
     runs = [local, WIN - local] if local < WIN else [WIN]
     tokens = canvases * steps * windows * SLOTS
@@ -200,7 +215,7 @@
             pltpu.VMEM((windows * SLOTS, 3 * channels), f32),
             pltpu.VMEM((RING, SLOTS, PACK * LANES), f32),
         ],
-        compiler_params=pltpu.CompilerParams(vmem_limit_bytes=56 << 20),
+        compiler_params=pltpu.CompilerParams(vmem_limit_bytes=VMEM_BYTES),
         cost_estimate=pl.CostEstimate(
             flops=2 * tokens * channels * (3 * channels + 2 * heads * LANES), bytes_accessed=tokens * 9000, transcendentals=0
         ),
@@ -208,29 +223,21 @@
     )(*args)
 
 
-def tail_probability(size, decay):
-    t = pl.reciprocal(1.0 + (0.3275911 * 0.5**0.5) * size, approx=True)
-    poly = 0.5 * 1.061405429 * t - 0.5 * 1.453152027
-    poly = poly * t + 0.5 * 1.421413741
-    poly = poly * t - 0.5 * 0.284496736
-    poly = poly * t + 0.5 * 0.254829592
-    return poly * t * decay
-
-
 def gelu_parts(act):
-    decay = jnp.exp2(act * act * (-0.5 * math.log2(math.e)))
-    tail = tail_probability(jnp.abs(act), decay)
-    phi = jnp.where(act >= 0.0, 1.0 - tail, tail)
-    return act * phi, phi + act * decay * (1.0 / math.sqrt(2.0 * math.pi))
+    phi = 0.5 + 0.5 * lax.erf(act * 0.5**0.5)
+    density = jnp.exp2(act * act * (-0.5 * math.log2(math.e)) - 0.5 * math.log2(2.0 * math.pi))
+    return act * phi, phi + act * density
 
 
 HIDDEN_STEP = 256
 ROWS_STEP = 16
+LATE = 2
 
 
 def feed_kernel(pieces, together, rows, chain, *refs):
     mixed_in, refs = refs[: len(pieces)], refs[len(pieces) :]
-    field, cot, w_proj, b_proj, gain, bias, w1, b1, w2, b2, *refs = refs
+    field, cot, par, w_proj, w1, w2, *refs = refs
+    gain, bias, b_proj, b2 = (par[n : n + 1] for n in (GAIN2, BIAS2, BIAS_PROJ, BIAS_FC2))
     if chain:
         before, refs = refs[:4], refs[4:]
     out, d_mid, refs = refs[0], refs[1], refs[2:]
@@ -239,9 +246,10 @@
         packed, gs, g1, g2t, gp, *refs = refs
     else:
         g1, g2t, gp, gs, *refs = refs
-    mix, x_hat, inv_s, mid, n2, n2t, d_out, d_outt, mixt, act, dh, hid, dact, acc, branch = refs
+    mix, x_hat, inv_s, mid, n2, n2t, d_out, d_outt, mixt, act, dh, hid, dact, acc, branch, w2t = refs
     columns, channels = field.shape[2], field.shape[3]
     hidden = w1.shape[1]
+    b1 = across(par, BIAS_FC1, hidden // channels)
     tokens = together * rows * columns
     padded = n2.shape[0]
 
@@ -254,6 +262,7 @@
         else:
             for ref in (g1, g2t, gp, gs):
                 ref[...] = jnp.zeros(ref.shape, ref.dtype)
+        w2t[...] = w2[...].T
         n2t[channels:] = jnp.ones((n2t.shape[0] - channels, padded), bf16)
         if padded > tokens:
             for ref in (n2, d_out, mix, branch):
@@ -268,76 +277,80 @@
             for k in range(count):
                 places.append((i, c, k, r, (c * rows + r) * columns))
                 r += 1
-    for a in range(0, len(places), 2):
-        pair = places[a : a + 2]
-        parts = [mixed_in[i][c, k].astype(f32) for i, c, k, _, _ in pair]
-        start = pair[0][4]
-        mix[start : start + len(pair) * columns] = jnp.concatenate(parts, 0).astype(bf16)
+    pairs = [places[a : a + 2] for a in range(0, len(places), 2)]
+    span = lambda pair: slice(pair[0][4], pair[-1][4] + columns)
+    chunks = hidden // HIDDEN_STEP
+    strip_of = lambda j: slice(j * HIDDEN_STEP, (j + 1) * HIDDEN_STEP)
+
+    for pair in pairs:
+        mix[span(pair)] = jnp.concatenate([mixed_in[i][c, k].astype(f32) for i, c, k, _, _ in pair], 0).astype(bf16)
     mid[...] = nn(mix[:tokens], w_proj[...])
-    for i, c, k, r, start in places:
-        rows_here = slice(start, start + columns)
-        middle = mid[rows_here] + (field[c, r] + b_proj[...])
-        mid[rows_here] = middle
-        hat, inv = norm_parts(middle)
-        x_hat[rows_here] = hat
-        inv_s[rows_here] = inv
-    for start in range(0, tokens, 112):
-        some = slice(start, min(start + 112, tokens))
-        n2[some] = (x_hat[some] * gain[...] + bias[...]).astype(bf16)
-    for a in range(0, len(places), 2):
-        pair = places[a : a + 2]
-        start = pair[0][4]
-        d_out[start : start + len(pair) * columns] = jnp.concatenate([cot[c, r] for _, c, _, r, _ in pair], 0).astype(bf16)
-    n2t[:channels] = n2[...].T
+    for pair in pairs:
+        d_out[span(pair)] = jnp.concatenate([cot[c, r] for _, c, _, r, _ in pair], 0).astype(bf16)
+    dh[0] = nt(d_out[:tokens], w2[strip_of(0)])
+    for pair in pairs:
+        for i, c, k, r, start in pair:
+            rows_here = slice(start, start + columns)
+            middle = mid[rows_here] + (field[c, r] + b_proj)
+            mid[rows_here] = middle
+            hat, inv = norm_parts(middle)
+            x_hat[rows_here] = hat
+            inv_s[rows_here] = inv
+        n2[span(pair)] = (x_hat[span(pair)] * gain + bias).astype(bf16)
     d_outt[...] = d_out[...].T
     mixt[...] = mix[...].T
 
-    chunks = hidden // HIDDEN_STEP
-    for j in range(chunks + 2):
+    def weight_step(j):
+        g1[:, strip_of(j)] += nn(n2t[...], dact[:, strip_of(j)])
+        g2t[:, strip_of(j)] += nn(d_outt[...], hid[:, strip_of(j)])
+
+    for j in range(chunks + 1):
         if j < chunks:
-            cols = slice(j * HIDDEN_STEP, (j + 1) * HIDDEN_STEP)
-            act[j % 2] = nn(n2[:tokens], w1[:, cols])
-            dh[j % 2] = nt(d_out[:tokens], w2[cols])
-        if 0 <= j - 1 < chunks:
-            cols = slice((j - 1) * HIDDEN_STEP, j * HIDDEN_STEP)
+            if j:
+                dh[j % 2] = nt(d_out[:tokens], w2[strip_of(j)])
+            act[j % 2] = nn(n2[:tokens], w1[:, strip_of(j)])
+        if j == 0:
+            n2t[:channels] = n2[...].T
+        if j >= 1:
+            cols = strip_of(j - 1)
             for start in range(0, tokens, ROWS_STEP):
                 some = slice(start, min(start + ROWS_STEP, tokens))
                 value, slope = gelu_parts(act[(j - 1) % 2, some] + b1[:, cols])
                 hid[some, cols] = value.astype(bf16)
                 dact[some, cols] = (dh[(j - 1) % 2, some] * slope).astype(bf16)
-        if 0 <= j - 2:
-            cols = slice((j - 2) * HIDDEN_STEP, (j - 1) * HIDDEN_STEP)
-            g1[:, cols] += nn(n2t[...], dact[:, cols])
-            g2t[:, cols] += nn(d_outt[...], hid[:, cols])
-
-    acc[...] = nt(dact[:tokens], w1[...])
-    x_out = nn(hid[:tokens], w2[...])
+        if 0 <= j - 2 < chunks - LATE:
+            weight_step(j - 2)
+
     total = [jnp.zeros((8, channels), f32) for _ in range(4)]
     fold = lambda v: jnp.sum(v.reshape(-1, 8, channels), 0)
+    acc[...] = nt(w1[...], dact[:tokens]).T
+    for j in range(chunks - LATE, chunks):
+        weight_step(j)
+    for pair in pairs:
+        for i, c, k, r, start in pair:
+            rows_here = slice(start, start + columns)
+            hat = x_hat[rows_here]
+            back = acc[rows_here]
+            scaled = back * gain
+            low = jnp.mean(scaled, -1, keepdims=True)
+            slope = jnp.mean(scaled * hat, -1, keepdims=True)
+            d_middle = cot[c, r] + inv_s[rows_here] * (scaled - low - hat * slope)
+            d_mid[c, r] = d_middle
+            total[0] += fold(back * hat)
+            total[1] += fold(back)
+            total[2] += fold(d_middle)
+            total[3] += fold(cot[c, r])
+        branch[span(pair)] = jnp.concatenate([d_mid[c, r] for _, c, _, r, _ in pair], 0).astype(bf16)
+    acc[...] = nt(w2t[...], hid[:tokens]).T
     for i, c, k, r, start in places:
         rows_here = slice(start, start + columns)
-        out[c, r] = mid[rows_here] + x_out[rows_here] + b2[...]
-        hat = x_hat[rows_here]
-        back = acc[rows_here]
-        scaled = back * gain[...]
-        low = jnp.mean(scaled, -1, keepdims=True)
-        slope = jnp.mean(scaled * hat, -1, keepdims=True)
-        d_middle = cot[c, r] + inv_s[rows_here] * (scaled - low - hat * slope)
-        d_mid[c, r] = d_middle
-        mid[rows_here] = d_middle
-        total[0] += fold(back * hat)
-        total[1] += fold(back)
-        total[2] += fold(d_middle)
-        total[3] += fold(cot[c, r])
-    for start in range(0, tokens, 112):
-        some = slice(start, min(start + 112, tokens))
-        branch[some] = mid[some].astype(bf16)
+        out[c, r] = mid[rows_here] + acc[rows_here] + b2
     for n in range(4):
         gs[n : n + 1] += jnp.sum(total[n], 0, keepdims=True)
-    acc[...] = nt(branch[:tokens], w_proj[...])
+    mid[...] = nt(branch[:tokens], w_proj[...])
     gp[...] += nn(mixt[...], branch[...])
     for i, c, k, r, start in places:
-        rest_out[i][c, k] = acc[start : start + columns].astype(bf16)
+        rest_out[i][c, k] = mid[start : start + columns].astype(bf16)
 
     if chain:
 
@@ -359,7 +372,7 @@
                     packed[c, m] = jnp.concatenate(parts, 1).astype(bf16)
 
 
-def feed(mixed_parts, first_row, together, field, cot, prev, w_proj, b_proj, gain, bias, w1, b1, w2, b2):
+def feed(mixed_parts, first_row, together, field, cot, prev, par, w_proj, w1, w2):
     canvases, _, columns, channels = field.shape
     hidden = w1.shape[1]
     pieces = tuple(count for _, count in mixed_parts)
@@ -372,7 +385,7 @@
     )
     part = lambda count: pl.BlockSpec((together, count, columns, channels), lambda n: (n, 0, 0, 0))
     whole = lambda shape: pl.BlockSpec(shape, lambda n: (0,) * len(shape))
-    consts = (w_proj, b_proj, gain, bias, w1, b1, w2, b2)
+    consts = (par, w_proj, w1, w2)
     args = [a for a, _ in mixed_parts] + [field, cot] + list(consts)
     specs = [part(count) for count in pieces] + [big, big] + [whole(a.shape) for a in consts]
     aliases = {}
@@ -417,9 +430,10 @@
             pltpu.VMEM((padded, hidden), bf16),
             pltpu.VMEM((tokens, channels), f32),
             pltpu.VMEM((padded, channels), bf16),
+            pltpu.VMEM((channels, hidden), bf16),
         ],
         input_output_aliases=aliases,
-        compiler_params=pltpu.CompilerParams(vmem_limit_bytes=60 << 20),
+        compiler_params=pltpu.CompilerParams(vmem_limit_bytes=VMEM_BYTES),
         cost_estimate=pl.CostEstimate(
             flops=6 * canvases * rows * columns * channels * (2 * hidden + channels),
             bytes_accessed=canvases * rows * columns * channels * 20,
@@ -429,15 +443,24 @@
     )(*args)
 
 
-def unattend_kernel(local, heads, refs):
+def unattend_kernel(local, heads, chain, final, refs):
     rest, refs = refs[0], refs[1:]
     if local < WIN:
         rim, rim_hat, refs = refs[0], refs[1], refs[2:]
-    cells, qkv, probs, field, d_mid, gain, weight, grad = refs[:8]
-    refs = refs[8:]
+    cells, qkv, probs, field, d_mid, par, weight, *refs = refs
+    gain = par[GAIN1 : GAIN1 + 1]
+    if final:
+        feed_sums, hot, *refs = refs
+    if chain:
+        before, refs = refs[:4], refs[4:]
+    grad, *refs = refs
     if local < WIN:
-        rim_out, refs = refs[0], refs[1:]
-    gw, gb, gt, gs, nat, d_win, raw, ds, wide = refs
+        rim_out, *refs = refs
+    if final:
+        gw, small, gb, gt, gs, *refs = refs
+    else:
+        gw, gb, gt, gs, *refs = refs
+    nat, d_win, raw, ds, wide = refs
     windows = qkv.shape[2]
     channels = field.shape[3]
     scale = (channels // heads) ** (-0.5)
@@ -446,8 +469,12 @@
 
     @pl.when(first_step)
     def _():
-        for ref in (gw, gb, gt, gs):
-            ref[...] = jnp.zeros(ref.shape, ref.dtype)
+        if chain:
+            for ref, old in zip((gw, gb, gt, gs), before):
+                pltpu.sync_copy(old, ref)
+        else:
+            for ref in (gw, gb, gt, gs):
+                ref[...] = jnp.zeros(ref.shape, ref.dtype)
 
     for r in range(WIN):
         source = rest[0, 0, r] if local == WIN else (rest[0, r] if r < local else rim[0, r - local])
@@ -511,7 +538,7 @@
         d_normed = take_rows(nat, r)
         if r < local:
             hat, inv = norm_parts(field[0, r])
-            scaled = d_normed * gain[...]
+            scaled = d_normed * gain
             low = jnp.mean(scaled, -1, keepdims=True)
             slope = jnp.mean(scaled * hat, -1, keepdims=True)
             grad[0, r] = d_mid[0, r] + inv * (scaled - low - hat * slope)
@@ -524,8 +551,34 @@
     for n in range(2):
         gs[n : n + 1] += jnp.sum(total[n], 0, keepdims=True)
 
-
-def unattend(local, row_of, steps, rest, rim, rim_hat, cells, qkv, probs, field, d_mid, prev, gain, weight):
+    if final:
+
+        @pl.when((pl.program_id(0) == pl.num_programs(0) - 1) & (pl.program_id(1) == pl.num_programs(1) - 1))
+        def _():
+            small[...] = jnp.zeros(small.shape, f32)
+            small[D_GAIN1 : D_BIAS1 + 1] = gs[:2]
+            for n in range(3):
+                small[D_QKV + n : D_QKV + n + 1] = gb[:, n * channels : (n + 1) * channels]
+            small[D_FEED : D_FEED + 4] = feed_sums[:4]
+            small[D_FC1 : D_FC1 + 4] = feed_sums[8:12]
+            own = (
+                lax.broadcasted_iota(jnp.int32, (16, heads * LANES), 1) // LANES
+                == lax.broadcasted_iota(jnp.int32, (16, heads * LANES), 0)
+            )
+            table = jnp.zeros((32, hot.shape[2]), f32)
+            for n in range(0, hot.shape[0], WIN):
+                lines = []
+                for k in range(n, n + WIN):
+                    key = k // WIN * SIDE + k % WIN
+                    line = jnp.where(own, gt[key : key + 1], 0.0)
+                    high = line.astype(bf16)
+                    lines.append(jnp.concatenate([high, (line - high.astype(f32)).astype(bf16)], 0))
+                places = jnp.concatenate([hot[k] for k in range(n, n + WIN) for _ in range(heads)], 0)
+                table += nn(jnp.concatenate(lines, 1), places)
+            small[D_TABLE : D_TABLE + 16, : hot.shape[2]] = table[:16] + table[16:]
+
+
+def unattend(local, row_of, steps, rest, rim, rim_hat, cells, qkv, probs, field, d_mid, prev, final, par, weight):
     canvases, _, columns, channels = field.shape
     heads = probs.shape[4] // LANES
     windows = columns // WIN
@@ -541,14 +594,17 @@
         specs = [line(local, columns, channels)] + [line(WIN - local, columns, channels)] * 2
     else:
         args, specs = [rest], [block(WIN, columns, channels)]
-    args += [cells, qkv, probs, field, d_mid, gain, weight]
-    specs += [block(*a.shape[2:]) for a in (cells, qkv, probs)] + [big, big] + [whole(a.shape) for a in (gain, weight)]
+    args += [cells, qkv, probs, field, d_mid, par, weight]
+    specs += [block(*a.shape[2:]) for a in (cells, qkv, probs)] + [big, big] + [whole(a.shape) for a in (par, weight)]
+    if final is not None:
+        args += list(final)
+        specs += [whole(a.shape) for a in final]
     aliases = {}
-    kernel = lambda *refs: unattend_kernel(local, heads, refs)
+    kernel = lambda *refs: unattend_kernel(local, heads, prev is not None, final is not None, refs)
     if prev is not None:
         base = len(args)
-        args.append(prev)
-        specs.append(pl.BlockSpec(memory_space=pl.ANY))
+        args += list(prev)
+        specs += [pl.BlockSpec(memory_space=pl.ANY)] * len(prev)
         aliases = {base: 0}
         inner = kernel
         kernel = lambda *refs: inner(*refs[:base], *refs[base + 1 :])
@@ -557,6 +613,10 @@
         outs.append(jax.ShapeDtypeStruct((canvases, WIN - local, columns, channels), bf16))
         out_specs.append(line(WIN - local, columns, channels))
     grads = [(channels, 3 * channels), (1, 3 * channels), (SLOTS, heads * LANES), (8, channels)]
+    held = []
+    if final is not None:
+        held = [pltpu.VMEM(s, f32) for s in grads[1:]]
+        grads = [grads[0], (SMALL, channels)]
     outs += [jax.ShapeDtypeStruct(s, f32) for s in grads]
     out_specs += [whole(s) for s in grads]
     tokens = canvases * steps * windows * SLOTS
@@ -566,7 +626,8 @@
         in_specs=specs,
         out_specs=out_specs,
         out_shape=outs,
-        scratch_shapes=[
+        scratch_shapes=held
+        + [
             pltpu.VMEM((WIN, NAT, channels), f32),
             pltpu.VMEM((windows, SLOTS, channels), bf16),
             pltpu.VMEM((RING, SLOTS, PACK * LANES), f32),
@@ -574,7 +635,7 @@
             pltpu.VMEM((windows * SLOTS, 3 * channels), f32),
         ],
         input_output_aliases=aliases,
-        compiler_params=pltpu.CompilerParams(vmem_limit_bytes=56 << 20),
+        compiler_params=pltpu.CompilerParams(vmem_limit_bytes=VMEM_BYTES),
         cost_estimate=pl.CostEstimate(
             flops=2 * tokens * channels * (6 * channels + 4 * heads * LANES), bytes_accessed=tokens * 9000, transcendentals=0
         ),
@@ -582,59 +643,127 @@
     )(*args)
 
 
-def rim_kernel(d_normed, field, d_mid, gain, _, grad):
+def finish_kernel(neat, entries, d_normed, field, d_mid, par, small, feed, qkv, _, grad, *outs):
+    gain = par[GAIN1 : GAIN1 + 1]
     for c in range(field.shape[0]):
         for r in range(field.shape[1]):
             hat, inv = norm_parts(field[c, r])
-            scaled = d_normed[c, r].astype(f32) * gain[...]
+            scaled = d_normed[c, r].astype(f32) * gain
             low = jnp.mean(scaled, -1, keepdims=True)
             slope = jnp.mean(scaled * hat, -1, keepdims=True)
             grad[c, r] = d_mid[c, r] + inv * (scaled - low - hat * slope)
-
-
-def rim_grad(d_normed, field, d_mid, gain, prev):
+    if not neat:
+        return
+    gain1, bias1, d_qkv, qkv_bias, table, d_proj, proj_bias, gain2, bias2, d_fc1, fc1_bias, d_fc2, fc2_bias = outs
+
+    @pl.when(pl.program_id(0) == 0)
+    def _():
+        heads = table.shape[1]
+        for ref, n in (
+            (gain1, D_GAIN1),
+            (bias1, D_BIAS1),
+            (gain2, D_FEED),
+            (bias2, D_FEED + 1),
+            (proj_bias, D_FEED + 2),
+            (fc2_bias, D_FEED + 3),
+            (qkv_bias, D_QKV),
+            (fc1_bias, D_FC1),
+        ):
+            width = small.shape[1]
+            for k in range(ref.shape[0] // width):
+                ref[k * width : (k + 1) * width] = small[n + k]
+        table[...] = small[D_TABLE : D_TABLE + 16, :256].T[:entries, :heads]
+        d_qkv[...] = qkv[...]
+        n_proj, n_fc1 = d_proj.shape[1], d_fc1.shape[1]
+        d_proj[...] = feed[:, :n_proj]
+        d_fc1[...] = feed[:, n_proj : n_proj + n_fc1]
+        deep, wide = d_fc2.shape
+        parts = [feed[:, at : at + deep] for at in range(n_proj + n_fc1, feed.shape[1], deep)]
+        turned = jnp.concatenate(parts, 0)
+        turned = jnp.pad(turned, ((0, -wide % 128), (0, -deep % 128))).T
+        d_fc2[...] = turned[:deep, :wide]
+
+
+def finish(d_normed, field, d_mid, par, prev, small, feed, qkv, shapes, entries, sizes):
     canvases, rows, columns, channels = d_normed.shape
-    together = 2
+    neat = qkv.shape[0] % 16 == 0
+    together = 2 if canvases % 2 == 0 else 1
     big = pl.BlockSpec(
         (pl.Element(together), pl.Element(rows), pl.Element(columns), pl.Element(channels)),
         lambda n: (n * together, 0, 0, 0),
     )
-    return pl.pallas_call(
-        rim_kernel,
+    whole = lambda shape: pl.BlockSpec(shape, lambda n: (0,) * len(shape))
+    shapes = shapes if neat else []
+    out = pl.pallas_call(
+        functools.partial(finish_kernel, neat, entries),
         grid=(canvases // together,),
         in_specs=[
             pl.BlockSpec((together, rows, columns, channels), lambda n: (n, 0, 0, 0)),
             big,
             big,
-            pl.BlockSpec(gain.shape, lambda n: (0, 0)),
+            *[whole(a.shape) for a in (par, small, feed, qkv)],
             pl.BlockSpec(memory_space=pl.ANY),
         ],
-        out_specs=big,
-        out_shape=jax.ShapeDtypeStruct(field.shape, f32),
-        input_output_aliases={4: 0},
+        out_specs=[big] + [whole(s) for s in shapes],
+        out_shape=[jax.ShapeDtypeStruct(field.shape, f32)] + [jax.ShapeDtypeStruct(s, f32) for s in shapes],
+        input_output_aliases={7: 0},
+        compiler_params=pltpu.CompilerParams(vmem_limit_bytes=VMEM_BYTES),
         cost_estimate=pl.CostEstimate(flops=d_normed.size * 30, bytes_accessed=d_normed.size * 14, transcendentals=0),
-        name="rim_grad",
-    )(d_normed, field, d_mid, gain, prev)
+        name="finish",
+    )(d_normed, field, d_mid, par, small, feed, qkv, prev)
+    if neat:
+        return out
+    n_proj, n_fc1, deep, heads = sizes
+    d_fc2 = jnp.concatenate([feed[:, at : at + deep] for at in range(n_proj + n_fc1, feed.shape[1], deep)], 0).T
+    return [
+        out[0],
+        small[D_GAIN1],
+        small[D_BIAS1],
+        qkv,
+        small[D_QKV : D_QKV + 3].reshape(-1),
+        small[D_TABLE : D_TABLE + heads, :entries].T,
+        feed[:, :n_proj],
+        small[D_FEED + 2],
+        small[D_FEED],
+        small[D_FEED + 1],
+        feed[:, n_proj : n_proj + n_fc1],
+        small[D_FC1 : D_FC1 + 4].reshape(-1),
+        d_fc2,
+        small[D_FEED + 3],
+    ]
 
 
 MESH = pl.DeviceIdType.MESH
 
 
-def gather_kernel(strips, lines, shard, qkv, proj, fc1, fc2, blocks, send_sem, recv_sem):
+def flip_bits(place, bits):
+    step = 1
+    while step <= bits:
+        if bits & step:
+            place = place + step - 2 * step * ((place // step) % 2)
+        step *= 2
+    return place
+
+
+def gather_kernel(strips, lines, shard, field, crops, *refs):
+    *outs, rim, rim_crops, blocks, crop_rows, crop_got, first_rows, send_sem, recv_sem, crop_sem, field_sem = refs
     strip, line = lax.axis_index("strip"), lax.axis_index("canvas")
     core, chip, chips = line % 2, line // 2, lines // 2
     other = (strip, line + 1 - 2 * core)
-    along = [((strip + n) % strips, line) for n in range(1, strips)]
+    along = [(flip_bits(strip, m), line) for m in range(1, strips)]
     across = [(strip, ((chip + n) % chips) * 2 + core) for n in range(1, chips)]
     partners = along + across + [other]
 
+    fetch = pltpu.make_async_copy(field.at[:, pl.ds(0, SHIFT)], first_rows, field_sem.at[0])
+    fetch.start()
     barrier = pltpu.get_barrier_semaphore()
     for partner in partners:
         pl.semaphore_signal(barrier, inc=1, device_id=partner, device_id_type=MESH)
+    crop_rows[...] = crops[:, :SHIFT]
     pl.semaphore_wait(barrier, len(partners))
 
-    place = lambda n, m: (((chip + n) % chips) * 2 + core, (strip + m) % strips)
-    twin = lambda n, m: (((chip + n) % chips) * 2 + 1 - core, (strip + m) % strips)
+    line_of = lambda n, twin=0: ((chip + n) % chips) * 2 + (1 - core if twin else core)
+    place = lambda n, m, twin=0: (line_of(n, twin), flip_bits(strip, m))
     number = lambda n, m, kind: (kind * chips + n) * strips + m
 
     def copy(source, at, target, index):
@@ -656,47 +785,83 @@
         sent.append(copy(source, at, target, index))
         sent[-1].start()
 
+    relay = strips == 4
+    direct = [1, 2] if relay else list(range(1, strips))
     for n in range(1, chips):
         send(shard, place(0, 0), across[n - 1], number(chips - n, 0, 0))
-    for m in range(1, strips):
-        send(shard, place(0, 0), along[m - 1], number(0, strips - m, 0))
+    for m in direct:
+        send(shard, place(0, 0), along[m - 1], number(0, m, 0))
     send(shard, place(0, 0), other, number(0, 0, 1))
+    crop_copy = pltpu.make_async_remote_copy(
+        src_ref=crop_rows,
+        dst_ref=crop_got,
+        send_sem=crop_sem.at[0],
+        recv_sem=crop_sem.at[1],
+        device_id=((strip + strips - 1) % strips, line),
+        device_id_type=MESH,
+    )
+    crop_copy.start()
     blocks[line, strip] = shard[...]
+
+    def norm_rows(c, carry):
+        for r in range(first_rows.shape[1]):
+            rim[c, r] = norm_parts(first_rows[c, r])[0].astype(bf16)
+        return carry
+
+    fetch.wait()
+    lax.fori_loop(0, first_rows.shape[0], norm_rows, 0)
+
     for n in range(1, chips):
         at = place(n, 0)
         arrived(at, number(n, 0, 0))
-        for m in range(1, strips):
-            send(blocks.at[at[0], at[1]], at, along[m - 1], number(n, strips - m, 0))
+        for m in direct:
+            send(blocks.at[at[0], at[1]], at, along[m - 1], number(n, m, 0))
         send(blocks.at[at[0], at[1]], at, other, number(n, 0, 1))
     for n in range(chips):
-        for m in range(1, strips):
+        for m in direct:
             at = place(n, m)
             arrived(at, number(n, m, 0))
+            if relay and m == 1 + n % 2:
+                send(blocks.at[at[0], at[1]], at, along[2 - m], number(n, 3, 0))
             send(blocks.at[at[0], at[1]], at, other, number(n, m, 1))
-    for n in range(chips):
-        for m in range(strips):
-            arrived(twin(n, m), number(n, m, 1))
-    for c in sent:
-        c.wait_send()
+
     rows = shard.shape[0]
-    if len(qkv.shape) == 2:
+    joined = len(outs) > 1
+
+    def join(c):
+        if not joined:
+            return
+        qkv, proj, fc1, fc2 = outs
         sizes = [ref.shape[1] // strips for ref in (qkv, proj, fc1)]
         edges = [0, sizes[0], sizes[0] + sizes[1], sum(sizes)]
         narrow = fc2.shape[1] // strips
-        for c in range(lines):
-            for ref, low, high in zip((qkv, proj, fc1), edges, edges[1:]):
-                ref[c * rows : (c + 1) * rows] = jnp.concatenate([blocks[c, m, :, low:high] for m in range(strips)], 1)
-            deep = fc2.shape[0] // lines // rows
-            for k in range(deep):
-                low = edges[3] + k * narrow
-                fc2[(c * deep + k) * rows : (c * deep + k + 1) * rows] = jnp.concatenate(
-                    [blocks[c, m, :, low : low + narrow] for m in range(strips)], 1
-                )
-    else:
-        qkv[...] = blocks[...]
-
-
-def gather_weights(qkv, proj, fc1, fc2):
+        whole = lambda low, high: jnp.concatenate([blocks[c, m, :, low:high] for m in range(strips)], 1)
+        for ref, low, high in zip((qkv, proj, fc1), edges, edges[1:]):
+            ref[pl.ds(pl.multiple_of(c * rows, rows), rows)] = whole(low, high)
+        deep = fc2.shape[0] // lines // rows
+        for k in range(deep):
+            low = edges[3] + k * narrow
+            fc2[pl.ds(pl.multiple_of((c * deep + k) * rows, rows), rows)] = whole(low, low + narrow)
+
+    for n in range(chips):
+        if relay:
+            at = place(n, 3)
+            arrived(at, number(n, 3, 0))
+            send(blocks.at[at[0], at[1]], at, other, number(n, 3, 1))
+        join(line_of(n))
+    for n in range(chips):
+        for m in range(strips):
+            arrived(place(n, m, 1), number(n, m, 1))
+        join(line_of(n, 1))
+    crop_copy.wait()
+    rim_crops[...] = crop_got[...]
+    for c in sent:
+        c.wait_send()
+    if not joined:
+        outs[0][...] = blocks[...]
+
+
+def gather_weights(qkv, proj, fc1, fc2, field, crop_ids):
     strips, lines = lax.axis_size("strip"), lax.axis_size("canvas")
     rows = qkv.shape[0]
     deep = fc2.shape[0] // rows
@@ -705,70 +870,73 @@
     joined = rows % 16 == 0
     full = [jax.ShapeDtypeStruct((lines * w.shape[0], strips * w.shape[1]), w.dtype) for w in (qkv, proj, fc1, fc2)]
     blocks = (lines, strips) + shard.shape
-    kernel = functools.partial(gather_kernel, strips, lines)
     if not joined:
         full = [jax.ShapeDtypeStruct(blocks, shard.dtype)]
-        inner = kernel
-        kernel = lambda shard, out, *refs: inner(shard, out, None, None, None, *refs)
+    rim = (field.shape[0], SHIFT) + field.shape[2:]
     vmem = pl.BlockSpec(memory_space=pltpu.VMEM)
     got = pl.pallas_call(
-        kernel,
-        in_specs=[vmem],
-        out_specs=[vmem] * len(full),
-        out_shape=full,
+        functools.partial(gather_kernel, strips, lines),
+        in_specs=[vmem, pl.BlockSpec(memory_space=pl.ANY), vmem],
+        out_specs=[vmem] * (len(full) + 2),
+        out_shape=full + [jax.ShapeDtypeStruct(rim, bf16), jax.ShapeDtypeStruct(rim[:3], jnp.int32)],
         scratch_shapes=[pltpu.VMEM(blocks, shard.dtype)]
-        + [pltpu.SemaphoreType.DMA((lines * strips,))] * 2,
-        compiler_params=pltpu.CompilerParams(collective_id=0, has_side_effects=True, vmem_limit_bytes=40 << 20),
+        + [pltpu.VMEM(rim[:3], jnp.int32)] * 2
+        + [pltpu.VMEM(rim, f32)]
+        + [pltpu.SemaphoreType.DMA((lines * strips,))] * 2
+        + [pltpu.SemaphoreType.DMA((2,)), pltpu.SemaphoreType.DMA((1,))],
+        compiler_params=pltpu.CompilerParams(collective_id=0, has_side_effects=True, vmem_limit_bytes=VMEM_BYTES),
         name="gather_weights",
-    )(shard)
+    )(shard, field, crop_ids)
     if joined:
         return got
-    got, at, out = got[0], 0, []
+    got, rim, crops, at, out = got[0], got[1], got[2], 0, []
     for w in (qkv, proj, fc1):
         part = got[..., at : at + w.shape[1]]
         out.append(part.transpose(0, 2, 1, 3).reshape(lines * rows, -1))
         at += w.shape[1]
     part = got[..., at:].reshape(lines, strips, rows, deep, narrow)
     out.append(part.transpose(0, 3, 2, 1, 4).reshape(lines * rows * deep, -1))
-    return out
-
-
-def reduce_kernel(strips, lines, first, second, small, out, small_out, *refs):
+    return out + [rim, crops]
+
+
+def reduce_kernel(strips, lines, grad, small, feed, out, small_out, feed_out, *refs):
     line_bits, strip_bits = lines.bit_length() - 1, strips.bit_length() - 1
     phases = line_bits + strip_bits
-    acc, *refs = refs
     sends, recvs, kept = refs[:phases], refs[phases : 2 * phases], refs[2 * phases : 3 * phases]
-    small_sends, small_recv, send_sem, recv_sem, small_send_sem, small_recv_sem = refs[3 * phases :]
+    small_sends, small_recv, feed_recv, *sems = refs[3 * phases :]
+    send_sem, recv_sem, small_send_sem, small_recv_sem, feed_send_sem, feed_recv_sem = sems
     strip, line = lax.axis_index("strip"), lax.axis_index("canvas")
     partners, bits = [], []
     for t in range(line_bits):
-        bit = (line // 2**t) % 2
-        bits.append(bit)
-        partners.append((strip, line + (1 - 2 * bit) * 2**t))
+        bits.append((line // 2**t) % 2)
+        partners.append((strip, flip_bits(line, 2**t)))
     for t in reversed(range(strip_bits)):
-        bit = (strip // 2**t) % 2
-        bits.append(bit)
-        partners.append((strip + (1 - 2 * bit) * 2**t, line))
+        bits.append((strip // 2**t) % 2)
+        partners.append((flip_bits(strip, 2**t), line))
+    along = [flip_bits(strip, m) for m in range(1, strips)]
+    greeted = partners[:line_bits] + [(s, line) for s in along]
 
     barrier = pltpu.get_barrier_semaphore()
-    for partner in partners:
+    for partner in greeted:
         pl.semaphore_signal(barrier, inc=1, device_id=partner, device_id_type=MESH)
     small_sends[0] = small[...]
-    acc[...] = first[...] + second[...] if second is not None else first[...]
-    pl.semaphore_wait(barrier, phases)
+    pl.semaphore_wait(barrier, len(greeted))
 
     def copy(source, target, send, recv, partner):
         return pltpu.make_async_remote_copy(
             src_ref=source, dst_ref=target, send_sem=send, recv_sem=recv, device_id=partner, device_id_type=MESH
         )
 
-    current = acc
+    feed_copies = [
+        copy(feed.at[s], feed_recv.at[m], feed_send_sem.at[m], feed_recv_sem.at[m], (s, line))
+        for m, s in enumerate(along)
+    ]
+    current = grad
     for t in range(phases):
         bit = bits[t]
         small_copy = copy(
             small_sends.at[t], small_recv.at[t], small_send_sem.at[t], small_recv_sem.at[t], partners[t]
         )
-        small_copy.start()
         if t < line_bits:
             count = sends[t].shape[0]
             for k in range(count):
@@ -781,6 +949,10 @@
             sends[t][...] = kept[t][1 - bit].astype(bf16)
         big_copy = copy(sends[t], recvs[t], send_sem.at[t], recv_sem.at[t], partners[t])
         big_copy.start()
+        small_copy.start()
+        if t == 0:
+            for c in feed_copies:
+                c.start()
         small_copy.wait()
         summed = small_sends[t] + small_recv[t]
         if t + 1 < phases:
@@ -795,16 +967,20 @@
         else:
             total = kept[t][bit] + recvs[t][...].astype(f32)
             if t + 1 < phases:
-                acc_next = kept[t].at[0]
-                acc_next[...] = total
-                current = acc_next
+                current = kept[t].at[0]
+                current[...] = total
             else:
                 out[...] = total
-
-
-def reduce_weight(first, second, small):
+    total = feed[strip].astype(f32)
+    for m, c in enumerate(feed_copies):
+        c.wait()
+        total += feed_recv[m].astype(f32)
+    feed_out[...] = total
+
+
+def reduce_weight(grad, small, feed):
     strips, lines = lax.axis_size("strip"), lax.axis_size("canvas")
-    rows, columns = first.shape
+    rows, columns = grad.shape
     rows //= lines
     line_bits, strip_bits = lines.bit_length() - 1, strips.bit_length() - 1
     phases = line_bits + strip_bits
@@ -812,30 +988,26 @@
     sends += [(rows, columns >> (t + 1)) for t in range(strip_bits)]
     kept = [(lines >> (t + 1), rows, columns) for t in range(line_bits)]
     kept += [(2, rows, columns >> (t + 1)) for t in range(strip_bits)]
-    blocked = lambda a: a.reshape(lines, rows, columns)
-    args = [blocked(first)] + ([] if second is None else [blocked(second)]) + [small]
-    kernel = functools.partial(reduce_kernel, strips, lines)
-    if second is None:
-        inner = kernel
-        kernel = lambda first, *refs: inner(first, None, *refs)
     vmem = pl.BlockSpec(memory_space=pltpu.VMEM)
     return pl.pallas_call(
-        kernel,
-        in_specs=[vmem] * len(args),
-        out_specs=[vmem] * 2,
+        functools.partial(reduce_kernel, strips, lines),
+        in_specs=[vmem] * 3,
+        out_specs=[vmem] * 3,
         out_shape=[
             jax.ShapeDtypeStruct((rows, columns // strips), f32),
             jax.ShapeDtypeStruct(small.shape, f32),
+            jax.ShapeDtypeStruct(feed.shape[1:], f32),
         ],
-        scratch_shapes=[pltpu.VMEM((lines, rows, columns), f32)]
-        + [pltpu.VMEM(s, bf16) for s in sends]
+        scratch_shapes=[pltpu.VMEM(s, bf16) for s in sends]
         + [pltpu.VMEM(s, bf16) for s in sends]
         + [pltpu.VMEM(s, f32) for s in kept]
         + [pltpu.VMEM((phases,) + small.shape, f32)] * 2
-        + [pltpu.SemaphoreType.DMA((phases,))] * 4,
-        compiler_params=pltpu.CompilerParams(collective_id=1, has_side_effects=True, vmem_limit_bytes=40 << 20),
+        + [pltpu.VMEM((strips - 1,) + feed.shape[1:], bf16)]
+        + [pltpu.SemaphoreType.DMA((phases,))] * 4
+        + [pltpu.SemaphoreType.DMA((strips - 1,))] * 2,
+        compiler_params=pltpu.CompilerParams(collective_id=1, has_side_effects=True, vmem_limit_bytes=VMEM_BYTES),
         name="reduce_weight",
-    )(*args)
+    )(grad.reshape(lines, rows, columns), small, feed)
 
 
 def from_behind(value, axis, steps):
@@ -858,22 +1030,20 @@
 
 
 def table_hot(entries):
-    key = jnp.arange(SLOTS, dtype=jnp.int32)[:, None]
-    query = jnp.arange(LANES, dtype=jnp.int32)[None, :]
+    key = np.arange(SLOTS)[:, None]
+    query = np.arange(LANES)[None, :]
     at = (query // SIDE - key // SIDE + WIN - 1) * (2 * WIN - 1) + query % SIDE - key % SIDE + WIN - 1
     real = (key % SIDE < WIN) & (query % SIDE < WIN) & (query < SLOTS)
-    return (jnp.where(real, at, -1)[..., None] == jnp.arange(entries, dtype=jnp.int32)).astype(f32)
+    return np.where(real, at, -1)[..., None] == np.arange(entries)
 
 
 def window_idents(ident):
     canvases, steps, _, columns = ident.shape
     cells = ident.reshape(canvases, steps, WIN, columns // WIN, WIN).transpose(0, 1, 3, 2, 4)
     lead = cells.shape[:3]
-    none = [(0, 0)] * 4
-    keys = jnp.pad(cells, none + [(0, SIDE - WIN)], constant_values=-1).reshape(lead + (SLOTS,))
-    queries = jnp.pad(cells, none + [(0, SIDE - WIN)], constant_values=-2).reshape(lead + (SLOTS,))
-    queries = jnp.pad(queries, [(0, 0)] * 3 + [(0, LANES - SLOTS)], constant_values=-2)
-    return jnp.broadcast_to(keys[..., None], lead + (SLOTS, 2 * LANES)), jnp.concatenate([queries, queries], -1)
+    slots = jnp.pad(cells, [(0, 0)] * 4 + [(0, SIDE - WIN)], constant_values=-2).reshape(lead + (SLOTS,))
+    slots = jnp.pad(slots, [(0, 0)] * 3 + [(0, LANES - SLOTS)], constant_values=-2)
+    return jnp.concatenate([slots, slots], -1)
 
 
 def body(
@@ -897,13 +1067,10 @@
     canvases, strip_rows, columns, channels = field.shape
     entries, heads = rel_table.shape
     tops = strip_rows // WIN - 1
-    row = lambda v: v.reshape(1, -1)
-
-    w_qkv, w_proj, w_fc1, w_fc2 = gather_weights(qkv_weight, proj_weight, fc1_weight, fc2_weight)
-    first = field[:, :SHIFT]
-    hat, _ = norm_parts(first)
-    rim_hat, rim_crops = from_behind((hat.astype(bf16), crop_ids[:, :SHIFT]), "strip", -1)
-    shifted_crops = jnp.roll(jnp.concatenate([crop_ids[:, SHIFT:], rim_crops], 1), -SHIFT, 2)
+    w_qkv, w_proj, w_fc1, w_fc2, rim_hat, rim_crops = gather_weights(
+        qkv_weight, proj_weight, fc1_weight, fc2_weight, field, crop_ids
+    )
+    rim_hat = from_behind(rim_hat, "strip", -1)
     total_rows = strip_rows * lax.axis_size("strip")
     global_rows = lax.axis_index("strip") * strip_rows + jnp.arange(strip_rows, dtype=jnp.int32)
     col_index = jnp.arange(columns, dtype=jnp.int32)
@@ -914,28 +1081,40 @@
         col_index >= columns - SHIFT
     ).astype(jnp.int32)
     region = row_band[:, None] * 3 + col_band[None, :]
-    ident = (shifted_crops * 9 + region[None]).reshape(canvases, tops + 1, WIN, columns)
+
+    def idents(crops, first):
+        count = crops.shape[1]
+        ident = jnp.roll(crops, -SHIFT, 2) * 9 + region[None, first : first + count]
+        return window_idents(ident.reshape(canvases, count // WIN, WIN, columns))
+
     hot = table_hot(entries)
+    left, parts = rel_table * math.log2(math.e), []
+    for _ in range(3):
+        parts.append(left.astype(bf16))
+        left = left - parts[-1].astype(f32)
     place = jnp.einsum(
-        "kqe,eh->khq", hot, rel_table * math.log2(math.e), precision=lax.Precision.HIGHEST
-    ).reshape(SLOTS, heads * LANES)
-    gain1, bias1, gain2, bias2 = (row(v) for v in (norm1_gain, norm1_bias, norm2_gain, norm2_bias))
-    fixed = (gain1, bias1, w_qkv, row(qkv_bias), place)
+        "kqe,esh->khqs", jnp.asarray(hot, bf16), jnp.stack(parts, 1), preferred_element_type=f32
+    )
+    place = jnp.sum(place, -1).reshape(SLOTS, heads * LANES)
+    small_params = (norm1_gain, norm1_bias, norm2_gain, norm2_bias, proj_bias, fc2_bias, qkv_bias, fc1_bias)
+    par = jnp.concatenate(small_params).reshape(-1, channels)
+    fixed = (par, w_qkv, place)
     top_row = lambda s: SHIFT + WIN * s
     low_row = strip_rows - (WIN - SHIFT)
     low = WIN - SHIFT
 
     if tops:
-        keys_top, queries_top = window_idents(ident[:, :tops])
+        ident_top = idents(crop_ids[:, SHIFT : SHIFT + tops * WIN], 0)
         mixed_top, cells_top, qkv_top, probs_top = attend(
-            WIN, top_row, tops, field, None, keys_top, queries_top, *fixed
+            WIN, top_row, tops, field, None, ident_top, *fixed
         )
-    keys_low, queries_low = window_idents(ident[:, tops:])
+    low_crops = jnp.concatenate([crop_ids[:, SHIFT + tops * WIN :], rim_crops], 1)
+    ident_low = idents(low_crops, tops * WIN)
     mixed_low, mixed_rim, cells_low, qkv_low, probs_low = attend(
-        low, lambda s: low_row, 1, field, rim_hat, keys_low, queries_low, *fixed
+        low, lambda s: low_row, 1, field, rim_hat, ident_low, *fixed
     )
     mixed_rim = from_behind(mixed_rim[:, 0], "strip", 1)
-    feed_fixed = (w_proj, row(proj_bias), gain2, bias2, w_fc1, row(fc1_bias), w_fc2, row(fc2_bias))
+    feed_fixed = (par, w_proj, w_fc1, w_fc2)
     parts = [(mixed_low[:, 0], low)]
     if tops:
         parts = [(mixed_top.reshape(canvases, tops * WIN, columns, channels), tops * WIN)] + parts
@@ -948,16 +1127,16 @@
         [(mixed_rim, SHIFT)], 0, together, field, cotangent, (output, d_mid, *grads_main), *feed_fixed
     )
     rest_rim = from_behind(rest_rim, "strip", -1)
-    shard = lax.psum_scatter(packed, "canvas", scatter_dimension=0)
-    shard = lax.psum_scatter(shard, "strip", scatter_dimension=0).astype(f32)
-    grad, attn = None, []
+    shard = lax.psum_scatter(packed, "canvas", scatter_dimension=0, tiled=False)
+    prev = None
     if tops:
         rest_top = others[0].reshape(canvases, tops, WIN, columns, channels)
-        grad, *grads_top = unattend(
-            WIN, top_row, tops, rest_top, None, None, cells_top, qkv_top, probs_top, field, d_mid, grad, gain1, w_qkv
+        prev = unattend(
+            WIN, top_row, tops, rest_top, None, None, cells_top, qkv_top, probs_top, field, d_mid, None, None, par, w_qkv
         )
-        attn.append(grads_top)
-    grad, rim_back, *grads_low = unattend(
+    real = [key for key in range(SLOTS) if key % SIDE < WIN]
+    hot_keys = jnp.asarray(np.pad(hot[real], ((0, 0), (0, 0), (0, 256 - entries))), bf16)
+    grad, rim_back, g_qkv, small = unattend(
         low,
         lambda s: low_row,
         1,
@@ -969,53 +1148,35 @@
         probs_low,
         field,
         d_mid,
-        grad,
-        gain1,
+        prev,
+        (gs, hot_keys),
+        par,
         w_qkv,
     )
-    attn.append(grads_low)
     rim_back = from_behind(rim_back, "strip", 1)
-    grad = rim_grad(rim_back, field, d_mid, gain1, grad)
-
-    n_proj, n_fc1 = proj_weight.shape[1], fc1_weight.shape[1]
-    d_proj = shard[:, :n_proj]
-    d_fc1 = shard[:, n_proj : n_proj + n_fc1]
-    width = fc2_weight.shape[0]
-    d_fc2 = jnp.concatenate(
-        [shard[:, at : at + width] for at in range(n_proj + n_fc1, shard.shape[1], width)], 0
-    ).T
-
-    gb, gt, g_norm1 = (sum(g[n] for g in attn) for n in (1, 2, 3))
-    d_table = jnp.einsum(
-        "kqe,khq->eh", hot, gt.reshape(SLOTS, heads, LANES), precision=lax.Precision.HIGHEST
-    )
-    g_fc1 = gs[8 : 8 + fc1_bias.shape[0] // channels]
-    pieces = (g_norm1[0], g_norm1[1], gb[0], d_table, gs[2], gs[0], gs[1], g_fc1.reshape(-1), gs[3])
-    packed = jnp.concatenate([v.reshape(-1) for v in pieces])
-    count = -(-packed.size // 1024) * 1024
-    packed = jnp.pad(packed, (0, count - packed.size)).reshape(-1, 128)
-    d_qkv, packed = reduce_weight(grads_low[0], grads_top[0] if tops else None, packed)
-    packed, small, at = packed.reshape(-1), [], 0
-    for v in pieces:
-        small.append(packed[at : at + v.size].reshape(v.shape))
-        at += v.size
-    return (
-        output,
-        grad,
-        small[0],
-        small[1],
-        d_qkv,
-        small[2],
-        small[3],
-        d_proj,
-        small[4],
-        small[5],
-        small[6],
-        d_fc1,
-        small[7],
-        d_fc2,
-        small[8],
-    )
+    d_qkv, small, shard = reduce_weight(g_qkv, small, shard)
+    rim_par, d_qkv = lax.optimization_barrier((par, d_qkv))
+    shapes = [
+        v.shape
+        for v in (
+            norm1_gain,
+            norm1_bias,
+            qkv_weight,
+            qkv_bias,
+            rel_table,
+            proj_weight,
+            proj_bias,
+            norm2_gain,
+            norm2_bias,
+            fc1_weight,
+            fc1_bias,
+            fc2_weight,
+            fc2_bias,
+        )
+    ]
+    sizes = (proj_weight.shape[1], fc1_weight.shape[1], fc2_weight.shape[0], heads)
+    grad, *rest = finish(rim_back, field, d_mid, rim_par, grad, small, shard, d_qkv, shapes, entries, sizes)
+    return (output, grad, *rest)
 
 
 def solution(mesh):

time: 425 us -> 345 us (0.81)
  the two profiles are of different devices: /device:TPU:0 before, /device:TPU:10 now
where the time goes in v3:
time: 345 us; the launch traced here: 339 us
  Pallas kernels  306 us (89%)
  between operations  14.9 us (4%)
  local copies, waits for them, and re-layouts  6.37 us (2%)
  starting transfers between devices  4.5 us (1%)
    pallas_call x2, Pallas kernels, feed(): pl.pallas_call(kernel, grid=(canvases // together,), in_specs=specs, out_...  109 us
    pallas_call x2, Pallas kernels, unattend(): pl.pallas_call(kernel, grid=(canvases, steps), in_specs=specs, out_specs=...  75.3 us
    pallas_call x2, Pallas kernels, attend(): pl.pallas_call(functools.partial(attend_kernel, local, heads), grid=grid,...  42.7 us
    pallas_call x1, Pallas kernels, reduce_weight(): pl.pallas_call(functools.partial(reduce_kernel, strips, lines), in_specs=...  40.1 us
    pallas_call x1, Pallas kernels, gather_weights(): pl.pallas_call(functools.partial(gather_kernel, strips, lines), in_specs=...  31.9 us
    pallas_call x1, Pallas kernels, finish(): pl.pallas_call(functools.partial(finish_kernel, neat, entries), grid=(can...  7.15 us
  transfers between devices with their start and end apart: 5, of which 1 were waited for; matrix products, arithmetic and copies ran while one was open for 2% of the time, Pallas kernels for 63%

profile of v3, /device:TPU:10, one launch (start us, length us, event | category | flops | bytes accessed | tf_op | source)
XLA Modules:
  0.0 338.6 jit_solution(4363988467790071250)
XLA Ops:
  7.2 0.0 reduce-scatter.2.cloned.1.call-start
  7.2 0.8 fusion.12
  8.0 1.5 concatenate.22.shard
  9.5 0.0 copy-start.1
  9.5 0.0 copy-start.5
  9.5 0.0 copy-start.6
  9.5 0.0 copy-start.7
  9.5 0.0 copy-start.8
  9.6 0.0 copy-start.9
  9.6 0.0 copy-start.10
  9.6 0.0 copy-start.3
  9.6 0.0 copy-start.4
  9.6 0.0 copy-start.2
  9.6 31.9 %gather_weights.1 = (bf16[384,1152]{1,0:T(8,128)(2,1)}, bf16[384,384]{1,0:T(8,128)(2,1)}, bf16[384,1536]{1,0:T(8,128)(2,1)}, bf16[1536,384]{1,0:T(8,128)(2,1)}, ...) custom-call(bf16[48,1152]{1,0:T(8,128)(2,1)} %concatenate.22.shard, f32[10,14,56,384]{3,2,1,0:T(8,128)} %field.3, ...), custom_call_target="tpu_custom_call" | custom-call | tf_op jit(solution)/shard_map/gather_weights/pallas_call | solution.py:877
  41.5 0.0 copy-start
  41.5 1.0 collective-permute-start
  42.5 0.0 copy-done.1
  42.5 0.1 slice.46
  42.6 0.7 pad_add_fusion
  43.3 0.8 slice_add_fusion
  44.2 0.1 broadcast_add_fusion
  44.3 0.0 copy-done.5
  44.3 0.0 copy-done.6
  44.3 0.0 copy-done.7
  44.3 0.0 copy-done.8
  44.3 0.0 copy-done.9
  44.4 0.0 copy-done.10
  44.4 0.0 copy-done.3
  44.4 0.0 copy-done.4
  44.4 0.6 reshape.108.refs_3_.refs_2_.refs_4_.refs_6_.refs_8_.par
  45.0 0.1 add.91
  45.1 0.0 copy-done.2
  45.1 0.1 add.88
  45.2 0.1 add_multiply_fusion.1
  45.3 0.1 mul.50
  45.5 0.1 copy.47
  45.6 0.1 reshape.110
  45.7 0.0 copy-done
  45.7 1.0 convolution_reduce_fusion
  46.7 0.8 reshape.109.refs_5_.refs_4_
  47.5 0.1 add_multiply_fusion
  47.6 0.1 mul.44
  47.8 0.1 copy.46
  47.9 0.1 reshape.107
  48.0 0.7 pad_add_fusion.2.refs_1_
  48.7 0.7 pad_add_fusion.1.refs_2_
  49.4 21.4 %attend.3 = (bf16[10,1,7,56,384]{4,3,2,1,0:T(8,128)(2,1)}, bf16[10,1,448,384]{3,2,1,0:T(8,128)(2,1)}, bf16[10,1,8,56,1152]{4,3,2,1,0:T(8,128)(2,1)}, bf16[10,1,8,56,768]{4,3,2,1,0:T(8,128)(2,1)}) custom-call(f32[10,14,56,384]{3,2,1,0:T(8,128)} %field.3, s32[10,1,8,128]{3,2,1,0:T(8,128)} %pad_add_fusion.2.refs_1_, ...), custom_call_target="tpu_custom_call" | custom-call | flops 9248440320 | bytes 40320000 | tf_op jit(solution)/shard_map/attend/pallas_call | solution.py:197
  70.8 2.8 collective-permute-done.refs_1_.refs_2_
  73.6 21.3 %attend.2 = (bf16[10,1,4,56,384]{4,3,2,1,0:T(8,128)(2,1)}, bf16[10,1,3,56,384]{4,3,2,1,0:T(8,128)(2,1)}, bf16[10,1,448,384]{3,2,1,0:T(8,128)(2,1)}, bf16[10,1,8,...) custom-call(f32[10,14,56,384]{3,2,1,0:T(8,128)} %field.3, ...), custom_call_target="tpu_custom_call" | custom-call | flops 9248440320 | bytes 40320000 | tf_op jit(solution)/shard_map/attend/pallas_call | solution.py:197
  94.9 0.4 collective-permute-start.1
  95.3 77.3 %feed.2 = (f32[10,14,56,384]{3,2,1,0:T(8,128)}, f32[10,14,56,384]{3,2,1,0:T(8,128)}, bf16[10,7,56,384]{3,2,1,0:T(8,128)(2,1)}, bf16[10,4,56,384]{3,2,1,0:T(8,128...) custom-call(bf16[10,7,56,384]{3,2,1,0:T(8,128)(2,1)} %bitcast.37, ...), custom_call_target="tpu_custom_call" | custom-call | flops 49049763840 | bytes 47308800 | tf_op jit(solution)/shard_map/feed/pallas_call | solution.py:408
  172.7 0.0 collective-permute-done.1.refs_0_
  172.7 31.3 %feed.3 = (f32[10,14,56,384]{3,2,1,0:T(8,128)}, f32[10,14,56,384]{3,2,1,0:T(8,128)}, bf16[10,3,56,384]{3,2,1,0:T(8,128)(2,1)}, bf16[8,4,48,864]{3,2,1,0:T(8,128)(2,1)}, f32[16,384]{1,0:T(8,128)}) custom-call(bf16[10,3,56,384]{3,2,1,0:T(8,128)(2,1)} %collective-permute-done.1.refs_0_, ...), custom_call_target="tpu_custom_call", output_to_operand_aliasing={{0}: (7, {}), {1}: (8, {})} | custom-call | flops 13377208320 | bytes 12902400 | tf_op jit(solution)/shard_map/feed/pallas_call | solution.py:408
  204.0 0.0 reduce-scatter.2.cloned.1.call-update
  204.0 1.7 collective-permute-start.2
  205.7 33.9 %unattend.2 = (f32[10,14,56,384]{3,2,1,0:T(8,128)}, f32[384,1152]{1,0:T(8,128)}, f32[1,1152]{1,0:T(1,128)}, f32[56,768]{1,0:T(8,128)}, f32[8,384]{1,0:T(8,128)}) custom-call(bf16[10,1,7,56,384]{4,3,2,1,0:T(8,128)(2,1)} %bitcast.36, bf16[10,1,448,384]{3,2,1,0:T(8,128)(2,1)} %get-tuple-element.95.refs_1_, ...), custom_call_target="tpu_custom_call" | custom-call | flops 18496880640 | bytes 40320000 | tf_op jit(solution)/shard_map/unattend/pallas_call | solution.py:623
  239.6 0.0 collective-permute-done.2.refs_1_
  239.6 41.4 %unattend.3 = (f32[10,14,56,384]{3,2,1,0:T(8,128)}, bf16[10,3,56,384]{3,2,1,0:T(8,128)(2,1)}, f32[384,1152]{1,0:T(8,128)}, f32[32,384]{1,0:T(8,128)}) custom-call(bf16[10,4,56,384]{3,2,1,0:T(8,128)(2,1)} %get-tuple-element.87.refs_0_, bf16[10,3,56,384]{3,2,1,0:T(8,128)(2,1)} %collective-permute-done.2.refs_1_, ...), custom_call_target="tpu_custom_call", output_to_operand_aliasing={{0}: (12, {})} | custom-call | flops 18496880640 | bytes 40320000 | tf_op jit(solution)/shard_map/unattend/pallas_call | solution.py:623
  281.0 1.4 collective-permute-start.3
  282.4 0.0 reduce-scatter.2.cloned.1.call-done
  282.4 40.1 %reduce_weight.1 = (f32[48,288]{1,0:T(8,128)}, f32[32,384]{1,0:T(8,128)}, f32[48,864]{1,0:T(8,128)}) custom-call(f32[8,48,1152]{2,1,0:T(8,128)} %bitcast.31, f32[32,384]{1,0:T(8,128)} %get-tuple-element.105.small, bf16[4,48,864]{2,1,0:T(8,128)(2,1)} %bitcast.32), custom_call_target="tpu_custom_call" | custom-call | tf_op jit(solution)/shard_map/reduce_weight/pallas_call | solution.py:992
  322.5 0.0 collective-permute-done.3.d_normed
  322.5 7.2 %finish.1 = (f32[10,14,56,384]{3,2,1,0:T(8,128)}, f32[384]{0:T(512)}, f32[384]{0:T(512)}, f32[48,288]{1,0:T(8,128)}, f32[1152]{0:T(1024)}, /*index=5*/f32[169,12...) custom-call(bf16[10,3,56,384]{3,2,1,0:T(8,128)(2,1)} %collective-per, ...), custom_call_target="tpu_custom_call", output_to_operand_aliasing={{0}: (7, {})} | custom-call | flops 19353600 | bytes 9031680 | tf_op jit(solution)/shard_map/finish/pallas_call | solution.py:697
  329.7 1.6 copy.44
  (21 shorter events, 0.2 us)
Async XLA Ops:
  7.2 275.2 %reduce-scatter.2.cloned.1.call-start = ((), (), s32[]{:S(2)}) async-start(), calls=%async_computation.1 | async-start | bytes 3096576 | tf_op jit(solution)/shard_map/reduce_scatter | solution.py:1130
  9.5 33.0 %copy-start.1 = (s32[10,14,56]{2,1,0:T(8,128)S(1)}, s32[10,14,56]{2,1,0:T(8,128)}, u32[]{:S(2)}) copy-start(s32[10,14,56]{2,1,0:T(8,128)} %crops.1) | copy-start | bytes 94084
  9.5 34.7 %copy-start.5 = (f32[384]{0:T(512)S(1)}, f32[384]{0:T(512)}, u32[]{:S(2)}) copy-start(f32[384]{0:T(512)} %param.20) | copy-start | bytes 4612
  9.5 34.7 %copy-start.6 = (f32[384]{0:T(512)S(1)}, f32[384]{0:T(512)}, u32[]{:S(2)}) copy-start(f32[384]{0:T(512)} %param.21) | copy-start | bytes 4612
  9.5 34.8 %copy-start.7 = (f32[384]{0:T(512)S(1)}, f32[384]{0:T(512)}, u32[]{:S(2)}) copy-start(f32[384]{0:T(512)} %param.27) | copy-start | bytes 4612
  9.5 34.8 %copy-start.8 = (f32[384]{0:T(512)S(1)}, f32[384]{0:T(512)}, u32[]{:S(2)}) copy-start(f32[384]{0:T(512)} %param.28) | copy-start | bytes 4612
  9.6 34.8 %copy-start.9 = (f32[384]{0:T(512)S(1)}, f32[384]{0:T(512)}, u32[]{:S(2)}) copy-start(f32[384]{0:T(512)} %param.26) | copy-start | bytes 4612
  9.6 34.8 %copy-start.10 = (f32[384]{0:T(512)S(1)}, f32[384]{0:T(512)}, u32[]{:S(2)}) copy-start(f32[384]{0:T(512)} %param.32) | copy-start | bytes 4612
  9.6 34.8 %copy-start.3 = (f32[1152]{0:T(1024)S(1)}, f32[1152]{0:T(1024)}, u32[]{:S(2)}) copy-start(f32[1152]{0:T(1024)} %param.23) | copy-start | bytes 13828
  9.6 34.8 %copy-start.4 = (f32[1536]{0:T(1024)S(1)}, f32[1536]{0:T(1024)}, u32[]{:S(2)}) copy-start(f32[1536]{0:T(1024)} %param.30) | copy-start | bytes 18436
  9.6 35.5 %copy-start.2 = (f32[169,12]{0,1:T(8,128)S(1)}, f32[169,12]{0,1:T(8,128)}, u32[]{:S(2)}) copy-start(f32[169,12]{0,1:T(8,128)} %param.24) | copy-start | bytes 24340
  41.5 4.3 %copy-start = (bf16[56,64,169,1]{2,1,0,3:T(8,128)(2,1)S(1)}, bf16[56,64,169,1]{2,1,0,3:T(8,128)(2,1)}, u32[]{:S(2)}) copy-start(bf16[56,64,169,1]{2,1,0,3:T(8,128)(2,1)} %constant.40) | copy-start | bytes 3634180
  41.5 32.1 %collective-permute-start = (bf16[10,3,56,384]{3,2,1,0:T(8,128)(2,1)}, bf16[10,3,56,384]{3,2,1,0:T(8,128)(2,1)}, u32[]{:S(2)}, u32[]{:S(2)}) collective-permute-start(bf16[10,3,56,384]{3,2,1,0:T(8,128)(2,1)} %get-tuple-element.71), channel_id=1, source_target_pairs={{0,24},{8,0},{16,8},{24,16},{1,25},{9,1},{17,9},{25,17},{2,26},{10... | collective-permute-start | bytes 3870728 | tf_op jit(solution)/shard_map/ppermute | solution.py:1016
  94.9 77.8 %collective-permute-start.1 = (bf16[10,3,56,384]{3,2,1,0:T(8,128)(2,1)}, bf16[10,3,56,384]{3,2,1,0:T(8,128)(2,1)}, u32[]{:S(2)}, u32[]{:S(2)}) collective-permute-start(bf16[10,3,56,384]{3,2,1,0:T(8,128)(2,1)} %bitcast.35), channel_id=1, source_target_pairs={{0,8},{8,16},{16,24},{24,0},{1,9},{9,17},{17,25},{25,1},{2,10},{10... | collective-permute-start | bytes 3870728 | tf_op jit(solution)/shard_map/ppermute | solution.py:1016
  204.0 35.6 %collective-permute-start.2 = (bf16[10,3,56,384]{3,2,1,0:T(8,128)(2,1)}, bf16[10,3,56,384]{3,2,1,0:T(8,128)(2,1)}, u32[]{:S(2)}, u32[]{:S(2)}) collective-permute-start(bf16[10,3,56,384]{3,2,1,0:T(8,128)(2,1)} %get-tuple-element.88), channel_id=1, source_target_pairs={{0,24},{8,0},{16,8},{24,16},{1,25},{9,1},{17,9},{25,17},{2,26},{10... | collective-permute-start | bytes 3870728 | tf_op jit(solution)/shard_map/ppermute | solution.py:1016
  281.0 41.5 %collective-permute-start.3 = (bf16[10,3,56,384]{3,2,1,0:T(8,128)(2,1)}, bf16[10,3,56,384]{3,2,1,0:T(8,128)(2,1)}, u32[]{:S(2)}, u32[]{:S(2)}) collective-permute-start(bf16[10,3,56,384]{3,2,1,0:T(8,128)(2,1)} %get-tuple-element.103), channel_id=1, source_target_pairs={{0,8},{8,16},{16,24},{24,0},{1,9},{9,17},{17,25},{25,1},{2,10},{10... | collective-permute-start | bytes 3870728 | tf_op jit(solution)/shard_map/ppermute | solution.py:1016
Sparse Core Ops, SparseCore 0:
  204.2 33.2 reduce-scatter.1

commit v4 on v3

--- a/solution.py
+++ b/solution.py
@@ -22,7 +22,7 @@
 
 GAIN1, BIAS1, GAIN2, BIAS2, BIAS_PROJ, BIAS_FC2, BIAS_QKV = range(7)
 BIAS_FC1 = BIAS_QKV + 3
-SMALL = 32
+SMALL = 24
 D_GAIN1, D_BIAS1, D_QKV, D_FEED, D_FC1, D_TABLE = 0, 1, 2, 5, 9, 16
 
 VMEM_BYTES = 63 << 20
@@ -243,7 +243,12 @@
     out, d_mid, refs = refs[0], refs[1], refs[2:]
     rest_out, refs = refs[: len(pieces)], refs[len(pieces) :]
     if chain:
-        packed, gs, g1, g2t, gp, *refs = refs
+        keep, away, gs, g1, g2t, gp, *refs = refs
+        *refs, old1, old2t, oldp, old_sem = refs
+        fetches = [
+            pltpu.make_async_copy(old, ref, old_sem.at[n])
+            for n, (old, ref) in enumerate(zip(before, (old1, old2t, oldp)))
+        ]
     else:
         g1, g2t, gp, gs, *refs = refs
     mix, x_hat, inv_s, mid, n2, n2t, d_out, d_outt, mixt, act, dh, hid, dact, acc, branch, w2t = refs
@@ -255,13 +260,12 @@
 
     @pl.when(pl.program_id(0) == 0)
     def _():
+        for ref in (g1, g2t, gp, gs):
+            ref[...] = jnp.zeros(ref.shape, ref.dtype)
         if chain:
-            for ref, old in zip((g1, g2t, gp), before):
-                pltpu.sync_copy(old, ref)
             gs[:8] = before[3][...]
-        else:
-            for ref in (g1, g2t, gp, gs):
-                ref[...] = jnp.zeros(ref.shape, ref.dtype)
+            for fetch in fetches:
+                fetch.start()
         w2t[...] = w2[...].T
         n2t[channels:] = jnp.ones((n2t.shape[0] - channels, padded), bf16)
         if padded > tokens:
@@ -356,20 +360,30 @@
 
         @pl.when(pl.program_id(0) == pl.num_programs(0) - 1)
         def _():
-            lines, strips, height, _ = packed.shape
+            for fetch, ref, old in zip(fetches, (g1, g2t, gp), (old1, old2t, oldp)):
+                fetch.wait()
+                ref[...] += old[...]
+            lines, strips, height = 2 * keep.shape[0], keep.shape[1], keep.shape[2]
+            odd = lax.axis_index("canvas") % 2 == 1
             sums = g1[channels : channels + 1]
             for k in range(hidden // channels):
                 gs[8 + k : 9 + k] = sums[:, k * channels : (k + 1) * channels]
             wide, tall = hidden // strips, channels // strips
             deep = hidden // lines
-            for c in range(lines):
+
+            def shard(c, m):
                 own = slice(c * height, (c + 1) * height)
+                parts = [gp[own, m * tall : (m + 1) * tall], g1[own, m * wide : (m + 1) * wide]]
+                for k in range(tall // height):
+                    at = m * tall + k * height
+                    parts.append(g2t[at : at + height, c * deep : (c + 1) * deep])
+                return jnp.concatenate(parts, 1).astype(bf16)
+
+            for c in range(0, lines, 2):
                 for m in range(strips):
-                    parts = [gp[own, m * tall : (m + 1) * tall], g1[own, m * wide : (m + 1) * wide]]
-                    for k in range(tall // height):
-                        at = m * tall + k * height
-                        parts.append(g2t[at : at + height, c * deep : (c + 1) * deep])
-                    packed[c, m] = jnp.concatenate(parts, 1).astype(bf16)
+                    low, high = shard(c, m), shard(c + 1, m)
+                    keep[c // 2, m] = jnp.where(odd, high, low)
+                    away[c // 2, m] = jnp.where(odd, low, high)
 
 
 def feed(mixed_parts, first_row, together, field, cot, prev, par, w_proj, w1, w2):
@@ -399,12 +413,13 @@
         inner = kernel
         kernel = lambda *refs: inner(*refs[:base], *refs[base + 2 :])
         strips, lines = lax.axis_size("strip"), lax.axis_size("canvas")
-        shard = (lines, strips, channels // lines, (channels + 2 * hidden) // strips)
-        sums = [jax.ShapeDtypeStruct(shard, bf16), jax.ShapeDtypeStruct((16, channels), f32)]
+        shard = (lines // 2, strips, channels // lines, (channels + 2 * hidden) // strips)
+        sums = [jax.ShapeDtypeStruct(shard, bf16)] * 2 + [jax.ShapeDtypeStruct((16, channels), f32)]
         held = [pltpu.VMEM(g, f32) for g in grads]
+        olds = held + [pltpu.SemaphoreType.DMA((3,))]
     else:
         sums = [jax.ShapeDtypeStruct(g, f32) for g in grads + [(8, channels)]]
-        held = []
+        held, olds = [], []
     return pl.pallas_call(
         kernel,
         grid=(canvases // together,),
@@ -431,7 +446,8 @@
             pltpu.VMEM((tokens, channels), f32),
             pltpu.VMEM((padded, channels), bf16),
             pltpu.VMEM((channels, hidden), bf16),
-        ],
+        ]
+        + olds,
         input_output_aliases=aliases,
         compiler_params=pltpu.CompilerParams(vmem_limit_bytes=VMEM_BYTES),
         cost_estimate=pl.CostEstimate(
@@ -443,6 +459,39 @@
     )(*args)
 
 
+def table_lines(gt, heads):
+    width = heads * LANES
+    slot = lax.broadcasted_iota(jnp.int32, (1, width), 1) % LANES
+    shift = lambda value, left: pltpu.roll(value, (width - left) % width, 1) if left else value
+
+    def split(value, place, n, unit):
+        ahead = shift(jnp.where(place >= n, value, 0.0), unit * n)
+        return ahead, shift(jnp.where(place < n, value, 0.0), unit * (n - WIN))
+
+    by_rows = [jnp.zeros((SIDE, width), f32)] * 2
+    for n in range(WIN):
+        parts = split(gt[n * SIDE : (n + 1) * SIDE], slot // SIDE, n, SIDE)
+        by_rows = [total + part for total, part in zip(by_rows, parts)]
+    lines = []
+    for total in by_rows:
+        by_cols = [jnp.zeros((1, width), f32)] * 2
+        for n in range(WIN):
+            parts = split(total[n : n + 1], slot % SIDE, n, 1)
+            by_cols = [total_n + part for total_n, part in zip(by_cols, parts)]
+        lines += by_cols
+    return lines
+
+
+def table_places():
+    hot = np.zeros((4, LANES, 256), np.float32)
+    for n in range(4):
+        for slot in range(WIN * SIDE):
+            rows, cols = slot // SIDE - WIN * (n // 2), slot % SIDE - WIN * (n % 2)
+            if abs(rows) < WIN and abs(cols) < WIN:
+                hot[n, slot, (rows + WIN - 1) * (2 * WIN - 1) + cols + WIN - 1] = 1.0
+    return hot.reshape(4 * LANES, 256)
+
+
 def unattend_kernel(local, heads, chain, final, refs):
     rest, refs = refs[0], refs[1:]
     if local < WIN:
@@ -450,7 +499,7 @@
     cells, qkv, probs, field, d_mid, par, weight, *refs = refs
     gain = par[GAIN1 : GAIN1 + 1]
     if final:
-        feed_sums, hot, *refs = refs
+        feed_sums, *refs = refs
     if chain:
         before, refs = refs[:4], refs[4:]
     grad, *refs = refs
@@ -460,7 +509,11 @@
         gw, small, gb, gt, gs, *refs = refs
     else:
         gw, gb, gt, gs, *refs = refs
-    nat, d_win, raw, ds, wide = refs
+    nat, d_win, raw, ds, wide, *refs = refs
+    sums = (gw, gb, gt, gs)
+    if chain:
+        *olds, old_sem = refs
+        fetches = [pltpu.make_async_copy(source, old, old_sem.at[n]) for n, (source, old) in enumerate(zip(before, olds))]
     windows = qkv.shape[2]
     channels = field.shape[3]
     scale = (channels // heads) ** (-0.5)
@@ -469,12 +522,11 @@
 
     @pl.when(first_step)
     def _():
+        for ref in sums:
+            ref[...] = jnp.zeros(ref.shape, ref.dtype)
         if chain:
-            for ref, old in zip((gw, gb, gt, gs), before):
-                pltpu.sync_copy(old, ref)
-        else:
-            for ref in (gw, gb, gt, gs):
-                ref[...] = jnp.zeros(ref.shape, ref.dtype)
+            for fetch in fetches:
+                fetch.start()
 
     for r in range(WIN):
         source = rest[0, 0, r] if local == WIN else (rest[0, r] if r < local else rim[0, r - local])
@@ -551,43 +603,35 @@
     for n in range(2):
         gs[n : n + 1] += jnp.sum(total[n], 0, keepdims=True)
 
-    if final:
-
-        @pl.when((pl.program_id(0) == pl.num_programs(0) - 1) & (pl.program_id(1) == pl.num_programs(1) - 1))
-        def _():
-            small[...] = jnp.zeros(small.shape, f32)
+    @pl.when((pl.program_id(0) == pl.num_programs(0) - 1) & (pl.program_id(1) == pl.num_programs(1) - 1))
+    def _():
+        if chain:
+            for fetch, ref, old in zip(fetches, sums, olds):
+                fetch.wait()
+                ref[...] += old[...]
+        if final:
             small[D_GAIN1 : D_BIAS1 + 1] = gs[:2]
             for n in range(3):
                 small[D_QKV + n : D_QKV + n + 1] = gb[:, n * channels : (n + 1) * channels]
             small[D_FEED : D_FEED + 4] = feed_sums[:4]
             small[D_FC1 : D_FC1 + 4] = feed_sums[8:12]
-            own = (
-                lax.broadcasted_iota(jnp.int32, (16, heads * LANES), 1) // LANES
-                == lax.broadcasted_iota(jnp.int32, (16, heads * LANES), 0)
-            )
-            table = jnp.zeros((32, hot.shape[2]), f32)
-            for n in range(0, hot.shape[0], WIN):
-                lines = []
-                for k in range(n, n + WIN):
-                    key = k // WIN * SIDE + k % WIN
-                    line = jnp.where(own, gt[key : key + 1], 0.0)
-                    high = line.astype(bf16)
-                    lines.append(jnp.concatenate([high, (line - high.astype(f32)).astype(bf16)], 0))
-                places = jnp.concatenate([hot[k] for k in range(n, n + WIN) for _ in range(heads)], 0)
-                table += nn(jnp.concatenate(lines, 1), places)
-            small[D_TABLE : D_TABLE + 16, : hot.shape[2]] = table[:16] + table[16:]
-
-
-def unattend(local, row_of, steps, rest, rim, rim_hat, cells, qkv, probs, field, d_mid, prev, final, par, weight):
+            for n, line in enumerate(table_lines(gt, heads)):
+                for k in range(2):
+                    at = D_TABLE + 2 * n + k
+                    small[at : at + 1] = line[:, k * channels : (k + 1) * channels]
+
+
+def unattend(local, row_of, steps, rest, rim, rim_hat, cells, qkv, probs, field, d_mid, prev, final, par, weight, base=0, span=None):
     canvases, _, columns, channels = field.shape
+    canvases = canvases if span is None else span
     heads = probs.shape[4] // LANES
     windows = columns // WIN
     whole = lambda shape: pl.BlockSpec(shape, lambda n, s: (0,) * len(shape))
-    block = lambda *shape: pl.BlockSpec((1, 1) + shape, lambda n, s: (n, s) + (0,) * len(shape))
-    line = lambda *shape: pl.BlockSpec((1,) + shape, lambda n, s: (n,) + (0,) * len(shape))
+    block = lambda *shape: pl.BlockSpec((1, 1) + shape, lambda n, s: (base + n, s) + (0,) * len(shape))
+    line = lambda *shape, first=base: pl.BlockSpec((1,) + shape, lambda n, s: (first + n,) + (0,) * len(shape))
     big = pl.BlockSpec(
         (pl.Element(1), pl.Element(local), pl.Element(columns), pl.Element(channels)),
-        lambda n, s: (n, row_of(s), 0, 0),
+        lambda n, s: (base + n, row_of(s), 0, 0),
     )
     if local < WIN:
         args = [rest, rim, rim_hat]
@@ -597,23 +641,25 @@
     args += [cells, qkv, probs, field, d_mid, par, weight]
     specs += [block(*a.shape[2:]) for a in (cells, qkv, probs)] + [big, big] + [whole(a.shape) for a in (par, weight)]
     if final is not None:
-        args += list(final)
-        specs += [whole(a.shape) for a in final]
+        args.append(final)
+        specs.append(whole(final.shape))
     aliases = {}
     kernel = lambda *refs: unattend_kernel(local, heads, prev is not None, final is not None, refs)
     if prev is not None:
-        base = len(args)
+        at = len(args)
         args += list(prev)
         specs += [pl.BlockSpec(memory_space=pl.ANY)] * len(prev)
-        aliases = {base: 0}
+        aliases = {at: 0}
         inner = kernel
-        kernel = lambda *refs: inner(*refs[:base], *refs[base + 1 :])
+        kernel = lambda *refs: inner(*refs[:at], *refs[at + 1 :])
     outs, out_specs = [jax.ShapeDtypeStruct(field.shape, f32)], [big]
     if local < WIN:
         outs.append(jax.ShapeDtypeStruct((canvases, WIN - local, columns, channels), bf16))
-        out_specs.append(line(WIN - local, columns, channels))
+        out_specs.append(line(WIN - local, columns, channels, first=0))
     grads = [(channels, 3 * channels), (1, 3 * channels), (SLOTS, heads * LANES), (8, channels)]
-    held = []
+    held, olds = [], []
+    if prev is not None:
+        olds = [pltpu.VMEM(s, f32) for s in grads] + [pltpu.SemaphoreType.DMA((4,))]
     if final is not None:
         held = [pltpu.VMEM(s, f32) for s in grads[1:]]
         grads = [grads[0], (SMALL, channels)]
@@ -633,7 +679,8 @@
             pltpu.VMEM((RING, SLOTS, PACK * LANES), f32),
             pltpu.VMEM((RING, SLOTS, PACK * LANES), bf16),
             pltpu.VMEM((windows * SLOTS, 3 * channels), f32),
-        ],
+        ]
+        + olds,
         input_output_aliases=aliases,
         compiler_params=pltpu.CompilerParams(vmem_limit_bytes=VMEM_BYTES),
         cost_estimate=pl.CostEstimate(
@@ -643,12 +690,13 @@
     )(*args)
 
 
-def finish_kernel(neat, entries, d_normed, field, d_mid, par, small, feed, qkv, _, grad, *outs):
+def finish_kernel(neat, heads, entries, early, d_normed, d_late, field, d_mid, par, small, feed, qkv, hot, _, grad, *outs):
+    is_late = pl.program_id(0) >= early
     gain = par[GAIN1 : GAIN1 + 1]
     for c in range(field.shape[0]):
         for r in range(field.shape[1]):
             hat, inv = norm_parts(field[c, r])
-            scaled = d_normed[c, r].astype(f32) * gain
+            scaled = jnp.where(is_late, d_late[c, r], d_normed[c, r]).astype(f32) * gain
             low = jnp.mean(scaled, -1, keepdims=True)
             slope = jnp.mean(scaled * hat, -1, keepdims=True)
             grad[c, r] = d_mid[c, r] + inv * (scaled - low - hat * slope)
@@ -658,7 +706,6 @@
 
     @pl.when(pl.program_id(0) == 0)
     def _():
-        heads = table.shape[1]
         for ref, n in (
             (gain1, D_GAIN1),
             (bias1, D_BIAS1),
@@ -672,7 +719,16 @@
             width = small.shape[1]
             for k in range(ref.shape[0] // width):
                 ref[k * width : (k + 1) * width] = small[n + k]
-        table[...] = small[D_TABLE : D_TABLE + 16, :256].T[:entries, :heads]
+        rows = []
+        for h in range(heads):
+            at, low = divmod(h * LANES, small.shape[1])
+            rows.append(jnp.concatenate([small[D_TABLE + 2 * n + at : D_TABLE + 2 * n + at + 1, low : low + LANES] for n in range(4)], 1))
+        left, got = jnp.concatenate(rows + [jnp.zeros((16 - heads, 4 * LANES), f32)], 0), jnp.zeros((16, 256), f32)
+        for _ in range(3):
+            high = left.astype(bf16)
+            got += nn(high, hot[...])
+            left = left - high.astype(f32)
+        table[...] = got[:heads, :entries]
         d_qkv[...] = qkv[...]
         n_proj, n_fc1 = d_proj.shape[1], d_fc1.shape[1]
         d_proj[...] = feed[:, :n_proj]
@@ -684,10 +740,13 @@
         d_fc2[...] = turned[:deep, :wide]
 
 
-def finish(d_normed, field, d_mid, par, prev, small, feed, qkv, shapes, entries, sizes):
-    canvases, rows, columns, channels = d_normed.shape
+def finish(d_normed, d_late, field, d_mid, par, prev, small, feed, qkv, shapes, entries, sizes):
+    canvases, rows, columns, channels = field.shape[:1] + d_normed.shape[1:]
     neat = qkv.shape[0] % 16 == 0
-    together = 2 if canvases % 2 == 0 else 1
+    together = math.gcd(d_normed.shape[0], d_late.shape[0])
+    early = d_normed.shape[0] // together
+    hot = table_places()
+    heads = sizes[3]
     big = pl.BlockSpec(
         (pl.Element(together), pl.Element(rows), pl.Element(columns), pl.Element(channels)),
         lambda n: (n * together, 0, 0, 0),
@@ -695,25 +754,30 @@
     whole = lambda shape: pl.BlockSpec(shape, lambda n: (0,) * len(shape))
     shapes = shapes if neat else []
     out = pl.pallas_call(
-        functools.partial(finish_kernel, neat, entries),
+        functools.partial(finish_kernel, neat, heads, entries, early),
         grid=(canvases // together,),
         in_specs=[
-            pl.BlockSpec((together, rows, columns, channels), lambda n: (n, 0, 0, 0)),
+            pl.BlockSpec((together, rows, columns, channels), lambda n: (jnp.minimum(n, early - 1), 0, 0, 0)),
+            pl.BlockSpec((together, rows, columns, channels), lambda n: (jnp.maximum(n - early, 0), 0, 0, 0)),
             big,
             big,
-            *[whole(a.shape) for a in (par, small, feed, qkv)],
+            *[whole(a.shape) for a in (par, small, feed, qkv, hot)],
             pl.BlockSpec(memory_space=pl.ANY),
         ],
         out_specs=[big] + [whole(s) for s in shapes],
         out_shape=[jax.ShapeDtypeStruct(field.shape, f32)] + [jax.ShapeDtypeStruct(s, f32) for s in shapes],
-        input_output_aliases={7: 0},
+        input_output_aliases={9: 0},
         compiler_params=pltpu.CompilerParams(vmem_limit_bytes=VMEM_BYTES),
         cost_estimate=pl.CostEstimate(flops=d_normed.size * 30, bytes_accessed=d_normed.size * 14, transcendentals=0),
         name="finish",
-    )(d_normed, field, d_mid, par, small, feed, qkv, prev)
+    )(d_normed, d_late, field, d_mid, par, small, feed, qkv, jnp.asarray(hot, bf16), prev)
     if neat:
+        out = list(out)
+        out[5] = out[5].T
         return out
-    n_proj, n_fc1, deep, heads = sizes
+    n_proj, n_fc1, deep, _ = sizes
+    lines = small[D_TABLE : D_TABLE + 8].reshape(4, heads, LANES).transpose(1, 0, 2).reshape(heads, -1)
+    table = jnp.dot(lines, hot, precision=lax.Precision.HIGHEST)[:, :entries].T
     d_fc2 = jnp.concatenate([feed[:, at : at + deep] for at in range(n_proj + n_fc1, feed.shape[1], deep)], 0).T
     return [
         out[0],
@@ -721,7 +785,7 @@
         small[D_BIAS1],
         qkv,
         small[D_QKV : D_QKV + 3].reshape(-1),
-        small[D_TABLE : D_TABLE + heads, :entries].T,
+        table,
         feed[:, :n_proj],
         small[D_FEED + 2],
         small[D_FEED],
@@ -899,27 +963,30 @@
     return out + [rim, crops]
 
 
-def reduce_kernel(strips, lines, grad, small, feed, out, small_out, feed_out, *refs):
-    line_bits, strip_bits = lines.bit_length() - 1, strips.bit_length() - 1
-    phases = line_bits + strip_bits
-    sends, recvs, kept = refs[:phases], refs[phases : 2 * phases], refs[2 * phases : 3 * phases]
-    small_sends, small_recv, feed_recv, *sems = refs[3 * phases :]
-    send_sem, recv_sem, small_send_sem, small_recv_sem, feed_send_sem, feed_recv_sem = sems
+def reduce_kernel(strips, lines, grad, small, feed_keep, feed_got, out, small_out, feed_out, *refs):
+    phases = lines.bit_length() - 1
+    late_bits = phases - 2
+    take = lambda count, refs: (refs[:count], refs[count:])
+    sends, refs = take(phases, refs)
+    recvs, refs = take(phases, refs)
+    kept, refs = take(phases, refs)
+    halves, refs = take(late_bits + 1, refs)
+    halves_got, refs = take(late_bits, refs)
+    small_sends, small_recv, small_all, blocks, blocks_out, blocks_got, feed_got_strips, *sems = refs
+    send_sem, recv_sem, small_send_sem, small_recv_sem, half_sem, half_got_sem, strip_sem, strip_got_sem = sems
     strip, line = lax.axis_index("strip"), lax.axis_index("canvas")
-    partners, bits = [], []
-    for t in range(line_bits):
-        bits.append((line // 2**t) % 2)
-        partners.append((strip, flip_bits(line, 2**t)))
-    for t in reversed(range(strip_bits)):
-        bits.append((strip // 2**t) % 2)
-        partners.append((flip_bits(strip, 2**t), line))
+    bits = [(line // 2**t) % 2 for t in range(phases)]
+    partners = [(strip, flip_bits(line, 2**t)) for t in range(phases)]
     along = [flip_bits(strip, m) for m in range(1, strips)]
-    greeted = partners[:line_bits] + [(s, line) for s in along]
+    greeted = partners + [(s, line) for s in along]
 
     barrier = pltpu.get_barrier_semaphore()
     for partner in greeted:
         pl.semaphore_signal(barrier, inc=1, device_id=partner, device_id_type=MESH)
     small_sends[0] = small[...]
+    for n in range(feed_keep.shape[0]):
+        for s in range(strips):
+            halves[0][n, s] = (feed_keep[n, s].astype(f32) + feed_got[n, s].astype(f32)).astype(bf16)
     pl.semaphore_wait(barrier, len(greeted))
 
     def copy(source, target, send, recv, partner):
@@ -927,87 +994,123 @@
             src_ref=source, dst_ref=target, send_sem=send, recv_sem=recv, device_id=partner, device_id_type=MESH
         )
 
-    feed_copies = [
-        copy(feed.at[s], feed_recv.at[m], feed_send_sem.at[m], feed_recv_sem.at[m], (s, line))
-        for m, s in enumerate(along)
-    ]
+    def half_copy(k):
+        bit = bits[k + 1]
+        return [
+            copy(
+                halves[k].at[2 * n + 1 - bit],
+                halves_got[k].at[n],
+                half_sem.at[k, n],
+                half_got_sem.at[k, n],
+                partners[k + 1],
+            )
+            for n in range(halves[k].shape[0] // 2)
+        ]
+
+    def along_strip(kind, source, target):
+        return [
+            copy(source(s), target(m), strip_sem.at[kind, m], strip_got_sem.at[kind, m], (s, line))
+            for m, s in enumerate(along)
+        ]
+
+    def feed_copies():
+        return along_strip(0, lambda s: halves[-1].at[0, s], lambda m: feed_got_strips.at[m])
+
+    def start_feed(k):
+        for c in half_copy(k) if k < late_bits else feed_copies():
+            c.start()
+
+    def end_feed(k):
+        for n, c in enumerate(half_copy(k)):
+            c.wait()
+            for s in range(strips):
+                total = halves[k][2 * n + bits[k + 1], s].astype(f32) + halves_got[k][n, s].astype(f32)
+                halves[k + 1][n, s] = total.astype(bf16)
+
     current = grad
     for t in range(phases):
         bit = bits[t]
         small_copy = copy(
             small_sends.at[t], small_recv.at[t], small_send_sem.at[t], small_recv_sem.at[t], partners[t]
         )
-        if t < line_bits:
-            count = sends[t].shape[0]
-            for k in range(count):
-                sends[t][k] = current[2 * k + 1 - bit].astype(bf16)
-        else:
-            width = current.shape[-1] // 2
-            block = current[0] if t == line_bits else current[...]
-            for k in range(2):
-                kept[t][k] = block[:, k * width : (k + 1) * width]
-            sends[t][...] = kept[t][1 - bit].astype(bf16)
+        count = sends[t].shape[0]
+        for k in range(count):
+            sends[t][k] = current[2 * k + 1 - bit].astype(bf16)
         big_copy = copy(sends[t], recvs[t], send_sem.at[t], recv_sem.at[t], partners[t])
         big_copy.start()
         small_copy.start()
         if t == 0:
-            for c in feed_copies:
-                c.start()
+            start_feed(0)
         small_copy.wait()
         summed = small_sends[t] + small_recv[t]
         if t + 1 < phases:
             small_sends[t + 1] = summed
         else:
-            small_out[...] = summed
+            small_all[strip] = summed
         big_copy.wait()
-        if t < line_bits:
-            for k in range(count):
-                kept[t][k] = current[2 * k + bit] + recvs[t][k].astype(f32)
-            current = kept[t]
-        else:
-            total = kept[t][bit] + recvs[t][...].astype(f32)
-            if t + 1 < phases:
-                current = kept[t].at[0]
-                current[...] = total
-            else:
-                out[...] = total
-    total = feed[strip].astype(f32)
-    for m, c in enumerate(feed_copies):
+        for k in range(count):
+            kept[t][k] = current[2 * k + bit] + recvs[t][k].astype(f32)
+        current = kept[t]
+        if 0 <= t - 1 < late_bits:
+            end_feed(t - 1)
+            start_feed(t)
+    width = blocks.shape[2]
+    for s in range(strips):
+        blocks[s] = current[0, :, s * width : (s + 1) * width]
+        blocks_out[s] = blocks[s].astype(bf16)
+    small_copies = along_strip(1, lambda s: small_all.at[strip], lambda m: small_all.at[strip])
+    big_copies = along_strip(2, lambda s: blocks_out.at[s], lambda m: blocks_got.at[m])
+    for c in big_copies + small_copies:
+        c.start()
+    total = halves[-1][0, strip].astype(f32)
+    for m, c in enumerate(feed_copies()):
         c.wait()
-        total += feed_recv[m].astype(f32)
+        total += feed_got_strips[m].astype(f32)
     feed_out[...] = total
-
-
-def reduce_weight(grad, small, feed):
+    total = blocks[strip]
+    for m, c in enumerate(big_copies):
+        c.wait()
+        total += blocks_got[m].astype(f32)
+    out[...] = total
+    for c in small_copies:
+        c.wait()
+    total = small_all[0]
+    for s in range(1, strips):
+        total += small_all[s]
+    small_out[...] = total
+
+
+def reduce_weight(grad, small, feed, feed_got):
     strips, lines = lax.axis_size("strip"), lax.axis_size("canvas")
     rows, columns = grad.shape
     rows //= lines
-    line_bits, strip_bits = lines.bit_length() - 1, strips.bit_length() - 1
-    phases = line_bits + strip_bits
-    sends = [(lines >> (t + 1), rows, columns) for t in range(line_bits)]
-    sends += [(rows, columns >> (t + 1)) for t in range(strip_bits)]
-    kept = [(lines >> (t + 1), rows, columns) for t in range(line_bits)]
-    kept += [(2, rows, columns >> (t + 1)) for t in range(strip_bits)]
+    phases = lines.bit_length() - 1
+    late_bits = phases - 2
+    parts = [(lines >> (t + 1), rows, columns) for t in range(phases)]
+    block = (rows, columns // strips)
     vmem = pl.BlockSpec(memory_space=pltpu.VMEM)
+    scratch = [pltpu.VMEM(s, bf16) for s in parts + parts] + [pltpu.VMEM(s, f32) for s in parts]
+    scratch += [pltpu.VMEM((feed.shape[0] >> k,) + feed.shape[1:], bf16) for k in range(late_bits + 1)]
+    scratch += [pltpu.VMEM((feed.shape[0] >> (k + 1),) + feed.shape[1:], bf16) for k in range(late_bits)]
+    scratch += [pltpu.VMEM((phases,) + small.shape, f32)] * 2 + [pltpu.VMEM((strips,) + small.shape, f32)]
+    scratch += [pltpu.VMEM((strips,) + block, kind) for kind in (f32, bf16)]
+    scratch += [pltpu.VMEM((strips - 1,) + block, bf16), pltpu.VMEM((strips - 1,) + feed.shape[2:], bf16)]
+    scratch += [pltpu.SemaphoreType.DMA((phases,))] * 4
+    scratch += [pltpu.SemaphoreType.DMA((late_bits, feed.shape[0] // 2))] * 2
+    scratch += [pltpu.SemaphoreType.DMA((3, strips - 1))] * 2
     return pl.pallas_call(
         functools.partial(reduce_kernel, strips, lines),
-        in_specs=[vmem] * 3,
+        in_specs=[vmem] * 4,
         out_specs=[vmem] * 3,
         out_shape=[
-            jax.ShapeDtypeStruct((rows, columns // strips), f32),
+            jax.ShapeDtypeStruct(block, f32),
             jax.ShapeDtypeStruct(small.shape, f32),
-            jax.ShapeDtypeStruct(feed.shape[1:], f32),
+            jax.ShapeDtypeStruct(feed.shape[2:], f32),
         ],
-        scratch_shapes=[pltpu.VMEM(s, bf16) for s in sends]
-        + [pltpu.VMEM(s, bf16) for s in sends]
-        + [pltpu.VMEM(s, f32) for s in kept]
-        + [pltpu.VMEM((phases,) + small.shape, f32)] * 2
-        + [pltpu.VMEM((strips - 1,) + feed.shape[1:], bf16)]
-        + [pltpu.SemaphoreType.DMA((phases,))] * 4
-        + [pltpu.SemaphoreType.DMA((strips - 1,))] * 2,
+        scratch_shapes=scratch,
         compiler_params=pltpu.CompilerParams(collective_id=1, has_side_effects=True, vmem_limit_bytes=VMEM_BYTES),
         name="reduce_weight",
-    )(grad.reshape(lines, rows, columns), small, feed)
+    )(grad.reshape(lines, rows, columns), small, feed, feed_got)
 
 
 def from_behind(value, axis, steps):
@@ -1123,38 +1226,61 @@
     rest_low = others[len(parts) - 1]
     grads_main = others[len(parts) :]
     together = max(n for n in (1, 2, 5) if canvases % n == 0)
-    output, d_mid, rest_rim, packed, gs = feed(
+    output, d_mid, rest_rim, keep, away, gs = feed(
         [(mixed_rim, SHIFT)], 0, together, field, cotangent, (output, d_mid, *grads_main), *feed_fixed
     )
     rest_rim = from_behind(rest_rim, "strip", -1)
-    shard = lax.psum_scatter(packed, "canvas", scatter_dimension=0, tiled=False)
+    line, lines = lax.axis_index("canvas"), lax.axis_size("canvas")
+
+    def swap(value, bit):
+        return lax.ppermute(value, "canvas", [(n, n ^ (1 << bit)) for n in range(lines)])
+
+    def halve(keep, got, bit):
+        total = (keep.astype(f32) + got.astype(f32)).astype(bf16)
+        total = total.reshape((2, -1) + total.shape[1:])
+        mine = (line >> bit) % 2
+        pick = lambda n: lax.dynamic_index_in_dim(total, n, 0, keepdims=False)
+        return pick(mine), pick(1 - mine)
+
+    got = swap(away, 0)
     prev = None
     if tops:
         rest_top = others[0].reshape(canvases, tops, WIN, columns, channels)
         prev = unattend(
             WIN, top_row, tops, rest_top, None, None, cells_top, qkv_top, probs_top, field, d_mid, None, None, par, w_qkv
         )
-    real = [key for key in range(SLOTS) if key % SIDE < WIN]
-    hot_keys = jnp.asarray(np.pad(hot[real], ((0, 0), (0, 0), (0, 256 - entries))), bf16)
-    grad, rim_back, g_qkv, small = unattend(
-        low,
-        lambda s: low_row,
-        1,
-        rest_low,
-        rest_rim,
-        rim_hat,
-        cells_low,
-        qkv_low,
-        probs_low,
-        field,
-        d_mid,
-        prev,
-        (gs, hot_keys),
-        par,
-        w_qkv,
-    )
-    rim_back = from_behind(rim_back, "strip", 1)
-    d_qkv, small, shard = reduce_weight(g_qkv, small, shard)
+
+    def low_part(prev, final, par, base, span):
+        return unattend(
+            low,
+            lambda s: low_row,
+            1,
+            rest_low,
+            rest_rim,
+            rim_hat,
+            cells_low,
+            qkv_low,
+            probs_low,
+            field,
+            d_mid,
+            prev,
+            final,
+            par,
+            w_qkv,
+            base,
+            span,
+        )
+
+    cut = canvases * 3 // 5
+    top_bit = lines.bit_length() - 2
+    keep, away = halve(keep, got, top_bit)
+    here, away = lax.optimization_barrier((par, away))
+    got = swap(away, top_bit)
+    grad, rim_early, *sums = low_part(prev, None, here, 0, cut)
+    rim_early = from_behind(rim_early, "strip", 1)
+    grad, rim_late, g_qkv, small = low_part((grad, *sums), gs, par, cut, canvases - cut)
+    rim_late = from_behind(rim_late, "strip", 1)
+    d_qkv, small, shard = reduce_weight(g_qkv, small, keep, got)
     rim_par, d_qkv = lax.optimization_barrier((par, d_qkv))
     shapes = [
         v.shape
@@ -1163,7 +1289,7 @@
             norm1_bias,
             qkv_weight,
             qkv_bias,
-            rel_table,
+            rel_table.T,
             proj_weight,
             proj_bias,
             norm2_gain,
@@ -1175,7 +1301,7 @@
         )
     ]
     sizes = (proj_weight.shape[1], fc1_weight.shape[1], fc2_weight.shape[0], heads)
-    grad, *rest = finish(rim_back, field, d_mid, rim_par, grad, small, shard, d_qkv, shapes, entries, sizes)
+    grad, *rest = finish(rim_early, rim_late, field, d_mid, rim_par, grad, small, shard, d_qkv, shapes, entries, sizes)
     return (output, grad, *rest)
 
 

time: 345 us -> 323 us (0.936)
  the two profiles are of different devices: /device:TPU:10 before, /device:TPU:0 now
where the time goes in v4:
time: 323 us; the launch traced here: 317 us
  Pallas kernels  292 us (90%)
  starting transfers between devices  9.14 us (3%)
  local copies, waits for them, and re-layouts  6.9 us (2%)
  other arithmetic  5.35 us (2%)
    pallas_call x2, Pallas kernels, feed(): pl.pallas_call(kernel, grid=(canvases // together,), in_specs=specs, out_...  105 us
    pallas_call x3, Pallas kernels, unattend(): pl.pallas_call(kernel, grid=(canvases, steps), in_specs=specs, out_specs=...  72.6 us
    pallas_call x2, Pallas kernels, attend(): pl.pallas_call(functools.partial(attend_kernel, local, heads), grid=grid,...  42.7 us
    pallas_call x1, Pallas kernels, reduce_weight(): pl.pallas_call(functools.partial(reduce_kernel, strips, lines), in_specs=...  32.8 us
    pallas_call x1, Pallas kernels, gather_weights(): pl.pallas_call(functools.partial(gather_kernel, strips, lines), in_specs=...  31.4 us
    pallas_call x1, Pallas kernels, finish(): pl.pallas_call(functools.partial(finish_kernel, neat, heads, entries, ear...  7.3 us
    ppermute x5, starting transfers between devices, from_behind(): return lax.ppermute(value, axis, pairs)  6.68 us
  transfers between devices with their start and end apart: 7, of which 1 were waited for; matrix products, arithmetic and copies ran while one was open for 3% of the time, Pallas kernels for 64%

profile of v4, /device:TPU:0, one launch (start us, length us, event | category | flops | bytes accessed | tf_op | source)
XLA Modules:
  0.0 316.9 jit_solution(9777382992042450438)
XLA Ops:
  0.6 0.8 fusion.12
  1.4 1.5 concatenate.22.shard
  3.0 31.4 %gather_weights.1 = (bf16[384,1152]{1,0:T(8,128)(2,1)}, bf16[384,384]{1,0:T(8,128)(2,1)}, bf16[384,1536]{1,0:T(8,128)(2,1)}, bf16[1536,384]{1,0:T(8,128)(2,1)}, ...) custom-call(bf16[48,1152]{1,0:T(8,128)(2,1)} %concatenate.22.shard, f32[10,14,56,384]{3,2,1,0:T(8,128)} %field.3, ...), custom_call_target="tpu_custom_call" | custom-call | tf_op jit(solution)/shard_map/gather_weights/pallas_call | solution.py:941
  34.4 0.0 copy-start.3
  34.4 0.0 copy-start
  34.4 1.5 collective-permute-start
  35.9 0.0 copy-done.2
  35.9 0.7 pad_add_fusion
  36.6 0.8 slice_add_fusion
  37.5 0.1 slice.46
  37.6 0.1 add_multiply_fusion
  37.7 0.1 mul.44
  37.8 0.1 broadcast_add_fusion
  37.9 0.1 add.101
  38.0 0.1 copy.45
  38.1 0.0 copy-start.6
  38.2 0.0 copy-start.7
  38.2 0.0 copy-start.8
  38.2 0.0 copy-start.9
  38.2 0.0 copy-start.10
  38.2 0.0 copy-start.11
  38.2 0.0 copy-start.4
  38.2 0.0 copy-start.5
  38.2 0.1 reshape.110
  38.4 0.0 copy-done.3
  38.4 1.0 convolution_reduce_fusion
  39.4 0.8 reshape.112.refs_5_.refs_4_
  40.3 0.0 copy-done.9
  40.3 0.0 copy-done.11
  40.3 0.0 copy-done.4
  40.4 0.6 reshape.111.refs_3_.refs_2_.refs_4_.refs_6_.refs_8_.par
  41.0 0.1 add.104
  41.1 0.1 add_multiply_fusion.1
  41.1 0.1 mul.50
  41.3 0.1 copy.46
  41.4 0.1 reshape.113
  41.6 0.7 pad_add_fusion.1.refs_2_
  42.3 0.7 pad_add_fusion.2.refs_1_
  43.0 21.4 %attend.3 = (bf16[10,1,7,56,384]{4,3,2,1,0:T(8,128)(2,1)}, bf16[10,1,448,384]{3,2,1,0:T(8,128)(2,1)}, bf16[10,1,8,56,1152]{4,3,2,1,0:T(8,128)(2,1)}, bf16[10,1,8,56,768]{4,3,2,1,0:T(8,128)(2,1)}) custom-call(f32[10,14,56,384]{3,2,1,0:T(8,128)} %field.3, s32[10,1,8,128]{3,2,1,0:T(8,128)} %pad_add_fusion.2.refs_1_, ...), custom_call_target="tpu_custom_call" | custom-call | flops 9248440320 | bytes 40320000 | tf_op jit(solution)/shard_map/attend/pallas_call | solution.py:197
  64.4 1.2 collective-permute-done.refs_1_.refs_2_
  65.6 21.3 %attend.2 = (bf16[10,1,4,56,384]{4,3,2,1,0:T(8,128)(2,1)}, bf16[10,1,3,56,384]{4,3,2,1,0:T(8,128)(2,1)}, bf16[10,1,448,384]{3,2,1,0:T(8,128)(2,1)}, bf16[10,1,8,...) custom-call(f32[10,14,56,384]{3,2,1,0:T(8,128)} %field.3, ...), custom_call_target="tpu_custom_call" | custom-call | flops 9248440320 | bytes 40320000 | tf_op jit(solution)/shard_map/attend/pallas_call | solution.py:197
  86.9 1.9 collective-permute-start.1
  88.8 77.5 %feed.2 = (f32[10,14,56,384]{3,2,1,0:T(8,128)}, f32[10,14,56,384]{3,2,1,0:T(8,128)}, bf16[10,7,56,384]{3,2,1,0:T(8,128)(2,1)}, bf16[10,4,56,384]{3,2,1,0:T(8,128...) custom-call(bf16[10,7,56,384]{3,2,1,0:T(8,128)(2,1)} %bitcast.43, ...), custom_call_target="tpu_custom_call" | custom-call | flops 49049763840 | bytes 47308800 | tf_op jit(solution)/shard_map/feed/pallas_call | solution.py:423
  166.3 0.0 collective-permute-done.1.refs_0_
  166.3 27.6 %feed.3 = (f32[10,14,56,384]{3,2,1,0:T(8,128)}, f32[10,14,56,384]{3,2,1,0:T(8,128)}, bf16[10,3,56,384]{3,2,1,0:T(8,128)(2,1)}, bf16[4,4,48,864]{3,2,1,0:T(8,128)...) custom-call(bf16[10,3,56,384]{3,2,1,0:T(8,128)(2,1)} %collective-permute-, ...), custom_call_target="tpu_custom_call", output_to_operand_aliasing={{0}: (7, {}), {1}: (8, {})} | custom-call | flops 13377208320 | bytes 12902400 | tf_op jit(solution)/shard_map/feed/pallas_call | solution.py:423
  193.9 0.1 collective-permute-start.3
  194.0 1.2 collective-permute-start.2
  195.2 33.8 %unattend.3 = (f32[10,14,56,384]{3,2,1,0:T(8,128)}, f32[384,1152]{1,0:T(8,128)}, f32[1,1152]{1,0:T(1,128)}, f32[56,768]{1,0:T(8,128)}, f32[8,384]{1,0:T(8,128)}) custom-call(bf16[10,1,7,56,384]{4,3,2,1,0:T(8,128)(2,1)} %bitcast.42, bf16[10,1,448,384]{3,2,1,0:T(8,128)(2,1)} %get-tuple-element.106.refs_1_, ...), custom_call_target="tpu_custom_call" | custom-call | flops 18496880640 | bytes 40320000 | tf_op jit(solution)/shard_map/unattend/pallas_call | solution.py:669
  229.0 0.0 collective-permute-done.3
  229.0 2.1 add_convert_fusion
  231.1 1.2 dynamic-slice_bitcast_fusion
  232.3 2.4 collective-permute-start.6
  234.7 0.0 collective-permute-done.2.refs_1_
  234.7 22.2 %unattend.4 = (f32[10,14,56,384]{3,2,1,0:T(8,128)}, bf16[6,3,56,384]{3,2,1,0:T(8,128)(2,1)}, f32[384,1152]{1,0:T(8,128)}, f32[1,1152]{1,0:T(1,128)}, f32[56,768]{1,0:T(8,128)}, /*index=5*/f32[8,384]{1,0:T(8,128)}) custom-call(bf16[10,4,56,384]{3,2,1,0:T(8,128)(2,1)} %get-tuple-element.96.refs_0_, ...), custom_call_target="tpu_custom_call", output_to_operand_aliasing={{0}: (10, {})} | custom-call | flops 11098128384 | bytes 24192000 | tf_op jit(solution)/shard_map/unattend/pallas_call | solution.py:669
  256.9 0.6 collective-permute-start.4
  257.6 16.5 %unattend.5 = (f32[10,14,56,384]{3,2,1,0:T(8,128)}, bf16[4,3,56,384]{3,2,1,0:T(8,128)(2,1)}, f32[384,1152]{1,0:T(8,128)}, f32[24,384]{1,0:T(8,128)}) custom-call(bf16[10,4,56,384]{3,2,1,0:T(8,128)(2,1)} %get-tuple-element.96.refs_0_, bf16[10,3,56,384]{3,2,1,0:T(8,128)(2,1)} %collective-permute-done.2.refs_1_, ...), custom_call_target="tpu_custom_call", output_to_operand_aliasing={{0}: (11, {})} | custom-call | flops 7398752256 | bytes 16128000 | tf_op jit(solution)/shard_map/unattend/pallas_call | solution.py:669
  274.1 1.5 collective-permute-start.5
  275.6 0.0 collective-permute-done.6.feed_got
  275.6 32.8 %reduce_weight.1 = (f32[48,288]{1,0:T(8,128)}, f32[24,384]{1,0:T(8,128)}, f32[48,864]{1,0:T(8,128)}) custom-call(f32[8,48,1152]{2,1,0:T(8,128)} %bitcast.37, f32[24,384]{1,0:T(8,128)} %get-tuple-element.123.small, bf16[2,4,48,864]{3,2,1,0:T(8,128)(2,1)} %get-tuple-element.145.feed_keep, bf16[2,4,48,864]{3,2,1,0:T(8,128)(2,1)} %collective-permute-done.6.feed_got), custom_call_target="tpu_custom_call" | custom-call | tf_op jit(solution)/shard_map/reduce_weight/pallas_call | solution.py:1101
  308.4 0.0 collective-permute-done.5.d_late
  308.4 0.0 collective-permute-done.4.d_normed
  308.4 0.0 copy-start.1
  308.4 0.9 copy-done.1
  309.4 7.3 %finish.1 = (f32[10,14,56,384]{3,2,1,0:T(8,128)}, f32[384]{0:T(512)}, f32[384]{0:T(512)}, f32[48,288]{1,0:T(8,128)}, f32[1152]{0:T(1024)}, /*index=5*/f32[12,169...) custom-call(bf16[6,3,56,384]{3,2,1,0:T(8,128)(2,1)} %copy-done.1, ...), custom_call_target="tpu_custom_call", output_to_operand_aliasing={{0}: (9, {})} | custom-call | flops 11612160 | bytes 5419008 | tf_op jit(solution)/shard_map/finish/pallas_call | solution.py:756
  (28 shorter events, 0.2 us)
Async XLA Ops:
  3.0 32.9 %copy-start.2 = (s32[10,14,56]{2,1,0:T(8,128)S(1)}, s32[10,14,56]{2,1,0:T(8,128)}, u32[]{:S(2)}) copy-start(s32[10,14,56]{2,1,0:T(8,128)} %crops.1) | copy-start | bytes 94084
  34.4 4.0 %copy-start.3 = (f32[169,12]{0,1:T(8,128)S(1)}, f32[169,12]{0,1:T(8,128)}, u32[]{:S(2)}) copy-start(f32[169,12]{0,1:T(8,128)} %param.24) | copy-start | bytes 24340
  34.4 4.0 %copy-start = (bf16[56,64,169,1]{2,1,0,3:T(8,128)(2,1)S(1)}, bf16[56,64,169,1]{2,1,0,3:T(8,128)(2,1)}, u32[]{:S(2)}) copy-start(bf16[56,64,169,1]{2,1,0,3:T(8,128)(2,1)} %constant.64) | copy-start | bytes 3634180
  34.4 31.2 %collective-permute-start = (bf16[10,3,56,384]{3,2,1,0:T(8,128)(2,1)}, bf16[10,3,56,384]{3,2,1,0:T(8,128)(2,1)}, u32[]{:S(2)}, u32[]{:S(2)}) collective-permute-start(bf16[10,3,56,384]{3,2,1,0:T(8,128)(2,1)} %get-tuple-element.80), channel_id=1, source_target_pairs={{0,24},{8,0},{16,8},{24,16},{1,25},{9,1},{17,9},{25,17},{2,26},{10... | collective-permute-start | bytes 3870728 | tf_op jit(solution)/shard_map/ppermute | solution.py:1119
  38.1 2.1 copy-start.6
  38.2 2.1 copy-start.7
  38.2 2.1 copy-start.8
  38.2 2.1 copy-start.9
  38.2 2.1 copy-start.10
  38.2 2.1 copy-start.11
  38.2 2.1 copy-start.4
  38.2 2.1 copy-start.5
  86.9 79.4 %collective-permute-start.1 = (bf16[10,3,56,384]{3,2,1,0:T(8,128)(2,1)}, bf16[10,3,56,384]{3,2,1,0:T(8,128)(2,1)}, u32[]{:S(2)}, u32[]{:S(2)}) collective-permute-start(bf16[10,3,56,384]{3,2,1,0:T(8,128)(2,1)} %bitcast.40), channel_id=1, source_target_pairs={{0,8},{8,16},{16,24},{24,0},{1,9},{9,17},{17,25},{25,1},{2,10},{10... | collective-permute-start | bytes 3870728 | tf_op jit(solution)/shard_map/ppermute | solution.py:1119
  193.9 35.0 %collective-permute-start.3 = (bf16[4,4,48,864]{3,2,1,0:T(8,128)(2,1)}, bf16[4,4,48,864]{3,2,1,0:T(8,128)(2,1)}, u32[]{:S(2)}, u32[]{:S(2)}) collective-permute-start(bf16[4,4,48,864]{3,2,1,0:T(8,128)(2,1)} %get-tuple-element.103), channel_id=1, source_target_pairs={{0,1},{1,0},{2,3},{3,2},{4,5},{5,4},{6,7},{7,6},{8,9},{9,8},{10,11... | collective-permute-start | bytes 3981320 | tf_op jit(solution)/shard_map/ppermute | solution.py:1236
  194.0 40.6 %collective-permute-start.2 = (bf16[10,3,56,384]{3,2,1,0:T(8,128)(2,1)}, bf16[10,3,56,384]{3,2,1,0:T(8,128)(2,1)}, u32[]{:S(2)}, u32[]{:S(2)}) collective-permute-start(bf16[10,3,56,384]{3,2,1,0:T(8,128)(2,1)} %get-tuple-element.97), channel_id=1, source_target_pairs={{0,24},{8,0},{16,8},{24,16},{1,25},{9,1},{17,9},{25,17},{2,26},{10... | collective-permute-start | bytes 3870728 | tf_op jit(solution)/shard_map/ppermute | solution.py:1119
  232.3 43.4 %collective-permute-start.6 = (bf16[2,4,48,864]{3,2,1,0:T(8,128)(2,1)}, bf16[2,4,48,864]{3,2,1,0:T(8,128)(2,1)}, u32[]{:S(2)}, u32[]{:S(2)}) collective-permute-start(bf16[2,4,48,864]{3,2,1,0:T(8,128)(2,1)} %get-tuple-element.124), channel_id=1, source_target_pairs={{0,4},{1,5},{2,6},{3,7},{4,0},{5,1},{6,2},{7,3},{8,12},{9,13},{10,... | collective-permute-start | bytes 1990664 | tf_op jit(solution)/shard_map/ppermute | solution.py:1236
  256.9 51.5 %collective-permute-start.4 = (bf16[6,3,56,384]{3,2,1,0:T(8,128)(2,1)}, bf16[6,3,56,384]{3,2,1,0:T(8,128)(2,1)S(1)}, u32[]{:S(2)}, u32[]{:S(2)}) collective-permute-start(bf16[6,3,56,384]{3,2,1,0:T(8,128)(2,1)} %get-tuple-element.114), channel_id=1, source_target_pairs={{0,8},{8,16},{16,24},{24,0},{1,9},{9,17},{17,25},{25,1},{2,10},{10... | collective-permute-start | bytes 2322440 | tf_op jit(solution)/shard_map/ppermute | solution.py:1119
  274.1 34.3 %collective-permute-start.5 = (bf16[4,3,56,384]{3,2,1,0:T(8,128)(2,1)}, bf16[4,3,56,384]{3,2,1,0:T(8,128)(2,1)}, u32[]{:S(2)}, u32[]{:S(2)}) collective-permute-start(bf16[4,3,56,384]{3,2,1,0:T(8,128)(2,1)} %get-tuple-element.121), channel_id=1, source_target_pairs={{0,8},{8,16},{16,24},{24,0},{1,9},{9,17},{17,25},{25,1},{2,10},{10... | collective-permute-start | bytes 1548296 | tf_op jit(solution)/shard_map/ppermute | solution.py:1119
  308.4 0.9 copy-start.1

commit v5 on v4

--- a/solution.py
+++ b/solution.py
@@ -171,7 +171,7 @@
             mixed_rim[0, 0, r - local] = take_rows(nat, r).astype(bf16)
 
 
-def attend(local, row_of, steps, field, rim, ident, par, weight, place):
+def attend(local, row_of, steps, field, rim, ident, par, weight, place, first=0):
     canvases, _, columns, channels = field.shape
     heads = place.shape[1] // LANES
     windows = columns // WIN
@@ -188,7 +188,7 @@
     if local < WIN:
         specs.append(pl.BlockSpec((1,) + rim.shape[1:], lambda n, s: (n, 0, 0, 0)))
         args.append(rim)
-    specs += [block(windows, 2 * LANES)]
+    specs.append(pl.BlockSpec((1, 1, windows, 2 * LANES), lambda n, s: (n, first + s, 0, 0)))
     specs += [whole(a) for a in (par, weight, place)]
     args += [ident, par, weight, place]
     lead = (canvases, steps)
@@ -809,8 +809,9 @@
     return place
 
 
-def gather_kernel(strips, lines, shard, field, crops, *refs):
-    *outs, rim, rim_crops, blocks, crop_rows, crop_got, first_rows, send_sem, recv_sem, crop_sem, field_sem = refs
+def gather_kernel(strips, lines, own_parts, *refs):
+    own_refs, (field, crops, *refs) = refs[:own_parts], refs[own_parts:]
+    *outs, rim, rim_crops, shard, blocks, crop_rows, crop_got, first_rows, send_sem, recv_sem, crop_sem, field_sem = refs
     strip, line = lax.axis_index("strip"), lax.axis_index("canvas")
     core, chip, chips = line % 2, line // 2, lines // 2
     other = (strip, line + 1 - 2 * core)
@@ -824,6 +825,13 @@
     for partner in partners:
         pl.semaphore_signal(barrier, inc=1, device_id=partner, device_id_type=MESH)
     crop_rows[...] = crops[:, :SHIFT]
+    if own_parts == 1:
+        shard[...] = own_refs[0][...]
+    else:
+        qkv, proj, fc1, fc2 = own_refs
+        height = shard.shape[0]
+        pieces = [fc2[k * height : (k + 1) * height] for k in range(fc2.shape[0] // height)]
+        shard[...] = jnp.concatenate([qkv[...], proj[...], fc1[...]] + pieces, 1)
     pl.semaphore_wait(barrier, len(partners))
 
     line_of = lambda n, twin=0: ((chip + n) % chips) * 2 + (1 - core if twin else core)
@@ -930,8 +938,11 @@
     rows = qkv.shape[0]
     deep = fc2.shape[0] // rows
     narrow = fc2.shape[1]
-    shard = jnp.concatenate([qkv, proj, fc1] + [fc2[k * rows : (k + 1) * rows] for k in range(deep)], 1)
     joined = rows % 16 == 0
+    own = [qkv, proj, fc1, fc2]
+    if not joined:
+        own = [jnp.concatenate([qkv, proj, fc1] + [fc2[k * rows : (k + 1) * rows] for k in range(deep)], 1)]
+    shard = jax.ShapeDtypeStruct((rows, qkv.shape[1] + proj.shape[1] + fc1.shape[1] + deep * narrow), qkv.dtype)
     full = [jax.ShapeDtypeStruct((lines * w.shape[0], strips * w.shape[1]), w.dtype) for w in (qkv, proj, fc1, fc2)]
     blocks = (lines, strips) + shard.shape
     if not joined:
@@ -939,18 +950,18 @@
     rim = (field.shape[0], SHIFT) + field.shape[2:]
     vmem = pl.BlockSpec(memory_space=pltpu.VMEM)
     got = pl.pallas_call(
-        functools.partial(gather_kernel, strips, lines),
-        in_specs=[vmem, pl.BlockSpec(memory_space=pl.ANY), vmem],
+        functools.partial(gather_kernel, strips, lines, len(own)),
+        in_specs=[vmem] * len(own) + [pl.BlockSpec(memory_space=pl.ANY), vmem],
         out_specs=[vmem] * (len(full) + 2),
         out_shape=full + [jax.ShapeDtypeStruct(rim, bf16), jax.ShapeDtypeStruct(rim[:3], jnp.int32)],
-        scratch_shapes=[pltpu.VMEM(blocks, shard.dtype)]
+        scratch_shapes=[pltpu.VMEM(shard.shape, shard.dtype), pltpu.VMEM(blocks, shard.dtype)]
         + [pltpu.VMEM(rim[:3], jnp.int32)] * 2
         + [pltpu.VMEM(rim, f32)]
         + [pltpu.SemaphoreType.DMA((lines * strips,))] * 2
         + [pltpu.SemaphoreType.DMA((2,)), pltpu.SemaphoreType.DMA((1,))],
         compiler_params=pltpu.CompilerParams(collective_id=0, has_side_effects=True, vmem_limit_bytes=VMEM_BYTES),
         name="gather_weights",
-    )(shard, field, crop_ids)
+    )(*own, field, crop_ids)
     if joined:
         return got
     got, rim, crops, at, out = got[0], got[1], got[2], 0, []
@@ -1185,10 +1196,9 @@
     ).astype(jnp.int32)
     region = row_band[:, None] * 3 + col_band[None, :]
 
-    def idents(crops, first):
-        count = crops.shape[1]
-        ident = jnp.roll(crops, -SHIFT, 2) * 9 + region[None, first : first + count]
-        return window_idents(ident.reshape(canvases, count // WIN, WIN, columns))
+    crops = jnp.concatenate([crop_ids[:, SHIFT:], rim_crops], 1)
+    ident = jnp.roll(crops, -SHIFT, 2) * 9 + region[None]
+    ident = window_idents(ident.reshape(canvases, tops + 1, WIN, columns))
 
     hot = table_hot(entries)
     left, parts = rel_table * math.log2(math.e), []
@@ -1207,14 +1217,11 @@
     low = WIN - SHIFT
 
     if tops:
-        ident_top = idents(crop_ids[:, SHIFT : SHIFT + tops * WIN], 0)
         mixed_top, cells_top, qkv_top, probs_top = attend(
-            WIN, top_row, tops, field, None, ident_top, *fixed
+            WIN, top_row, tops, field, None, ident, *fixed
         )
-    low_crops = jnp.concatenate([crop_ids[:, SHIFT + tops * WIN :], rim_crops], 1)
-    ident_low = idents(low_crops, tops * WIN)
     mixed_low, mixed_rim, cells_low, qkv_low, probs_low = attend(
-        low, lambda s: low_row, 1, field, rim_hat, ident_low, *fixed
+        low, lambda s: low_row, 1, field, rim_hat, ident, *fixed, first=tops
     )
     mixed_rim = from_behind(mixed_rim[:, 0], "strip", 1)
     feed_fixed = (par, w_proj, w_fc1, w_fc2)

time: 323 us -> 320 us (level)
  transfers between devices with their start and end apart: 7 -> 7, of which waited for: 1 -> 1; matrix products, arithmetic and copies ran while one was open for 3% -> 3% of each run, Pallas kernels for 64% -> 65%
where the time goes in v5:
time: 320 us; the launch traced here: 314 us
  Pallas kernels  292 us (91%)
  starting transfers between devices  9.12 us (3%)
  local copies, waits for them, and re-layouts  5.16 us (2%)
  other arithmetic  4.62 us (1%)
    pallas_call x2, Pallas kernels, feed(): pl.pallas_call(kernel, grid=(canvases // together,), in_specs=specs, out_...  105 us
    pallas_call x3, Pallas kernels, unattend(): pl.pallas_call(kernel, grid=(canvases, steps), in_specs=specs, out_specs=...  72.5 us
    pallas_call x2, Pallas kernels, attend(): pl.pallas_call(functools.partial(attend_kernel, local, heads), grid=grid,...  42.7 us
    pallas_call x1, Pallas kernels, reduce_weight(): pl.pallas_call(functools.partial(reduce_kernel, strips, lines), in_specs=...  32.8 us
    pallas_call x1, Pallas kernels, gather_weights(): pl.pallas_call(functools.partial(gather_kernel, strips, lines, len(own)),...  31.5 us
    pallas_call x1, Pallas kernels, finish(): pl.pallas_call(functools.partial(finish_kernel, neat, heads, entries, ear...  7.3 us
    ppermute x5, starting transfers between devices, from_behind(): return lax.ppermute(value, axis, pairs)  6.67 us
  transfers between devices with their start and end apart: 7, of which 1 were waited for; matrix products, arithmetic and copies ran while one was open for 3% of the time, Pallas kernels for 65%

profile of v5, /device:TPU:0, one launch (start us, length us, event | category | flops | bytes accessed | tf_op | source)
XLA Modules:
  0.0 314.5 jit_solution(17786292660216515923)
XLA Ops:
  0.6 0.0 copy-start.2
  0.7 31.5 %gather_weights.1 = (bf16[384,1152]{1,0:T(8,128)(2,1)}, bf16[384,384]{1,0:T(8,128)(2,1)}, bf16[384,1536]{1,0:T(8,128)(2,1)}, bf16[1536,384]{1,0:T(8,128)(2,1)}, ...) custom-call(bf16[48,288]{1,0:T(8,128)(2,1)} %refs_0_.3, bf16[48,96]{1,0:T(8,128)(2,1)} %refs_1_.2, ...), custom_call_target="tpu_custom_call" | custom-call | tf_op jit(solution)/shard_map/gather_weights/pallas_call | solution.py:952
  32.1 1.5 collective-permute-start
  33.6 0.0 copy-done.2
  33.6 0.7 pad_add_fusion
  34.4 0.8 slice_add_fusion
  35.2 0.1 add_multiply_fusion
  35.3 0.2 mul.30
  35.6 0.1 broadcast_add_fusion
  35.7 0.0 copy-start.3
  35.7 0.0 copy-start
  35.7 0.1 copy.41
  35.9 0.1 pad.8.clone
  35.9 0.0 copy-start.6
  35.9 0.0 copy-start.7
  36.0 0.0 copy-start.8
  36.0 0.0 copy-start.9
  36.0 0.0 copy-start.10
  36.0 0.0 copy-start.11
  36.0 0.0 copy-start.4
  36.0 0.0 copy-start.5
  36.0 0.2 reshape.108
  36.3 0.2 copy-done.3
  36.4 0.8 copy-done
  37.2 1.0 convolution_reduce_fusion
  38.2 0.8 reshape.110.refs_5_.refs_4_
  39.0 0.0 copy-done.6
  39.0 0.0 copy-done.7
  39.0 0.0 copy-done.8
  39.1 0.0 copy-done.9
  39.1 0.0 copy-done.10
  39.1 0.0 copy-done.11
  39.1 0.0 copy-done.4
  39.2 0.0 copy-done.5
  39.2 0.6 reshape.109.refs_3_.refs_2_.refs_4_.refs_6_.refs_8_.par
  39.8 0.7 pad_add_fusion.1.refs_2_.refs_1_
  40.5 21.4 %attend.3 = (bf16[10,1,7,56,384]{4,3,2,1,0:T(8,128)(2,1)}, bf16[10,1,448,384]{3,2,1,0:T(8,128)(2,1)}, bf16[10,1,8,56,1152]{4,3,2,1,0:T(8,128)(2,1)}, bf16[10,1,8,56,768]{4,3,2,1,0:T(8,128)(2,1)}) custom-call(f32[10,14,56,384]{3,2,1,0:T(8,128)} %field.1, s32[10,2,8,128]{3,2,1,0:T(8,128)} %pad_add_fusion.1.refs_2_.refs_1_, ...), custom_call_target="tpu_custom_call" | custom-call | flops 9248440320 | bytes 40320000 | tf_op jit(solution)/shard_map/attend/pallas_call | solution.py:197
  61.9 1.4 collective-permute-done.refs_1_.refs_2_
  63.3 21.3 %attend.2 = (bf16[10,1,4,56,384]{4,3,2,1,0:T(8,128)(2,1)}, bf16[10,1,3,56,384]{4,3,2,1,0:T(8,128)(2,1)}, bf16[10,1,448,384]{3,2,1,0:T(8,128)(2,1)}, bf16[10,1,8,...) custom-call(f32[10,14,56,384]{3,2,1,0:T(8,128)} %field.1, ...), custom_call_target="tpu_custom_call" | custom-call | flops 9248440320 | bytes 40320000 | tf_op jit(solution)/shard_map/attend/pallas_call | solution.py:197
  84.6 1.9 collective-permute-start.1
  86.5 77.5 %feed.2 = (f32[10,14,56,384]{3,2,1,0:T(8,128)}, f32[10,14,56,384]{3,2,1,0:T(8,128)}, bf16[10,7,56,384]{3,2,1,0:T(8,128)(2,1)}, bf16[10,4,56,384]{3,2,1,0:T(8,128...) custom-call(bf16[10,7,56,384]{3,2,1,0:T(8,128)(2,1)} %bitcast.33, ...), custom_call_target="tpu_custom_call" | custom-call | flops 49049763840 | bytes 47308800 | tf_op jit(solution)/shard_map/feed/pallas_call | solution.py:423
  164.0 0.0 collective-permute-done.1.refs_0_
  164.0 27.6 %feed.3 = (f32[10,14,56,384]{3,2,1,0:T(8,128)}, f32[10,14,56,384]{3,2,1,0:T(8,128)}, bf16[10,3,56,384]{3,2,1,0:T(8,128)(2,1)}, bf16[4,4,48,864]{3,2,1,0:T(8,128)...) custom-call(bf16[10,3,56,384]{3,2,1,0:T(8,128)(2,1)} %collective-permute-, ...), custom_call_target="tpu_custom_call", output_to_operand_aliasing={{0}: (7, {}), {1}: (8, {})} | custom-call | flops 13377208320 | bytes 12902400 | tf_op jit(solution)/shard_map/feed/pallas_call | solution.py:423
  191.7 0.1 collective-permute-start.3
  191.7 1.2 collective-permute-start.2
  192.9 33.8 %unattend.3 = (f32[10,14,56,384]{3,2,1,0:T(8,128)}, f32[384,1152]{1,0:T(8,128)}, f32[1,1152]{1,0:T(1,128)}, f32[56,768]{1,0:T(8,128)}, f32[8,384]{1,0:T(8,128)}) custom-call(bf16[10,1,7,56,384]{4,3,2,1,0:T(8,128)(2,1)} %bitcast.32, bf16[10,1,448,384]{3,2,1,0:T(8,128)(2,1)} %get-tuple-element.106.refs_1_, ...), custom_call_target="tpu_custom_call" | custom-call | flops 18496880640 | bytes 40320000 | tf_op jit(solution)/shard_map/unattend/pallas_call | solution.py:669
  226.7 0.0 collective-permute-done.3
  226.7 2.1 add_convert_fusion
  228.8 1.2 dynamic-slice_bitcast_fusion
  230.0 2.4 collective-permute-start.6
  232.4 0.0 collective-permute-done.2.refs_1_
  232.4 22.2 %unattend.4 = (f32[10,14,56,384]{3,2,1,0:T(8,128)}, bf16[6,3,56,384]{3,2,1,0:T(8,128)(2,1)}, f32[384,1152]{1,0:T(8,128)}, f32[1,1152]{1,0:T(1,128)}, f32[56,768]{1,0:T(8,128)}, /*index=5*/f32[8,384]{1,0:T(8,128)}) custom-call(bf16[10,4,56,384]{3,2,1,0:T(8,128)(2,1)} %get-tuple-element.96.refs_0_, ...), custom_call_target="tpu_custom_call", output_to_operand_aliasing={{0}: (10, {})} | custom-call | flops 11098128384 | bytes 24192000 | tf_op jit(solution)/shard_map/unattend/pallas_call | solution.py:669
  254.6 0.7 collective-permute-start.4
  255.3 16.5 %unattend.5 = (f32[10,14,56,384]{3,2,1,0:T(8,128)}, bf16[4,3,56,384]{3,2,1,0:T(8,128)(2,1)}, f32[384,1152]{1,0:T(8,128)}, f32[24,384]{1,0:T(8,128)}) custom-call(bf16[10,4,56,384]{3,2,1,0:T(8,128)(2,1)} %get-tuple-element.96.refs_0_, bf16[10,3,56,384]{3,2,1,0:T(8,128)(2,1)} %collective-permute-done.2.refs_1_, ...), custom_call_target="tpu_custom_call", output_to_operand_aliasing={{0}: (11, {})} | custom-call | flops 7398752256 | bytes 16128000 | tf_op jit(solution)/shard_map/unattend/pallas_call | solution.py:669
  271.8 1.5 collective-permute-start.5
  273.3 0.0 collective-permute-done.6.feed_got
  273.3 32.8 %reduce_weight.1 = (f32[48,288]{1,0:T(8,128)}, f32[24,384]{1,0:T(8,128)}, f32[48,864]{1,0:T(8,128)}) custom-call(f32[8,48,1152]{2,1,0:T(8,128)} %bitcast.29, f32[24,384]{1,0:T(8,128)} %get-tuple-element.123.small, bf16[2,4,48,864]{3,2,1,0:T(8,128)(2,1)} %get-tuple-element.145.feed_keep, bf16[2,4,48,864]{3,2,1,0:T(8,128)(2,1)} %collective-permute-done.6.feed_got), custom_call_target="tpu_custom_call" | custom-call | tf_op jit(solution)/shard_map/reduce_weight/pallas_call | solution.py:1112
  306.1 0.0 collective-permute-done.5.d_late
  306.1 0.0 collective-permute-done.4.d_normed
  306.1 0.0 copy-start.1
  306.1 0.9 copy-done.1
  307.0 7.3 %finish.1 = (f32[10,14,56,384]{3,2,1,0:T(8,128)}, f32[384]{0:T(512)}, f32[384]{0:T(512)}, f32[48,288]{1,0:T(8,128)}, f32[1152]{0:T(1024)}, /*index=5*/f32[12,169...) custom-call(bf16[6,3,56,384]{3,2,1,0:T(8,128)(2,1)} %copy-done.1, ...), custom_call_target="tpu_custom_call", output_to_operand_aliasing={{0}: (9, {})} | custom-call | flops 11612160 | bytes 5419008 | tf_op jit(solution)/shard_map/finish/pallas_call | solution.py:756
  (15 shorter events, 0.1 us)
Async XLA Ops:
  0.6 33.0 %copy-start.2 = (s32[10,14,56]{2,1,0:T(8,128)S(1)}, s32[10,14,56]{2,1,0:T(8,128)}, u32[]{:S(2)}) copy-start(s32[10,14,56]{2,1,0:T(8,128)} %refs_5_.1) | copy-start | bytes 94084
  32.1 31.2 %collective-permute-start = (bf16[10,3,56,384]{3,2,1,0:T(8,128)(2,1)}, bf16[10,3,56,384]{3,2,1,0:T(8,128)(2,1)}, u32[]{:S(2)}, u32[]{:S(2)}) collective-permute-start(bf16[10,3,56,384]{3,2,1,0:T(8,128)(2,1)} %get-tuple-element.80), channel_id=1, source_target_pairs={{0,24},{8,0},{16,8},{24,16},{1,25},{9,1},{17,9},{25,17},{2,26},{10... | collective-permute-start | bytes 3870728 | tf_op jit(solution)/shard_map/ppermute | solution.py:1130
  35.7 0.7 copy-start.3
  35.7 1.5 copy-start
  35.9 3.1 copy-start.6
  35.9 3.1 copy-start.7
  36.0 3.1 copy-start.8
  36.0 3.1 copy-start.9
  36.0 3.1 copy-start.10
  36.0 3.1 copy-start.11
  36.0 3.1 copy-start.4
  36.0 3.1 copy-start.5
  84.6 79.4 %collective-permute-start.1 = (bf16[10,3,56,384]{3,2,1,0:T(8,128)(2,1)}, bf16[10,3,56,384]{3,2,1,0:T(8,128)(2,1)}, u32[]{:S(2)}, u32[]{:S(2)}) collective-permute-start(bf16[10,3,56,384]{3,2,1,0:T(8,128)(2,1)} %bitcast.30), channel_id=1, source_target_pairs={{0,8},{8,16},{16,24},{24,0},{1,9},{9,17},{17,25},{25,1},{2,10},{10... | collective-permute-start | bytes 3870728 | tf_op jit(solution)/shard_map/ppermute | solution.py:1130
  191.7 35.0 %collective-permute-start.3 = (bf16[4,4,48,864]{3,2,1,0:T(8,128)(2,1)}, bf16[4,4,48,864]{3,2,1,0:T(8,128)(2,1)}, u32[]{:S(2)}, u32[]{:S(2)}) collective-permute-start(bf16[4,4,48,864]{3,2,1,0:T(8,128)(2,1)} %get-tuple-element.103), channel_id=1, source_target_pairs={{0,1},{1,0},{2,3},{3,2},{4,5},{5,4},{6,7},{7,6},{8,9},{9,8},{10,11... | collective-permute-start | bytes 3981320 | tf_op jit(solution)/shard_map/ppermute | solution.py:1243
  191.7 40.6 %collective-permute-start.2 = (bf16[10,3,56,384]{3,2,1,0:T(8,128)(2,1)}, bf16[10,3,56,384]{3,2,1,0:T(8,128)(2,1)}, u32[]{:S(2)}, u32[]{:S(2)}) collective-permute-start(bf16[10,3,56,384]{3,2,1,0:T(8,128)(2,1)} %get-tuple-element.97), channel_id=1, source_target_pairs={{0,24},{8,0},{16,8},{24,16},{1,25},{9,1},{17,9},{25,17},{2,26},{10... | collective-permute-start | bytes 3870728 | tf_op jit(solution)/shard_map/ppermute | solution.py:1130
  230.0 43.3 %collective-permute-start.6 = (bf16[2,4,48,864]{3,2,1,0:T(8,128)(2,1)}, bf16[2,4,48,864]{3,2,1,0:T(8,128)(2,1)}, u32[]{:S(2)}, u32[]{:S(2)}) collective-permute-start(bf16[2,4,48,864]{3,2,1,0:T(8,128)(2,1)} %get-tuple-element.124), channel_id=1, source_target_pairs={{0,4},{1,5},{2,6},{3,7},{4,0},{5,1},{6,2},{7,3},{8,12},{9,13},{10,... | collective-permute-start | bytes 1990664 | tf_op jit(solution)/shard_map/ppermute | solution.py:1243
  254.6 51.5 %collective-permute-start.4 = (bf16[6,3,56,384]{3,2,1,0:T(8,128)(2,1)}, bf16[6,3,56,384]{3,2,1,0:T(8,128)(2,1)S(1)}, u32[]{:S(2)}, u32[]{:S(2)}) collective-permute-start(bf16[6,3,56,384]{3,2,1,0:T(8,128)(2,1)} %get-tuple-element.114), channel_id=1, source_target_pairs={{0,8},{8,16},{16,24},{24,0},{1,9},{9,17},{17,25},{25,1},{2,10},{10... | collective-permute-start | bytes 2322440 | tf_op jit(solution)/shard_map/ppermute | solution.py:1130
  271.8 34.3 %collective-permute-start.5 = (bf16[4,3,56,384]{3,2,1,0:T(8,128)(2,1)}, bf16[4,3,56,384]{3,2,1,0:T(8,128)(2,1)}, u32[]{:S(2)}, u32[]{:S(2)}) collective-permute-start(bf16[4,3,56,384]{3,2,1,0:T(8,128)(2,1)} %get-tuple-element.121), channel_id=1, source_target_pairs={{0,8},{8,16},{16,24},{24,0},{1,9},{9,17},{17,25},{25,1},{2,10},{10... | collective-permute-start | bytes 1548296 | tf_op jit(solution)/shard_map/ppermute | solution.py:1130
  306.1 0.9 copy-start.1

commit v6 on v5

--- a/solution.py
+++ b/solution.py
@@ -66,6 +66,26 @@
 def spread(part, mask, order):
     padded = jnp.concatenate([part, jnp.zeros((LANES - SLOTS, part.shape[1]), part.dtype)], 0)
     return jnp.concatenate([padded * mask[h : h + 1] for h in order], 0)
+
+
+def turn_pair(one, two):
+    none = jnp.zeros((LANES - SLOTS, one.shape[1]), one.dtype)
+    return jnp.concatenate([one, none, two, none], 0).T
+
+
+def spread_turned(pair, odd):
+    size = pair.shape[0] // PACK
+    swapped = jnp.concatenate([pair[:, LANES:], pair[:, :LANES]], 1)
+    low = (lax.broadcasted_iota(jnp.int32, (1, 2 * LANES), 1) < LANES).astype(pair.dtype)
+    zero = jnp.zeros((size, 2 * LANES), pair.dtype)
+
+    def block(h):
+        source = pair if h % 2 == odd else swapped
+        return source[h * size : (h + 1) * size] * (low if h % 2 == 0 else 1 - low)
+
+    left = jnp.concatenate([block(0), block(1), zero, zero], 0)
+    right = jnp.concatenate([zero, zero, block(2), block(3)], 0)
+    return jnp.concatenate([left, right], 1)
 
 
 def flip(wide):
@@ -127,16 +147,20 @@
     def part(w, base, p):
         return qkv_out[0, 0, w, :, base + p * group : base + (p + 1) * group]
 
-    packs = [(w, p) for w in range(windows) for p in range(heads // PACK)]
+    packs = [(w + odd, p) for w in range(0, windows, 2) for p in range(heads // PACK) for odd in range(2)]
+    turned = {}
     keys = jnp.where(ident[0, 0] < 0, -1, ident[0, 0]).T
 
     def first(i):
         w, p = packs[i]
-        if p == 0:
-            rows = slice(w * SLOTS, (w + 1) * SLOTS)
-            qkv_out[0, 0, w, :, :channels] = (wide[rows, :channels] * scale).astype(bf16)
-            qkv_out[0, 0, w, :, channels:] = wide[rows, channels:].astype(bf16)
-        raw[i % RING] = nt(part(w, channels, p), spread(part(w, 0, p), mask, range(PACK)))
+        if p == 0 and w % 2 == 0:
+            for n in (w, w + 1):
+                rows = slice(n * SLOTS, (n + 1) * SLOTS)
+                qkv_out[0, 0, n, :, :channels] = (wide[rows, :channels] * scale).astype(bf16)
+                qkv_out[0, 0, n, :, channels:] = wide[rows, channels:].astype(bf16)
+        if w % 2 == 0:
+            turned[p] = turn_pair(part(w, 0, p), part(w + 1, 0, p))
+        raw[i % RING] = nn(part(w, channels, p), spread_turned(turned[p], w % 2))
 
     def second(i):
         w, p = packs[i]
@@ -231,7 +255,7 @@
 
 HIDDEN_STEP = 256
 ROWS_STEP = 16
-LATE = 2
+LATE = 6
 
 
 def feed_kernel(pieces, together, rows, chain, *refs):
@@ -535,7 +559,8 @@
     for w in range(windows):
         d_win[w] = jnp.where(real, take_window(nat, w), 0.0).astype(bf16)
     mask = head_rows(channels, heads)
-    packs = [(w, p) for w in range(windows) for p in range(heads // PACK)]
+    packs = [(w + odd, p) for w in range(0, windows, 2) for p in range(heads // PACK) for odd in range(2)]
+    turned = {}
 
     def part(w, base, p):
         return qkv[0, 0, w, :, base + p * group : base + (p + 1) * group]
@@ -546,7 +571,10 @@
 
     def first(i):
         w, p = packs[i]
-        raw[i % RING] = nt(part(w, 2 * channels, p), spread_d(i))
+        if w % 2 == 0:
+            lanes = slice(p * group, (p + 1) * group)
+            turned[p] = turn_pair(d_win[w, :, lanes], d_win[w + 1, :, lanes])
+        raw[i % RING] = nn(part(w, 2 * channels, p), spread_turned(turned[p], w % 2))
 
     def second(i):
         w, p = packs[i]

time: 320 us -> 318 us (level)
  no operation moved by 1% of the time
where the time goes in v6:
time: 318 us; the launch traced here: 312 us
  Pallas kernels  290 us (91%)
  starting transfers between devices  9.13 us (3%)
  local copies, waits for them, and re-layouts  5.16 us (2%)
  other arithmetic  4.62 us (1%)
    pallas_call x2, Pallas kernels, feed(): pl.pallas_call(kernel, grid=(canvases // together,), in_specs=specs, out_...  105 us
    pallas_call x3, Pallas kernels, unattend(): pl.pallas_call(kernel, grid=(canvases, steps), in_specs=specs, out_specs=...  71.6 us
    pallas_call x2, Pallas kernels, attend(): pl.pallas_call(functools.partial(attend_kernel, local, heads), grid=grid,...  41.7 us
    pallas_call x1, Pallas kernels, reduce_weight(): pl.pallas_call(functools.partial(reduce_kernel, strips, lines), in_specs=...  32.8 us
    pallas_call x1, Pallas kernels, gather_weights(): pl.pallas_call(functools.partial(gather_kernel, strips, lines, len(own)),...  31.5 us
    pallas_call x1, Pallas kernels, finish(): pl.pallas_call(functools.partial(finish_kernel, neat, heads, entries, ear...  7.3 us
    ppermute x5, starting transfers between devices, from_behind(): return lax.ppermute(value, axis, pairs)  6.67 us
  transfers between devices with their start and end apart: 7, of which 1 were waited for; matrix products, arithmetic and copies ran while one was open for 3% of the time, Pallas kernels for 65%

profile of v6, /device:TPU:0, one launch (start us, length us, event | category | flops | bytes accessed | tf_op | source)
XLA Modules:
  0.0 312.4 jit_solution(472836361538054067)
XLA Ops:
  0.6 0.0 copy-start.2
  0.7 31.5 %gather_weights.1 = (bf16[384,1152]{1,0:T(8,128)(2,1)}, bf16[384,384]{1,0:T(8,128)(2,1)}, bf16[384,1536]{1,0:T(8,128)(2,1)}, bf16[1536,384]{1,0:T(8,128)(2,1)}, ...) custom-call(bf16[48,288]{1,0:T(8,128)(2,1)} %refs_0_.3, bf16[48,96]{1,0:T(8,128)(2,1)} %refs_1_.2, ...), custom_call_target="tpu_custom_call" | custom-call | tf_op jit(solution)/shard_map/gather_weights/pallas_call | solution.py:980
  32.1 1.5 collective-permute-start
  33.6 0.0 copy-done.2
  33.6 0.7 pad_add_fusion
  34.4 0.8 slice_add_fusion
  35.2 0.1 add_multiply_fusion
  35.3 0.2 mul.30
  35.6 0.1 broadcast_add_fusion
  35.7 0.0 copy-start.3
  35.7 0.0 copy-start
  35.7 0.1 copy.41
  35.9 0.1 pad.8.clone
  35.9 0.0 copy-start.6
  35.9 0.0 copy-start.7
  36.0 0.0 copy-start.8
  36.0 0.0 copy-start.9
  36.0 0.0 copy-start.10
  36.0 0.0 copy-start.11
  36.0 0.0 copy-start.4
  36.0 0.0 copy-start.5
  36.0 0.2 reshape.108
  36.3 0.2 copy-done.3
  36.4 0.8 copy-done
  37.2 1.0 convolution_reduce_fusion
  38.2 0.8 reshape.110.refs_5_.refs_4_
  39.0 0.0 copy-done.6
  39.0 0.0 copy-done.7
  39.0 0.0 copy-done.8
  39.1 0.0 copy-done.9
  39.1 0.0 copy-done.10
  39.1 0.0 copy-done.11
  39.1 0.0 copy-done.4
  39.2 0.0 copy-done.5
  39.2 0.6 reshape.109.refs_3_.refs_2_.refs_4_.refs_6_.refs_8_.par
  39.8 0.7 pad_add_fusion.1.refs_2_.refs_1_
  40.5 21.1 %attend.3 = (bf16[10,1,7,56,384]{4,3,2,1,0:T(8,128)(2,1)}, bf16[10,1,448,384]{3,2,1,0:T(8,128)(2,1)}, bf16[10,1,8,56,1152]{4,3,2,1,0:T(8,128)(2,1)}, bf16[10,1,8,56,768]{4,3,2,1,0:T(8,128)(2,1)}) custom-call(f32[10,14,56,384]{3,2,1,0:T(8,128)} %field.1, s32[10,2,8,128]{3,2,1,0:T(8,128)} %pad_add_fusion.1.refs_2_.refs_1_, ...), custom_call_target="tpu_custom_call" | custom-call | flops 9248440320 | bytes 40320000 | tf_op jit(solution)/shard_map/attend/pallas_call | solution.py:221
  61.6 1.7 collective-permute-done.refs_1_.refs_2_
  63.3 20.6 %attend.2 = (bf16[10,1,4,56,384]{4,3,2,1,0:T(8,128)(2,1)}, bf16[10,1,3,56,384]{4,3,2,1,0:T(8,128)(2,1)}, bf16[10,1,448,384]{3,2,1,0:T(8,128)(2,1)}, bf16[10,1,8,...) custom-call(f32[10,14,56,384]{3,2,1,0:T(8,128)} %field.1, ...), custom_call_target="tpu_custom_call" | custom-call | flops 9248440320 | bytes 40320000 | tf_op jit(solution)/shard_map/attend/pallas_call | solution.py:221
  84.0 1.9 collective-permute-start.1
  85.8 76.9 %feed.2 = (f32[10,14,56,384]{3,2,1,0:T(8,128)}, f32[10,14,56,384]{3,2,1,0:T(8,128)}, bf16[10,7,56,384]{3,2,1,0:T(8,128)(2,1)}, bf16[10,4,56,384]{3,2,1,0:T(8,128...) custom-call(bf16[10,7,56,384]{3,2,1,0:T(8,128)(2,1)} %bitcast.33, ...), custom_call_target="tpu_custom_call" | custom-call | flops 49049763840 | bytes 47308800 | tf_op jit(solution)/shard_map/feed/pallas_call | solution.py:447
  162.8 0.0 collective-permute-done.1.refs_0_
  162.8 27.7 %feed.3 = (f32[10,14,56,384]{3,2,1,0:T(8,128)}, f32[10,14,56,384]{3,2,1,0:T(8,128)}, bf16[10,3,56,384]{3,2,1,0:T(8,128)(2,1)}, bf16[4,4,48,864]{3,2,1,0:T(8,128)...) custom-call(bf16[10,3,56,384]{3,2,1,0:T(8,128)(2,1)} %collective-permute-, ...), custom_call_target="tpu_custom_call", output_to_operand_aliasing={{0}: (7, {}), {1}: (8, {})} | custom-call | flops 13377208320 | bytes 12902400 | tf_op jit(solution)/shard_map/feed/pallas_call | solution.py:447
  190.5 0.1 collective-permute-start.3
  190.6 1.2 collective-permute-start.2
  191.7 33.6 %unattend.3 = (f32[10,14,56,384]{3,2,1,0:T(8,128)}, f32[384,1152]{1,0:T(8,128)}, f32[1,1152]{1,0:T(1,128)}, f32[56,768]{1,0:T(8,128)}, f32[8,384]{1,0:T(8,128)}) custom-call(bf16[10,1,7,56,384]{4,3,2,1,0:T(8,128)(2,1)} %bitcast.32, bf16[10,1,448,384]{3,2,1,0:T(8,128)(2,1)} %get-tuple-element.106.refs_1_, ...), custom_call_target="tpu_custom_call" | custom-call | flops 18496880640 | bytes 40320000 | tf_op jit(solution)/shard_map/unattend/pallas_call | solution.py:697
  225.3 0.0 collective-permute-done.3
  225.3 2.1 add_convert_fusion
  227.4 1.2 dynamic-slice_bitcast_fusion
  228.6 2.4 collective-permute-start.6
  231.0 0.0 collective-permute-done.2.refs_1_
  231.0 21.8 %unattend.4 = (f32[10,14,56,384]{3,2,1,0:T(8,128)}, bf16[6,3,56,384]{3,2,1,0:T(8,128)(2,1)}, f32[384,1152]{1,0:T(8,128)}, f32[1,1152]{1,0:T(1,128)}, f32[56,768]{1,0:T(8,128)}, /*index=5*/f32[8,384]{1,0:T(8,128)}) custom-call(bf16[10,4,56,384]{3,2,1,0:T(8,128)(2,1)} %get-tuple-element.96.refs_0_, ...), custom_call_target="tpu_custom_call", output_to_operand_aliasing={{0}: (10, {})} | custom-call | flops 11098128384 | bytes 24192000 | tf_op jit(solution)/shard_map/unattend/pallas_call | solution.py:697
  252.8 0.6 collective-permute-start.4
  253.5 16.2 %unattend.5 = (f32[10,14,56,384]{3,2,1,0:T(8,128)}, bf16[4,3,56,384]{3,2,1,0:T(8,128)(2,1)}, f32[384,1152]{1,0:T(8,128)}, f32[24,384]{1,0:T(8,128)}) custom-call(bf16[10,4,56,384]{3,2,1,0:T(8,128)(2,1)} %get-tuple-element.96.refs_0_, bf16[10,3,56,384]{3,2,1,0:T(8,128)(2,1)} %collective-permute-done.2.refs_1_, ...), custom_call_target="tpu_custom_call", output_to_operand_aliasing={{0}: (11, {})} | custom-call | flops 7398752256 | bytes 16128000 | tf_op jit(solution)/shard_map/unattend/pallas_call | solution.py:697
  269.7 1.5 collective-permute-start.5
  271.2 0.0 collective-permute-done.6.feed_got
  271.2 32.8 %reduce_weight.1 = (f32[48,288]{1,0:T(8,128)}, f32[24,384]{1,0:T(8,128)}, f32[48,864]{1,0:T(8,128)}) custom-call(f32[8,48,1152]{2,1,0:T(8,128)} %bitcast.29, f32[24,384]{1,0:T(8,128)} %get-tuple-element.123.small, bf16[2,4,48,864]{3,2,1,0:T(8,128)(2,1)} %get-tuple-element.145.feed_keep, bf16[2,4,48,864]{3,2,1,0:T(8,128)(2,1)} %collective-permute-done.6.feed_got), custom_call_target="tpu_custom_call" | custom-call | tf_op jit(solution)/shard_map/reduce_weight/pallas_call | solution.py:1140
  304.0 0.0 collective-permute-done.5.d_late
  304.0 0.0 collective-permute-done.4.d_normed
  304.0 0.0 copy-start.1
  304.0 0.9 copy-done.1
  304.9 7.3 %finish.1 = (f32[10,14,56,384]{3,2,1,0:T(8,128)}, f32[384]{0:T(512)}, f32[384]{0:T(512)}, f32[48,288]{1,0:T(8,128)}, f32[1152]{0:T(1024)}, /*index=5*/f32[12,169...) custom-call(bf16[6,3,56,384]{3,2,1,0:T(8,128)(2,1)} %copy-done.1, ...), custom_call_target="tpu_custom_call", output_to_operand_aliasing={{0}: (9, {})} | custom-call | flops 11612160 | bytes 5419008 | tf_op jit(solution)/shard_map/finish/pallas_call | solution.py:784
  (15 shorter events, 0.1 us)
Async XLA Ops:
  0.6 33.0 %copy-start.2 = (s32[10,14,56]{2,1,0:T(8,128)S(1)}, s32[10,14,56]{2,1,0:T(8,128)}, u32[]{:S(2)}) copy-start(s32[10,14,56]{2,1,0:T(8,128)} %refs_5_.1) | copy-start | bytes 94084
  32.1 31.2 %collective-permute-start = (bf16[10,3,56,384]{3,2,1,0:T(8,128)(2,1)}, bf16[10,3,56,384]{3,2,1,0:T(8,128)(2,1)}, u32[]{:S(2)}, u32[]{:S(2)}) collective-permute-start(bf16[10,3,56,384]{3,2,1,0:T(8,128)(2,1)} %get-tuple-element.80), channel_id=1, source_target_pairs={{0,24},{8,0},{16,8},{24,16},{1,25},{9,1},{17,9},{25,17},{2,26},{10... | collective-permute-start | bytes 3870728 | tf_op jit(solution)/shard_map/ppermute | solution.py:1158
  35.7 0.7 copy-start.3
  35.7 1.5 copy-start
  35.9 3.1 copy-start.6
  35.9 3.1 copy-start.7
  36.0 3.1 copy-start.8
  36.0 3.1 copy-start.9
  36.0 3.1 copy-start.10
  36.0 3.1 copy-start.11
  36.0 3.1 %copy-start.4 = (f32[1152]{0:T(1024)S(1)}, f32[1152]{0:T(1024)}, u32[]{:S(2)}) copy-start(f32[1152]{0:T(1024)} %param.23) | copy-start | bytes 13828
  36.0 3.1 %copy-start.5 = (f32[1536]{0:T(1024)S(1)}, f32[1536]{0:T(1024)}, u32[]{:S(2)}) copy-start(f32[1536]{0:T(1024)} %param.30) | copy-start | bytes 18436
  84.0 78.8 %collective-permute-start.1 = (bf16[10,3,56,384]{3,2,1,0:T(8,128)(2,1)}, bf16[10,3,56,384]{3,2,1,0:T(8,128)(2,1)}, u32[]{:S(2)}, u32[]{:S(2)}) collective-permute-start(bf16[10,3,56,384]{3,2,1,0:T(8,128)(2,1)} %bitcast.30), channel_id=1, source_target_pairs={{0,8},{8,16},{16,24},{24,0},{1,9},{9,17},{17,25},{25,1},{2,10},{10... | collective-permute-start | bytes 3870728 | tf_op jit(solution)/shard_map/ppermute | solution.py:1158
  190.5 34.9 %collective-permute-start.3 = (bf16[4,4,48,864]{3,2,1,0:T(8,128)(2,1)}, bf16[4,4,48,864]{3,2,1,0:T(8,128)(2,1)}, u32[]{:S(2)}, u32[]{:S(2)}) collective-permute-start(bf16[4,4,48,864]{3,2,1,0:T(8,128)(2,1)} %get-tuple-element.103), channel_id=1, source_target_pairs={{0,1},{1,0},{2,3},{3,2},{4,5},{5,4},{6,7},{7,6},{8,9},{9,8},{10,11... | collective-permute-start | bytes 3981320 | tf_op jit(solution)/shard_map/ppermute | solution.py:1271
  190.6 40.4 %collective-permute-start.2 = (bf16[10,3,56,384]{3,2,1,0:T(8,128)(2,1)}, bf16[10,3,56,384]{3,2,1,0:T(8,128)(2,1)}, u32[]{:S(2)}, u32[]{:S(2)}) collective-permute-start(bf16[10,3,56,384]{3,2,1,0:T(8,128)(2,1)} %get-tuple-element.97), channel_id=1, source_target_pairs={{0,24},{8,0},{16,8},{24,16},{1,25},{9,1},{17,9},{25,17},{2,26},{10... | collective-permute-start | bytes 3870728 | tf_op jit(solution)/shard_map/ppermute | solution.py:1158
  228.6 42.6 %collective-permute-start.6 = (bf16[2,4,48,864]{3,2,1,0:T(8,128)(2,1)}, bf16[2,4,48,864]{3,2,1,0:T(8,128)(2,1)}, u32[]{:S(2)}, u32[]{:S(2)}) collective-permute-start(bf16[2,4,48,864]{3,2,1,0:T(8,128)(2,1)} %get-tuple-element.124), channel_id=1, source_target_pairs={{0,4},{1,5},{2,6},{3,7},{4,0},{5,1},{6,2},{7,3},{8,12},{9,13},{10,... | collective-permute-start | bytes 1990664 | tf_op jit(solution)/shard_map/ppermute | solution.py:1271
  252.8 51.1 %collective-permute-start.4 = (bf16[6,3,56,384]{3,2,1,0:T(8,128)(2,1)}, bf16[6,3,56,384]{3,2,1,0:T(8,128)(2,1)S(1)}, u32[]{:S(2)}, u32[]{:S(2)}) collective-permute-start(bf16[6,3,56,384]{3,2,1,0:T(8,128)(2,1)} %get-tuple-element.114), channel_id=1, source_target_pairs={{0,8},{8,16},{16,24},{24,0},{1,9},{9,17},{17,25},{25,1},{2,10},{10... | collective-permute-start | bytes 2322440 | tf_op jit(solution)/shard_map/ppermute | solution.py:1158
  269.7 34.3 %collective-permute-start.5 = (bf16[4,3,56,384]{3,2,1,0:T(8,128)(2,1)}, bf16[4,3,56,384]{3,2,1,0:T(8,128)(2,1)}, u32[]{:S(2)}, u32[]{:S(2)}) collective-permute-start(bf16[4,3,56,384]{3,2,1,0:T(8,128)(2,1)} %get-tuple-element.121), channel_id=1, source_target_pairs={{0,8},{8,16},{16,24},{24,0},{1,9},{9,17},{17,25},{25,1},{2,10},{10... | collective-permute-start | bytes 1548296 | tf_op jit(solution)/shard_map/ppermute | solution.py:1158
  304.0 0.9 copy-start.1

commit v7 on v6

--- a/solution.py
+++ b/solution.py
@@ -1271,10 +1271,14 @@
         return lax.ppermute(value, "canvas", [(n, n ^ (1 << bit)) for n in range(lines)])
 
     def halve(keep, got, bit):
-        total = (keep.astype(f32) + got.astype(f32)).astype(bf16)
-        total = total.reshape((2, -1) + total.shape[1:])
         mine = (line >> bit) % 2
-        pick = lambda n: lax.dynamic_index_in_dim(total, n, 0, keepdims=False)
+
+        def pick(n):
+            one, two = (
+                lax.dynamic_index_in_dim(v.reshape((2, -1) + v.shape[1:]), n, 0, keepdims=False) for v in (keep, got)
+            )
+            return (one.astype(f32) + two.astype(f32)).astype(bf16)
+
         return pick(mine), pick(1 - mine)
 
     got = swap(away, 0)

time: 318 us -> 318 us (level)
  no operation moved by 1% of the time
where the time goes in v7:
time: 318 us; the launch traced here: 312 us
  Pallas kernels  290 us (91%)
  starting transfers between devices  9.13 us (3%)
  other arithmetic  5.71 us (2%)
  local copies, waits for them, and re-layouts  3.98 us (1%)
    pallas_call x2, Pallas kernels, feed(): pl.pallas_call(kernel, grid=(canvases // together,), in_specs=specs, out_...  105 us
    pallas_call x3, Pallas kernels, unattend(): pl.pallas_call(kernel, grid=(canvases, steps), in_specs=specs, out_specs=...  71.6 us
    pallas_call x2, Pallas kernels, attend(): pl.pallas_call(functools.partial(attend_kernel, local, heads), grid=grid,...  41.7 us
    pallas_call x1, Pallas kernels, reduce_weight(): pl.pallas_call(functools.partial(reduce_kernel, strips, lines), in_specs=...  32.8 us
    pallas_call x1, Pallas kernels, gather_weights(): pl.pallas_call(functools.partial(gather_kernel, strips, lines, len(own)),...  31.5 us
    pallas_call x1, Pallas kernels, finish(): pl.pallas_call(functools.partial(finish_kernel, neat, heads, entries, ear...  7.3 us
    ppermute x5, starting transfers between devices, from_behind(): return lax.ppermute(value, axis, pairs)  6.67 us
  transfers between devices with their start and end apart: 7, of which 1 were waited for; matrix products, arithmetic and copies ran while one was open for 3% of the time, Pallas kernels for 65%

profile of v7, /device:TPU:0, one launch (start us, length us, event | category | flops | bytes accessed | tf_op | source)
XLA Modules:
  0.0 312.3 jit_solution(3790603016425786626)
XLA Ops:
  0.6 0.0 copy-start.2
  0.7 31.5 %gather_weights.1 = (bf16[384,1152]{1,0:T(8,128)(2,1)}, bf16[384,384]{1,0:T(8,128)(2,1)}, bf16[384,1536]{1,0:T(8,128)(2,1)}, bf16[1536,384]{1,0:T(8,128)(2,1)}, ...) custom-call(bf16[48,288]{1,0:T(8,128)(2,1)} %refs_0_.3, bf16[48,96]{1,0:T(8,128)(2,1)} %refs_1_.2, ...), custom_call_target="tpu_custom_call" | custom-call | tf_op jit(solution)/shard_map/gather_weights/pallas_call | solution.py:980
  32.1 1.5 collective-permute-start
  33.6 0.0 copy-done.2
  33.6 0.7 pad_add_fusion
  34.4 0.8 slice_add_fusion
  35.2 0.1 add_multiply_fusion
  35.3 0.2 mul.30
  35.6 0.1 broadcast_add_fusion
  35.7 0.0 copy-start.3
  35.7 0.0 copy-start
  35.7 0.1 copy.41
  35.9 0.1 pad.8.clone
  35.9 0.0 copy-start.6
  35.9 0.0 copy-start.7
  36.0 0.2 reshape.121
  36.2 0.0 copy-start.8
  36.2 0.0 copy-start.9
  36.2 0.0 copy-start.10
  36.2 0.0 copy-start.11
  36.2 0.0 copy-start.4
  36.2 0.0 copy-start.5
  36.3 0.2 copy-done.3
  36.4 0.8 copy-done
  37.2 1.0 convolution_reduce_fusion
  38.2 0.8 reshape.123.refs_5_.refs_4_
  39.0 0.0 copy-done.6
  39.0 0.0 copy-done.7
  39.0 0.0 copy-done.8
  39.1 0.0 copy-done.9
  39.1 0.0 copy-done.10
  39.1 0.0 copy-done.11
  39.1 0.0 copy-done.4
  39.2 0.0 copy-done.5
  39.2 0.6 reshape.122.refs_3_.refs_2_.refs_4_.refs_6_.refs_8_.par
  39.8 0.7 pad_add_fusion.1.refs_2_.refs_1_
  40.5 21.1 %attend.3 = (bf16[10,1,7,56,384]{4,3,2,1,0:T(8,128)(2,1)}, bf16[10,1,448,384]{3,2,1,0:T(8,128)(2,1)}, bf16[10,1,8,56,1152]{4,3,2,1,0:T(8,128)(2,1)}, bf16[10,1,8,56,768]{4,3,2,1,0:T(8,128)(2,1)}) custom-call(f32[10,14,56,384]{3,2,1,0:T(8,128)} %field.1, s32[10,2,8,128]{3,2,1,0:T(8,128)} %pad_add_fusion.1.refs_2_.refs_1_, ...), custom_call_target="tpu_custom_call" | custom-call | flops 9248440320 | bytes 40320000 | tf_op jit(solution)/shard_map/attend/pallas_call | solution.py:221
  61.6 1.7 collective-permute-done.refs_1_.refs_2_
  63.3 20.6 %attend.2 = (bf16[10,1,4,56,384]{4,3,2,1,0:T(8,128)(2,1)}, bf16[10,1,3,56,384]{4,3,2,1,0:T(8,128)(2,1)}, bf16[10,1,448,384]{3,2,1,0:T(8,128)(2,1)}, bf16[10,1,8,...) custom-call(f32[10,14,56,384]{3,2,1,0:T(8,128)} %field.1, ...), custom_call_target="tpu_custom_call" | custom-call | flops 9248440320 | bytes 40320000 | tf_op jit(solution)/shard_map/attend/pallas_call | solution.py:221
  84.0 1.9 collective-permute-start.1
  85.8 76.9 %feed.2 = (f32[10,14,56,384]{3,2,1,0:T(8,128)}, f32[10,14,56,384]{3,2,1,0:T(8,128)}, bf16[10,7,56,384]{3,2,1,0:T(8,128)(2,1)}, bf16[10,4,56,384]{3,2,1,0:T(8,128...) custom-call(bf16[10,7,56,384]{3,2,1,0:T(8,128)(2,1)} %bitcast.34, ...), custom_call_target="tpu_custom_call" | custom-call | flops 49049763840 | bytes 47308800 | tf_op jit(solution)/shard_map/feed/pallas_call | solution.py:447
  162.8 0.0 collective-permute-done.1.refs_0_
  162.8 27.7 %feed.3 = (f32[10,14,56,384]{3,2,1,0:T(8,128)}, f32[10,14,56,384]{3,2,1,0:T(8,128)}, bf16[10,3,56,384]{3,2,1,0:T(8,128)(2,1)}, bf16[4,4,48,864]{3,2,1,0:T(8,128)...) custom-call(bf16[10,3,56,384]{3,2,1,0:T(8,128)(2,1)} %collective-permute-, ...), custom_call_target="tpu_custom_call", output_to_operand_aliasing={{0}: (7, {}), {1}: (8, {})} | custom-call | flops 13377208320 | bytes 12902400 | tf_op jit(solution)/shard_map/feed/pallas_call | solution.py:447
  190.5 0.1 collective-permute-start.3
  190.6 1.2 collective-permute-start.2
  191.7 33.6 %unattend.3 = (f32[10,14,56,384]{3,2,1,0:T(8,128)}, f32[384,1152]{1,0:T(8,128)}, f32[1,1152]{1,0:T(1,128)}, f32[56,768]{1,0:T(8,128)}, f32[8,384]{1,0:T(8,128)}) custom-call(bf16[10,1,7,56,384]{4,3,2,1,0:T(8,128)(2,1)} %bitcast.33, bf16[10,1,448,384]{3,2,1,0:T(8,128)(2,1)} %get-tuple-element.106.refs_1_, ...), custom_call_target="tpu_custom_call" | custom-call | flops 18496880640 | bytes 40320000 | tf_op jit(solution)/shard_map/unattend/pallas_call | solution.py:697
  225.3 0.0 collective-permute-done.3
  225.3 3.2 %fusion.1 = (bf16[2,4,48,864]{3,2,1,0:T(8,128)(2,1)}, bf16[2,4,48,864]{3,2,1,0:T(8,128)(2,1)}) fusion(bf16[2,2,4,48,864]{4,3,2,1,0:T(8,128)(2,1)} %bitcast.12, s32[]{:T(128)S(6)} %select_n.18, bf16[2,2,4,48,864]{4,3,2,1,0:T(8,128)(2,1)} %bitcast.30, s32[]{:T(128)S(6)} %select_n.17), kind=kLoop, calls=%fused_computation.4 | loop fusion | flops 2654208 | bytes 3981320 | tf_op jit(solution)/shard_map/convert_element_type | solution.py:1280
  228.5 2.4 collective-permute-start.6
  230.9 0.0 collective-permute-done.2.refs_1_
  230.9 21.8 %unattend.4 = (f32[10,14,56,384]{3,2,1,0:T(8,128)}, bf16[6,3,56,384]{3,2,1,0:T(8,128)(2,1)}, f32[384,1152]{1,0:T(8,128)}, f32[1,1152]{1,0:T(1,128)}, f32[56,768]{1,0:T(8,128)}, /*index=5*/f32[8,384]{1,0:T(8,128)}) custom-call(bf16[10,4,56,384]{3,2,1,0:T(8,128)(2,1)} %get-tuple-element.96.refs_0_, ...), custom_call_target="tpu_custom_call", output_to_operand_aliasing={{0}: (10, {})} | custom-call | flops 11098128384 | bytes 24192000 | tf_op jit(solution)/shard_map/unattend/pallas_call | solution.py:697
  252.7 0.6 collective-permute-start.4
  253.4 16.2 %unattend.5 = (f32[10,14,56,384]{3,2,1,0:T(8,128)}, bf16[4,3,56,384]{3,2,1,0:T(8,128)(2,1)}, f32[384,1152]{1,0:T(8,128)}, f32[24,384]{1,0:T(8,128)}) custom-call(bf16[10,4,56,384]{3,2,1,0:T(8,128)(2,1)} %get-tuple-element.96.refs_0_, bf16[10,3,56,384]{3,2,1,0:T(8,128)(2,1)} %collective-permute-done.2.refs_1_, ...), custom_call_target="tpu_custom_call", output_to_operand_aliasing={{0}: (11, {})} | custom-call | flops 7398752256 | bytes 16128000 | tf_op jit(solution)/shard_map/unattend/pallas_call | solution.py:697
  269.6 1.5 collective-permute-start.5
  271.1 0.0 collective-permute-done.6.feed_got
  271.1 32.8 %reduce_weight.1 = (f32[48,288]{1,0:T(8,128)}, f32[24,384]{1,0:T(8,128)}, f32[48,864]{1,0:T(8,128)}) custom-call(f32[8,48,1152]{2,1,0:T(8,128)} %bitcast.29, f32[24,384]{1,0:T(8,128)} %get-tuple-element.123.small, bf16[2,4,48,864]{3,2,1,0:T(8,128)(2,1)} %get-tuple-element.145.feed_keep, bf16[2,4,48,864]{3,2,1,0:T(8,128)(2,1)} %collective-permute-done.6.feed_got), custom_call_target="tpu_custom_call" | custom-call | tf_op jit(solution)/shard_map/reduce_weight/pallas_call | solution.py:1140
  303.9 0.0 collective-permute-done.5.d_late
  303.9 0.0 collective-permute-done.4.d_normed
  303.9 0.0 copy-start.1
  303.9 0.9 copy-done.1
  304.8 7.3 %finish.1 = (f32[10,14,56,384]{3,2,1,0:T(8,128)}, f32[384]{0:T(512)}, f32[384]{0:T(512)}, f32[48,288]{1,0:T(8,128)}, f32[1152]{0:T(1024)}, /*index=5*/f32[12,169...) custom-call(bf16[6,3,56,384]{3,2,1,0:T(8,128)(2,1)} %copy-done.1, ...), custom_call_target="tpu_custom_call", output_to_operand_aliasing={{0}: (9, {})} | custom-call | flops 11612160 | bytes 5419008 | tf_op jit(solution)/shard_map/finish/pallas_call | solution.py:784
  (15 shorter events, 0.1 us)
Async XLA Ops:
  0.6 33.0 %copy-start.2 = (s32[10,14,56]{2,1,0:T(8,128)S(1)}, s32[10,14,56]{2,1,0:T(8,128)}, u32[]{:S(2)}) copy-start(s32[10,14,56]{2,1,0:T(8,128)} %refs_5_.1) | copy-start | bytes 94084
  32.1 31.2 %collective-permute-start = (bf16[10,3,56,384]{3,2,1,0:T(8,128)(2,1)}, bf16[10,3,56,384]{3,2,1,0:T(8,128)(2,1)}, u32[]{:S(2)}, u32[]{:S(2)}) collective-permute-start(bf16[10,3,56,384]{3,2,1,0:T(8,128)(2,1)} %get-tuple-element.80), channel_id=1, source_target_pairs={{0,24},{8,0},{16,8},{24,16},{1,25},{9,1},{17,9},{25,17},{2,26},{10... | collective-permute-start | bytes 3870728 | tf_op jit(solution)/shard_map/ppermute | solution.py:1158
  35.7 0.7 copy-start.3
  35.7 1.5 copy-start
  35.9 3.1 copy-start.6
  35.9 3.1 copy-start.7
  36.2 2.9 copy-start.8
  36.2 2.9 copy-start.9
  36.2 2.9 copy-start.10
  36.2 2.9 copy-start.11
  36.2 2.9 copy-start.4
  36.2 2.9 copy-start.5
  84.0 78.8 %collective-permute-start.1 = (bf16[10,3,56,384]{3,2,1,0:T(8,128)(2,1)}, bf16[10,3,56,384]{3,2,1,0:T(8,128)(2,1)}, u32[]{:S(2)}, u32[]{:S(2)}) collective-permute-start(bf16[10,3,56,384]{3,2,1,0:T(8,128)(2,1)} %bitcast.31), channel_id=1, source_target_pairs={{0,8},{8,16},{16,24},{24,0},{1,9},{9,17},{17,25},{25,1},{2,10},{10... | collective-permute-start | bytes 3870728 | tf_op jit(solution)/shard_map/ppermute | solution.py:1158
  190.5 34.9 %collective-permute-start.3 = (bf16[4,4,48,864]{3,2,1,0:T(8,128)(2,1)}, bf16[4,4,48,864]{3,2,1,0:T(8,128)(2,1)}, u32[]{:S(2)}, u32[]{:S(2)}) collective-permute-start(bf16[4,4,48,864]{3,2,1,0:T(8,128)(2,1)} %get-tuple-element.103), channel_id=1, source_target_pairs={{0,1},{1,0},{2,3},{3,2},{4,5},{5,4},{6,7},{7,6},{8,9},{9,8},{10,11... | collective-permute-start | bytes 3981320 | tf_op jit(solution)/shard_map/ppermute | solution.py:1271
  190.6 40.3 %collective-permute-start.2 = (bf16[10,3,56,384]{3,2,1,0:T(8,128)(2,1)}, bf16[10,3,56,384]{3,2,1,0:T(8,128)(2,1)}, u32[]{:S(2)}, u32[]{:S(2)}) collective-permute-start(bf16[10,3,56,384]{3,2,1,0:T(8,128)(2,1)} %get-tuple-element.97), channel_id=1, source_target_pairs={{0,24},{8,0},{16,8},{24,16},{1,25},{9,1},{17,9},{25,17},{2,26},{10... | collective-permute-start | bytes 3870728 | tf_op jit(solution)/shard_map/ppermute | solution.py:1158
  228.5 42.6 %collective-permute-start.6 = (bf16[2,4,48,864]{3,2,1,0:T(8,128)(2,1)}, bf16[2,4,48,864]{3,2,1,0:T(8,128)(2,1)}, u32[]{:S(2)}, u32[]{:S(2)}) collective-permute-start(bf16[2,4,48,864]{3,2,1,0:T(8,128)(2,1)} %get-tuple-element.124), channel_id=1, source_target_pairs={{0,4},{1,5},{2,6},{3,7},{4,0},{5,1},{6,2},{7,3},{8,12},{9,13},{10,... | collective-permute-start | bytes 1990664 | tf_op jit(solution)/shard_map/ppermute | solution.py:1271
  252.7 51.1 %collective-permute-start.4 = (bf16[6,3,56,384]{3,2,1,0:T(8,128)(2,1)}, bf16[6,3,56,384]{3,2,1,0:T(8,128)(2,1)S(1)}, u32[]{:S(2)}, u32[]{:S(2)}) collective-permute-start(bf16[6,3,56,384]{3,2,1,0:T(8,128)(2,1)} %get-tuple-element.114), channel_id=1, source_target_pairs={{0,8},{8,16},{16,24},{24,0},{1,9},{9,17},{17,25},{25,1},{2,10},{10... | collective-permute-start | bytes 2322440 | tf_op jit(solution)/shard_map/ppermute | solution.py:1158
  269.6 34.3 %collective-permute-start.5 = (bf16[4,3,56,384]{3,2,1,0:T(8,128)(2,1)}, bf16[4,3,56,384]{3,2,1,0:T(8,128)(2,1)}, u32[]{:S(2)}, u32[]{:S(2)}) collective-permute-start(bf16[4,3,56,384]{3,2,1,0:T(8,128)(2,1)} %get-tuple-element.121), channel_id=1, source_target_pairs={{0,8},{8,16},{16,24},{24,0},{1,9},{9,17},{17,25},{25,1},{2,10},{10... | collective-permute-start | bytes 1548296 | tf_op jit(solution)/shard_map/ppermute | solution.py:1158
  303.9 0.9 copy-start.1
